TPU v7x, 128 devices: a whole 4x4x4 slice. The times are simulated.
128 devices in a mesh: section: 2 (over x_lo), fsdp: 16 (over y, x_hi, core), replica: 4 (over z).
Axes of the slice: x: 4 (x_hi: 2, x_lo: 2; x = x_hi * 2 + x_lo), y: 4, z: 4, core: 2. Of those that a mesh axis runs over, the one named last changes fastest.
Arguments:
- inputs: bfloat16 [8, 1024, 1088], P('replica', 'fsdp'), may hold values from -6 to 6
- segment_ids: int32 [8, 1024], P('replica'), may hold values from 0 to 5, as said below
- sequence_order: int32 [4, 2], P('replica'), may hold values from 0 to 1, each once within a row
- ln1_gain: bfloat16 [2, 1088], P('section', 'fsdp'), may hold values from 0.5 to 1.5
- ln1_bias: bfloat16 [2, 1088], P('section', 'fsdp'), may hold values from -1.75 to 1.75
- w_qkv: bfloat16 [2, 1088, 3264], P('section', 'fsdp'), may hold values from -0.1875 to 0.1875
- qv_bias: bfloat16 [2, 2176], P('section', 'fsdp'), may hold values from -1.75 to 1.75
- w_out: bfloat16 [2, 1088, 1088], P('section', 'fsdp'), may hold values from -1.5 to 1.5
- out_bias: bfloat16 [2, 1088], P('section', 'fsdp'), may hold values from -1.75 to 1.75
- ln2_gain: bfloat16 [2, 1088], P('section', 'fsdp'), may hold values from 0.5 to 1.5
- ln2_bias: bfloat16 [2, 1088], P('section', 'fsdp'), may hold values from -1.75 to 1.75
- w_fc: bfloat16 [2, 1088, 4352], P('section', 'fsdp'), may hold values from -0.1875 to 0.1875
- fc_bias: bfloat16 [2, 4352], P('section', 'fsdp'), may hold values from -1.75 to 1.75
- w_proj: bfloat16 [2, 4352, 1088], P('section', 'fsdp'), may hold values from -0.09375 to 0.09375
- proj_bias: bfloat16 [2, 1088], P('section', 'fsdp'), may hold values from -1.75 to 1.75
- cotangent: bfloat16 [8, 1024, 1088], P('replica', 'fsdp'), may hold values from -6 to 6
Outputs:
- activations: bfloat16 [2, 8, 1024, 1088], P('section', 'replica', 'fsdp')
- input_grads: bfloat16 [2, 8, 1024, 1088], P('section', 'replica', 'fsdp')
- grad_ln1_gain: float32 [2, 1088], P('section', 'fsdp')
- grad_ln1_bias: float32 [2, 1088], P('section', 'fsdp')
- grad_w_qkv: float32 [2, 1088, 3264], P('section', 'fsdp')
- grad_qv_bias: float32 [2, 2176], P('section', 'fsdp')
- grad_w_out: float32 [2, 1088, 1088], P('section', 'fsdp')
- grad_out_bias: float32 [2, 1088], P('section', 'fsdp')
- grad_ln2_gain: float32 [2, 1088], P('section', 'fsdp')
- grad_ln2_bias: float32 [2, 1088], P('section', 'fsdp')
- grad_w_fc: float32 [2, 1088, 4352], P('section', 'fsdp')
- grad_fc_bias: float32 [2, 4352], P('section', 'fsdp')
- grad_w_proj: float32 [2, 4352, 1088], P('section', 'fsdp')
- grad_proj_bias: float32 [2, 1088], P('section', 'fsdp')
Inputs may be any that keep to these rules, and one draw needn't show every extreme that they name: `segment_ids`: within each sequence the document numbers start at 0 and rise by one at each document boundary; every document but a sequence's last has at least 204 tokens; in each replica group one of its 2 sequences, drawn from the seed, is a single document; the most is reached. `sequence_order`: each row is a permutation.
All inputs are finite; a program needn't handle non-finite values.
Results may differ from a plain program's by a relative error of at most 0.02.
Values may be sent and summed in bfloat16 or wider, within the bound.
No kernel may reach another device: no remote copies, remote signals or barrier semaphores. Data moves between devices by JAX's collectives and lax.ppermute only.
A program may use at most 256 MiB of HBM per device.

v0:
```python
import jax
import jax.numpy as jnp
from jax import lax
from jax.sharding import PartitionSpec as P

D = 1088
HEADS = 17
HEAD_DIM = 64
FF = 4352


epsilon = 1e-05


def sent_together(arrays, axis, dim, along):
    columns = [a.reshape(*a.shape[:along], -1) for a in arrays]
    both = jnp.concatenate(columns, axis=along)
    filled, at, finished = (lax.all_gather(both, axis, axis=dim, tiled=True), 0, [])
    for a, column in zip(arrays, columns):
        piece = filled[..., at : at + column.shape[along]]
        finished.append(piece.reshape(*piece.shape[:along], *a.shape[along:]))
        at += column.shape[along]
    return tuple(finished)


def from_behind(value, axis, steps):
    count = lax.axis_size(axis)
    first, last = (max(0, -steps), min(count, count - steps))
    return lax.ppermute(value, axis, [(source, source + steps) for source in range(first, last)])


def in_one_piece(arrays, axis, dim, along):
    both = jnp.concatenate(arrays, axis=along)
    filled, at, finished = (lax.all_gather(both, axis, axis=dim, tiled=True), 0, [])
    for a in arrays:
        finished.append(lax.slice_in_dim(filled, at, at + a.shape[along], axis=along))
        at += a.shape[along]
    return tuple(finished)


def layer_norm(values, gain_vec, bias_vec):
    average = jnp.mean(values, axis=-1, keepdims=True)
    centred = values - average
    variance = jnp.mean(centred * centred, axis=-1, keepdims=True)
    return centred * lax.rsqrt(variance + epsilon) * gain_vec + bias_vec


def gelu_tanh(values):
    return jax.nn.gelu(values, approximate=True)


def matmul(left, right):
    return jnp.dot(left, right, preferred_element_type=jnp.float32)


def matmul_right_t(left, right):
    return lax.dot_general(
        left, right, (((1,), (1,)), ((), ())), preferred_element_type=jnp.float32
    )


def matmul_left_t(left, right):
    return lax.dot_general(
        left, right, (((0,), (0,)), ((), ())), preferred_element_type=jnp.float32
    )


def shards(
    inputs,
    segment_ids,
    sequence_order,
    ln1_gain,
    ln1_bias,
    w_qkv,
    qv_bias,
    w_out,
    out_bias,
    ln2_gain,
    ln2_bias,
    w_fc,
    fc_bias,
    w_proj,
    proj_bias,
    cotangent,
):
    gathered = (
        *sent_together((ln1_gain, ln1_bias, w_qkv), "fsdp", 1, 2),
        lax.all_gather(qv_bias, "fsdp", axis=1, tiled=True),
        *sent_together((w_out, out_bias, ln2_gain, ln2_bias, w_fc), "fsdp", 1, 2),
        *sent_together((fc_bias, w_proj), "fsdp", 1, 2),
        lax.all_gather(proj_bias, "fsdp", axis=1, tiled=True),
    )
    full_set = [member[0] for member in gathered]
    gain_one = full_set[0].astype(jnp.float32)
    bias_one = full_set[1].astype(jnp.float32)
    full_qkv = full_set[2]
    qv_full = full_set[3].astype(jnp.float32)
    full_out = full_set[4]
    out_shift = full_set[5].astype(jnp.float32)
    gain_two = full_set[6].astype(jnp.float32)
    bias_two = full_set[7].astype(jnp.float32)
    full_fc = full_set[8]
    fc_shift = full_set[9].astype(jnp.float32)
    full_proj = full_set[10]
    proj_shift = full_set[11].astype(jnp.float32)
    qkv_shift = jnp.concatenate([qv_full[:D], jnp.zeros((D,), jnp.float32), qv_full[D:]])
    section_count = lax.axis_size("section")
    section_index = lax.axis_index("section")
    shard_index = lax.axis_index("fsdp")
    micro_count = inputs.shape[0]
    span_rows = inputs.shape[1]
    seq_len = segment_ids.shape[1]
    score_scale = HEAD_DIM ** (-0.5)
    order_row = sequence_order[0]
    ordered_inputs = jnp.take(inputs, order_row, axis=0)
    ordered_segments = jnp.take(segment_ids, order_row, axis=0)
    query_pos = shard_index * span_rows + jnp.arange(span_rows)
    causal = jnp.arange(seq_len)[None, :] <= query_pos[:, None]
    step_count = micro_count + section_count - 1
    is_first = section_index == 0
    is_last = section_index == section_count - 1

    def mask_for(mb_index):
        seg_row = lax.dynamic_index_in_dim(ordered_segments, mb_index, 0, keepdims=False)
        query_seg = lax.dynamic_slice_in_dim(seg_row, shard_index * span_rows, span_rows)
        return causal & (seg_row[None, :] == query_seg[:, None])

    def masked_scores(queries, keys_all, allowed):
        raw_scores = (
            jnp.einsum("qhd,khd->hqk", queries, keys_all, preferred_element_type=jnp.float32)
            * score_scale
        )
        return jnp.where(allowed[None], raw_scores, -1e30)

    def forward_step(received, step_now):
        mb_index = jnp.clip(step_now - section_index, 0, micro_count - 1)
        own_input = lax.dynamic_index_in_dim(ordered_inputs, mb_index, 0, keepdims=False)
        layer_in = jnp.where(is_first, own_input, received)
        allowed = mask_for(mb_index)
        layer_wide = layer_in.astype(jnp.float32)
        normed_one = layer_norm(layer_wide, gain_one, bias_one).astype(jnp.bfloat16)
        packed = (matmul(normed_one, full_qkv) + qkv_shift).astype(jnp.bfloat16)
        kv_all = lax.all_gather(packed[:, D:], "fsdp", axis=0, tiled=True)
        queries = packed[:, :D].reshape(span_rows, HEADS, HEAD_DIM)
        keys_all = kv_all[:, :D].reshape(seq_len, HEADS, HEAD_DIM)
        values_all = kv_all[:, D:].reshape(seq_len, HEADS, HEAD_DIM)
        masked = masked_scores(queries, keys_all, allowed)
        row_max = jnp.max(masked, axis=-1, keepdims=True)
        shifted = jnp.exp(masked - row_max)
        row_sum = jnp.sum(shifted, axis=-1, keepdims=True)
        log_total = row_max + jnp.log(row_sum)
        probs_low = (shifted / row_sum).astype(jnp.bfloat16)
        attended = (
            jnp.einsum("hqk,khd->qhd", probs_low, values_all, preferred_element_type=jnp.float32)
            .reshape(span_rows, D)
            .astype(jnp.bfloat16)
        )
        hidden = layer_wide + matmul(attended, full_out) + out_shift
        normed_two = layer_norm(hidden, gain_two, bias_two).astype(jnp.bfloat16)
        pre_act = matmul(normed_two, full_fc) + fc_shift
        activ = gelu_tanh(pre_act).astype(jnp.bfloat16)
        out_low = (hidden + matmul(activ, full_proj) + proj_shift).astype(jnp.bfloat16)
        sent_on = from_behind(out_low, "section", 1)
        kept_values = (
            layer_in,
            packed,
            kv_all,
            log_total,
            attended,
            hidden,
            normed_two,
            pre_act,
            activ,
            normed_one,
            out_low,
        )
        return (sent_on, kept_values)

    start_recv = jnp.zeros((span_rows, D), jnp.bfloat16)
    _, kept_all = lax.scan(forward_step, start_recv, jnp.arange(step_count))

    def backward_step(carried, step_now):
        received_grad, vec_sums = carried
        mb_raw = micro_count - 1 - step_now + (section_count - 1 - section_index)
        is_valid = ((mb_raw >= 0) & (mb_raw < micro_count)).astype(jnp.float32)
        mb_index = jnp.clip(mb_raw, 0, micro_count - 1)
        slot = mb_index + section_index
        (
            layer_in,
            packed,
            kv_all,
            log_total,
            attended,
            hidden,
            normed_two,
            pre_act,
            activ,
            normed_one,
            out_low,
        ) = [lax.dynamic_index_in_dim(member, slot, 0, keepdims=False) for member in kept_all]
        own_cot = lax.dynamic_index_in_dim(cotangent, mb_index, 0, keepdims=False)
        grad_out = jnp.where(is_last, own_cot, received_grad)
        grad_wide = grad_out.astype(jnp.float32)
        grad_act = matmul_right_t(grad_out, full_proj)
        _, gelu_back = jax.vjp(gelu_tanh, pre_act)
        grad_pre = gelu_back(grad_act)[0].astype(jnp.bfloat16)
        grad_normed_two = matmul_right_t(grad_pre, full_fc)
        _, norm_two_back = jax.vjp(layer_norm, hidden, gain_two, bias_two)
        grad_hidden_ln, grad_gain_two, grad_bias_two = norm_two_back(grad_normed_two)
        grad_hidden = grad_wide + grad_hidden_ln
        grad_branch = grad_hidden.astype(jnp.bfloat16)
        grad_att = matmul_right_t(grad_branch, full_out).astype(jnp.bfloat16)
        grad_att_heads = grad_att.reshape(span_rows, HEADS, HEAD_DIM)
        queries = packed[:, :D].reshape(span_rows, HEADS, HEAD_DIM)
        keys_all = kv_all[:, :D].reshape(seq_len, HEADS, HEAD_DIM)
        values_all = kv_all[:, D:].reshape(seq_len, HEADS, HEAD_DIM)
        masked = masked_scores(queries, keys_all, mask_for(mb_index))
        probs_wide = jnp.exp(masked - log_total)
        grad_probs = jnp.einsum(
            "qhd,khd->hqk", grad_att_heads, values_all, preferred_element_type=jnp.float32
        )
        row_dot = jnp.sum(grad_probs * probs_wide, axis=-1, keepdims=True)
        grad_scores = (probs_wide * (grad_probs - row_dot)).astype(jnp.bfloat16)
        grad_queries = (
            jnp.einsum("hqk,khd->qhd", grad_scores, keys_all, preferred_element_type=jnp.float32)
            * score_scale
        )
        query_all, grad_att_all = in_one_piece((packed[:, :D], grad_att), "fsdp", 0, 1)
        total_all, dot_all = in_one_piece((log_total, row_dot), "fsdp", 1, 0)
        query_heads = query_all.reshape(seq_len, HEADS, HEAD_DIM)
        grad_heads_all = grad_att_all.reshape(seq_len, HEADS, HEAD_DIM)
        own_keys = packed[:, D : 2 * D].reshape(span_rows, HEADS, HEAD_DIM)
        own_values = packed[:, 2 * D :].reshape(span_rows, HEADS, HEAD_DIM)
        seg_row = lax.dynamic_index_in_dim(ordered_segments, mb_index, 0, keepdims=False)
        own_seg = lax.dynamic_slice_in_dim(seg_row, shard_index * span_rows, span_rows)
        column_allowed = (query_pos[None, :] <= jnp.arange(seq_len)[:, None]) & (
            seg_row[:, None] == own_seg[None, :]
        )
        column_masked = masked_scores(query_heads, own_keys, column_allowed)
        column_probs = jnp.exp(column_masked - total_all)
        column_grad_probs = jnp.einsum(
            "qhd,khd->hqk", grad_heads_all, own_values, preferred_element_type=jnp.float32
        )
        column_grad_scores = (column_probs * (column_grad_probs - dot_all)).astype(jnp.bfloat16)
        key_grads = (
            jnp.einsum(
                "hqk,qhd->khd", column_grad_scores, query_heads, preferred_element_type=jnp.float32
            )
            * score_scale
        ).reshape(span_rows, D)
        value_grads = jnp.einsum(
            "hqk,qhd->khd",
            column_probs.astype(jnp.bfloat16),
            grad_heads_all,
            preferred_element_type=jnp.float32,
        ).reshape(span_rows, D)
        grad_packed = jnp.concatenate(
            [grad_queries.reshape(span_rows, D), key_grads, value_grads], axis=1
        ).astype(jnp.bfloat16)
        grad_normed_one = matmul_right_t(grad_packed, full_qkv)
        _, norm_one_back = jax.vjp(layer_norm, layer_in.astype(jnp.float32), gain_one, bias_one)
        grad_in_ln, grad_gain_one, grad_bias_one = norm_one_back(grad_normed_one)
        grad_input = (grad_hidden + grad_in_ln).astype(jnp.bfloat16)
        sent_back = from_behind(grad_input, "section", -1)
        packed_wide = grad_packed.astype(jnp.float32)
        column_qv = jnp.concatenate(
            [jnp.sum(packed_wide[:, :D], axis=0), jnp.sum(packed_wide[:, 2 * D :], axis=0)]
        )
        step_terms = (
            grad_gain_one,
            grad_bias_one,
            column_qv,
            jnp.sum(grad_branch.astype(jnp.float32), axis=0),
            grad_gain_two,
            grad_bias_two,
            jnp.sum(grad_pre.astype(jnp.float32), axis=0),
            jnp.sum(grad_wide, axis=0),
        )
        new_sums = tuple((total + is_valid * term for total, term in zip(vec_sums, step_terms)))
        return ((sent_back, new_sums), (grad_packed, grad_branch, grad_pre, grad_out, grad_input))

    zero_sums = (
        jnp.zeros((D,), jnp.float32),
        jnp.zeros((D,), jnp.float32),
        jnp.zeros((2 * D,), jnp.float32),
        jnp.zeros((D,), jnp.float32),
        jnp.zeros((D,), jnp.float32),
        jnp.zeros((D,), jnp.float32),
        jnp.zeros((FF,), jnp.float32),
        jnp.zeros((D,), jnp.float32),
    )
    (_, vec_sums), back_all = lax.scan(
        backward_step, (start_recv, zero_sums), jnp.arange(step_count)
    )

    def take_forward(stacked):
        picked = lax.dynamic_slice_in_dim(stacked, section_index, micro_count, 0)
        return picked.reshape(micro_count * span_rows, stacked.shape[-1])

    def take_backward(stacked):
        picked = jnp.flip(
            lax.dynamic_slice_in_dim(stacked, section_count - 1 - section_index, micro_count, 0), 0
        )
        return picked.reshape(micro_count * span_rows, stacked.shape[-1])

    grad_qkv_w = matmul_left_t(take_forward(kept_all[9]), take_backward(back_all[0]))
    grad_out_w = matmul_left_t(take_forward(kept_all[4]), take_backward(back_all[1]))
    grad_fc_w = matmul_left_t(take_forward(kept_all[6]), take_backward(back_all[2]))
    grad_proj_w = matmul_left_t(take_forward(kept_all[8]), take_backward(back_all[3]))
    shares = (
        lax.psum_scatter(
            vec_sums[0].astype(jnp.bfloat16), "fsdp", scatter_dimension=0, tiled=True
        ).astype(jnp.float32),
        lax.psum_scatter(
            vec_sums[1].astype(jnp.bfloat16), "fsdp", scatter_dimension=0, tiled=True
        ).astype(jnp.float32),
        lax.psum_scatter(
            grad_qkv_w.astype(jnp.bfloat16), "fsdp", scatter_dimension=0, tiled=True
        ).astype(jnp.float32),
        lax.psum_scatter(
            vec_sums[2].astype(jnp.bfloat16), "fsdp", scatter_dimension=0, tiled=True
        ).astype(jnp.float32),
        lax.psum_scatter(
            grad_out_w.astype(jnp.bfloat16), "fsdp", scatter_dimension=0, tiled=True
        ).astype(jnp.float32),
        lax.psum_scatter(
            vec_sums[3].astype(jnp.bfloat16), "fsdp", scatter_dimension=0, tiled=True
        ).astype(jnp.float32),
        lax.psum_scatter(
            vec_sums[4].astype(jnp.bfloat16), "fsdp", scatter_dimension=0, tiled=True
        ).astype(jnp.float32),
        lax.psum_scatter(
            vec_sums[5].astype(jnp.bfloat16), "fsdp", scatter_dimension=0, tiled=True
        ).astype(jnp.float32),
        lax.psum_scatter(
            grad_fc_w.astype(jnp.bfloat16), "fsdp", scatter_dimension=0, tiled=True
        ).astype(jnp.float32),
        lax.psum_scatter(
            vec_sums[6].astype(jnp.bfloat16), "fsdp", scatter_dimension=0, tiled=True
        ).astype(jnp.float32),
        lax.psum_scatter(
            grad_proj_w.astype(jnp.bfloat16), "fsdp", scatter_dimension=0, tiled=True
        ).astype(jnp.float32),
        lax.psum_scatter(
            vec_sums[7].astype(jnp.bfloat16), "fsdp", scatter_dimension=0, tiled=True
        ).astype(jnp.float32),
    )
    totals = (
        lax.psum(shares[0].astype(jnp.bfloat16), "replica").astype(jnp.float32),
        lax.psum(shares[1].astype(jnp.bfloat16), "replica").astype(jnp.float32),
        lax.psum(shares[2].astype(jnp.bfloat16), "replica").astype(jnp.float32),
        lax.psum(shares[3].astype(jnp.bfloat16), "replica").astype(jnp.float32),
        lax.psum(shares[4].astype(jnp.bfloat16), "replica").astype(jnp.float32),
        lax.psum(shares[5].astype(jnp.bfloat16), "replica").astype(jnp.float32),
        lax.psum(shares[6].astype(jnp.bfloat16), "replica").astype(jnp.float32),
        lax.psum(shares[7].astype(jnp.bfloat16), "replica").astype(jnp.float32),
        lax.psum(shares[8].astype(jnp.bfloat16), "replica").astype(jnp.float32),
        lax.psum(shares[9].astype(jnp.bfloat16), "replica").astype(jnp.float32),
        lax.psum(shares[10].astype(jnp.bfloat16), "replica").astype(jnp.float32),
        lax.psum(shares[11].astype(jnp.bfloat16), "replica").astype(jnp.float32),
    )
    activations = lax.dynamic_slice_in_dim(kept_all[10], section_index, micro_count, 0)[None]
    input_grads = jnp.flip(
        lax.dynamic_slice_in_dim(back_all[4], section_count - 1 - section_index, micro_count, 0), 0
    )[None]
    return (activations, input_grads) + tuple((total[None] for total in totals))


def solution(mesh):
    return jax.shard_map(
        shards,
        mesh=mesh,
        in_specs=(
            P("replica", "fsdp", None),
            P("replica", None),
            P("replica", None),
            P("section", "fsdp"),
            P("section", "fsdp"),
            P("section", "fsdp", None),
            P("section", "fsdp"),
            P("section", "fsdp", None),
            P("section", "fsdp"),
            P("section", "fsdp"),
            P("section", "fsdp"),
            P("section", "fsdp", None),
            P("section", "fsdp"),
            P("section", "fsdp", None),
            P("section", "fsdp"),
            P("replica", "fsdp", None),
        ),
        out_specs=(
            P("section", "replica", "fsdp", None),
            P("section", "replica", "fsdp", None),
            P("section", "fsdp"),
            P("section", "fsdp"),
            P("section", "fsdp", None),
            P("section", "fsdp"),
            P("section", "fsdp", None),
            P("section", "fsdp"),
            P("section", "fsdp"),
            P("section", "fsdp"),
            P("section", "fsdp", None),
            P("section", "fsdp"),
            P("section", "fsdp", None),
            P("section", "fsdp"),
        ),
        check_vma=False,
    )
```

profile of v0, /device:TPU:0, one launch (start us, length us, event | category | flops | bytes accessed | tf_op | source)
XLA Modules:
  0.0 1527.7 jit_solution(18334523431450015825)
XLA Ops:
  19.1 8.2 concatenate.63
  29.9 71.3 %all-reduce.17 = (bf16[2176]{0:T(1024)(128)(2,1)S(1)}, bf16[1088]{0:T(1024)(128)(2,1)S(1)}) all-reduce(bf16[2176]{0:T(1024)(128)(2,1)S(1)} %dynamic-update-slice, bf16[1088]{0:T(1024)(128)(2,1)S(1)} %dynamic-update-slice.1), channel_id=1, replica_groups=mesh['section'=2,'fsdp'=16,'replica'=4] {'fsdp'}, use_global_device_ids=true, to_apply=%add | all-reduce | flops 3264 | bytes 13056
  104.5 13.7 all-gather.6.cloned.1.call-done
  118.2 24.1 %slice.198 = bf16[1,1088,3264]{2,0,1:T(2,128)(2,1)} slice(bf16[1,1088,3266]{2,0,1:T(2,128)(2,1)} %all-gather.6.cloned.1.call-done), slice={[0:1], [0:1088], [2:3266]} | slice | bytes 14204928 | tf_op jit(solution)/shard_map/slice | solution.py:20
  142.3 9.3 copy.203
  151.6 19.1 %fusion.100 = (f32[1088]{0:T(1024)S(1)}, f32[1088]{0:T(1024)S(1)}) fusion(bf16[1,1088,3266]{2,0,1:T(2,128)(2,1)} %all-gather.6.cloned.1.call-done), kind=kLoop, calls=%fused_computation.194 | loop fusion | flops 2176 | bytes 13056 | tf_op jit(solution)/shard_map/convert_element_type | solution.py:95
  170.7 28.0 %all-gather.10.cloned.1.call-done = bf16[1,4352,1089]{2,1,0:T(8,128)(2,1)} async-done(((bf16[1,272,1089]{2,1,0:T(8,128)(2,1)}), bf16[1,4352,1089]{2,1,0:T(8,128)(2,1)}) %all-gather.10.cloned.1.call-update) | async-done | bytes 9478672 | tf_op jit(solution)/shard_map/all_gather | solution.py:18
  201.0 13.9 slice_bitcast_fusion
  214.9 126.1 %all-gather.8.cloned.1.call-done = bf16[1,1088,5443]{2,0,1:T(2,128)(2,1)} async-done(((bf16[1,68,5443]{2,0,1:T(2,128)(2,1)}), bf16[1,1088,5443]{2,0,1:T(2,128)(2,1)}) %all-gather.8.cloned.1.call-update) | async-done | bytes 11843984 | tf_op jit(solution)/shard_map/all_gather | solution.py:18
  340.9 45.8 %slice.205 = bf16[1,1088,4352]{2,0,1:T(2,128)(2,1)S(1)} slice(bf16[1,1088,5443]{2,0,1:T(2,128)(2,1)} %all-gather.8.cloned.1.call-done), slice={[0:1], [0:1088], [1091:5443]} | slice | bytes 18939904 | tf_op jit(solution)/shard_map/slice | solution.py:20
  394.0 31.8 %fusion.97 = (f32[1088]{0:T(1024)S(1)}, f32[1088]{0:T(1024)S(1)}, f32[1088]{0:T(1024)}) fusion(bf16[1,1088,5443]{2,0,1:T(2,128)(2,1)} %all-gather.8.cloned.1.call-done), kind=kLoop, calls=%fused_computation.188 | loop fusion | flops 3264 | bytes 19584 | tf_op jit(solution)/shard_map/convert_element_type | solution.py:101
  431.9 308.2 %while.76 = (s32[]{:T(128)}, bf16[64,1088]{1,0:T(8,128)(2,1)}, bf16[3,64,1088]{2,1,0:T(8,128)(2,1)}, bf16[3,64,3264]{2,1,0:T(8,128)(2,1)}, bf16[3,1024,2176]{2,1...) while((s32[]{:T(128)}, bf16[64,1088]{1,0:T(8,128)(2,1)}, ...), condition=%wide.region_7.8_spmd.clone, body=%wide.region_0.7_spmd.clone.sunk | while | flops 2125503488 | bytes 154849824 | solution.py:180
  444.3 51.0 %all-gather.12.cloned.1.call-done = bf16[1024,2176]{1,0:T(8,128)(2,1)} async-done(((bf16[64,2176]{1,0:T(8,128)(2,1)}), bf16[1024,2176]{1,0:T(8,128)(2,1)}) %all-gather.12.cloned.1.call-update) | async-done | bytes 4456464 | tf_op jit(solution)/shard_map/while/body/eval_jaxpr/all_gather | solution.py:143
  546.7 51.6 %all-gather.12.cloned.1.call-done = bf16[1024,2176]{1,0:T(8,128)(2,1)} async-done(((bf16[64,2176]{1,0:T(8,128)(2,1)}), bf16[1024,2176]{1,0:T(8,128)(2,1)}) %all-gather.12.cloned.1.call-update) | async-done | bytes 4456464 | tf_op jit(solution)/shard_map/while/body/eval_jaxpr/all_gather | solution.py:143
  649.6 51.6 %all-gather.12.cloned.1.call-done = bf16[1024,2176]{1,0:T(8,128)(2,1)} async-done(((bf16[64,2176]{1,0:T(8,128)(2,1)}), bf16[1024,2176]{1,0:T(8,128)(2,1)}) %all-gather.12.cloned.1.call-update) | async-done | bytes 4456464 | tf_op jit(solution)/shard_map/while/body/eval_jaxpr/all_gather | solution.py:143
  745.0 382.9 %while.77 = (s32[]{:T(128)}, bf16[64,1088]{1,0:T(8,128)(2,1)}, f32[1088]{0:T(1024)}, f32[1088]{0:T(1024)}, f32[2176]{0:T(1024)}, /*index=5*/f32[1088]{0:T(1024)}...) while((s32[]{:T(128)}, bf16[64,1088]{1,0:T(8,128)(2,1)}, ...), condition=%wide.region_27.28_spmd.clone, body=%wide.region_8.27_spmd.clone.sunk | while | flops 2855614464 | bytes 277491904 | solution.py:292
  751.4 8.0 bitcast_dynamic-update-slice_fusion.39
  789.8 25.5 %all_gather.49 = f32[34,1024,1]{0,2,1:T(1,128)S(1)} all-gather(f32[34,64,1]{0,2,1:T(1,128)S(1)} %copy.229), channel_id=1, replica_groups=mesh['section'=2,'fsdp'=16,'replica'=4] {'fsdp'}, dimensions={1}, use_global_device_ids=true | all-gather | bytes 147968 | tf_op jit(solution)/shard_map/while/body/eval_jaxpr/all_gather | solution.py:34
  877.8 8.0 bitcast_dynamic-update-slice_fusion.39
  916.2 26.0 %all_gather.49 = f32[34,1024,1]{0,2,1:T(1,128)S(1)} all-gather(f32[34,64,1]{0,2,1:T(1,128)S(1)} %copy.229), channel_id=1, replica_groups=mesh['section'=2,'fsdp'=16,'replica'=4] {'fsdp'}, dimensions={1}, use_global_device_ids=true | all-gather | bytes 147968 | tf_op jit(solution)/shard_map/while/body/eval_jaxpr/all_gather | solution.py:34
  1044.5 25.2 %all_gather.49 = f32[34,1024,1]{0,2,1:T(1,128)S(1)} all-gather(f32[34,64,1]{0,2,1:T(1,128)S(1)} %copy.229), channel_id=1, replica_groups=mesh['section'=2,'fsdp'=16,'replica'=4] {'fsdp'}, dimensions={1}, use_global_device_ids=true | all-gather | bytes 147968 | tf_op jit(solution)/shard_map/while/body/eval_jaxpr/all_gather | solution.py:34
  1150.2 249.8 %fusion.112 = (bf16[72,3264]{1,0:T(8,128)(2,1)}, bf16[80,1088]{1,0:T(8,128)(2,1)S(1)}, bf16[72,4352]{1,0:T(8,128)(2,1)S(1)}) fusion(bf16[1088,3264]{1,0:T(8,128)(2,1)} %fusion.92, bf16[1088,1088]{1,0:T(8,128)(2,1)S(1)} %fusion.93, bf16[1088,4352]{1,0:T(8,128)(2,1)} %fusion.90), kind=kCustom, calls=%all-reduce-scatter.3 | all-reduce-scatter fusion | flops 10166274 | bytes 20211200
  1430.2 65.9 %all-reduce.16 = (bf16[1088]{0:T(1024)(128)(2,1)S(1)}, bf16[1088]{0:T(1024)(128)(2,1)S(1)}, bf16[2176]{0:T(1024)(128)(2,1)S(1)}, bf16[1088]{0:T(1024)(128)(2,1)S...) all-reduce(bf16[1088]{0:T(1024)(128)(2,1)S(1)} %convert_element_typ, ...), channel_id=2, replica_groups=mesh['section'=2,'fsdp'=16,'replica'=4] {'fsdp'}, use_global_device_ids=true, to_apply=%region_28.29.clone | all-reduce | flops 13056 | bytes 52224
  1496.5 10.9 all-reduce.18
  (821 shorter events, 536.6 us)
Async XLA Ops:
  7.2 95.2 %copy-start = (bf16[2,64,1088]{2,1,0:T(8,128)(2,1)S(1)}, bf16[2,64,1088]{2,1,0:T(8,128)(2,1)}, u32[]{:S(2)}) copy-start(bf16[2,64,1088]{2,1,0:T(8,128)(2,1)} %param.20) | copy-start | bytes 835588
  7.2 111.0 %all-gather.6.cloned.1.call-start = ((), (), s32[]{:S(2)}) async-start(), calls=%async_computation.1 | async-start | bytes 15388672 | tf_op jit(solution)/shard_map/all_gather | solution.py:18
  16.0 182.7 %all-gather.10.cloned.1.call-start = ((), (), s32[]{:S(2)}) async-start(), calls=%async_computation.3 | async-start | bytes 10653696 | tf_op jit(solution)/shard_map/all_gather | solution.py:18
  17.4 323.6 %all-gather.8.cloned.1.call-start = ((), (), s32[]{:S(2)}) async-start(), calls=%async_computation.2 | async-start | bytes 25450496 | tf_op jit(solution)/shard_map/all_gather | solution.py:18
  432.1 63.3 %all-gather.12.cloned.1.call-start = ((), (), s32[]{:S(2)}) async-start(), calls=%async_computation.6 | async-start | bytes 4734976 | tf_op jit(solution)/shard_map/while/body/eval_jaxpr/all_gather | solution.py:143
  526.7 7.6 collective-permute-start
  534.4 63.8 %all-gather.12.cloned.1.call-start = ((), (), s32[]{:S(2)}) async-start(), calls=%async_computation.6 | async-start | bytes 4734976 | tf_op jit(solution)/shard_map/while/body/eval_jaxpr/all_gather | solution.py:143
  629.6 7.6 collective-permute-start
  637.3 63.9 %all-gather.12.cloned.1.call-start = ((), (), s32[]{:S(2)}) async-start(), calls=%async_computation.6 | async-start | bytes 4734976 | tf_op jit(solution)/shard_map/while/body/eval_jaxpr/all_gather | solution.py:143
  732.5 7.6 collective-permute-start
  745.4 86.0 %all-gather.14.cloned.1.call-start = ((), (), s32[]{:S(2)}) async-start(), calls=%async_computation.7 | async-start | bytes 4734976 | tf_op jit(solution)/shard_map/while/body/eval_jaxpr/all_gather | solution.py:34
  863.7 8.0 collective-permute-start.1
  871.8 87.8 %all-gather.14.cloned.1.call-start = ((), (), s32[]{:S(2)}) async-start(), calls=%async_computation.7 | async-start | bytes 4734976 | tf_op jit(solution)/shard_map/while/body/eval_jaxpr/all_gather | solution.py:34
  992.0 8.1 collective-permute-start.1
  1000.2 87.1 %all-gather.14.cloned.1.call-start = ((), (), s32[]{:S(2)}) async-start(), calls=%async_computation.7 | async-start | bytes 4734976 | tf_op jit(solution)/shard_map/while/body/eval_jaxpr/all_gather | solution.py:34
  1119.6 8.1 collective-permute-start.1
  1127.9 300.1 %reduce-scatter.8.cloned.1.call-start = ((), (), s32[]{:S(2)}) async-start(), calls=%async_computation.4 | async-start | bytes 10653696 | tf_op jit(solution)/shard_map/reduce_scatter | solution.py:341
  1135.9 377.1 %all-reduce.23.cloned.1.call-start = ((), (), s32[]{:S(2)}) async-start(), calls=%async_computation.5 | async-start | bytes 3796992 | tf_op jit(solution)/shard_map/psum | solution.py:351
  1400.0 15.9 %collective-permute-start.3 = (bf16[80,1088]{1,0:T(8,128)(2,1)S(1)}, bf16[80,1088]{1,0:T(8,128)(2,1)S(1)}, u32[]{:S(2)}, u32[]{:S(2)}) collective-permute-start(bf16[80,1088]{1,0:T(8,128)(2,1)S(1)} %get-tuple-element.1842), channel_id=1, source_target_pairs={{0,4},{4,8},{8,12},{12,16},{16,20},{20,24},{24,28},{28,32},{32,36}... | collective-permute-start | bytes 522248
  1401.5 14.5 collective-permute-start.4
  1407.3 11.3 collective-permute-start.2
  1411.1 4.9 collective-permute-start.5
  1414.6 8.9 collective-permute-start.6
  1423.5 88.1 %copy-start.26 = (bf16[3,64,1088]{2,1,0:T(8,128)(2,1)S(1)}, bf16[3,64,1088]{2,1,0:T(8,128)(2,1)}, u32[]{:S(2)}) copy-start(bf16[3,64,1088]{2,1,0:T(8,128)(2,1)} %get-tuple-element.1052) | copy-start | bytes 1253380
  (186 other events, 1731.2 us)
Sparse Core Ops, SparseCore 0:
  16.1 102.0 all-gather.5
  121.1 77.5 all-gather.9
  201.1 139.7 all-gather.7
  440.5 54.7 all-gather.11
  542.9 55.3 all-gather.11
  645.7 55.3 all-gather.11
  767.6 57.1 all-gather.13
  894.0 57.0 all-gather.13
  1022.3 56.0 all-gather.13
  1136.0 153.4 reduce-scatter.7
  1428.2 59.1 all-reduce.22
where the time goes:
time: 1540 us; the launch traced here: 1530 us
  blocking collectives  475 us (31%)
  local copies, waits for them, and re-layouts  341 us (22%)
  waiting for transfers between devices  336 us (22%)
  matrix products  190 us (12%)
  other arithmetic  133 us (9%)
  starting transfers between devices  26.2 us (2%)
  between operations  19.3 us (1%)
    unnamed x3, blocking collectives  387 us
    all_gather x3, waiting for transfers between devices, sent_together(): lax.all_gather(both, axis, axis=dim, tiled=True)  168 us
    all_gather x3, waiting for transfers between devices, forward_step(): kv_all = lax.all_gather(packed[:, D:], 'fsdp', axis=0, tiled=True)  154 us
    all_gather x3, blocking collectives, in_one_piece(): lax.all_gather(both, axis, axis=dim, tiled=True)  76.7 us
    slice x4, local copies, waits for them, and re-layouts, sent_together(): piece = filled[..., at:at + column.shape[along]]  72.3 us
    dot_general x12, matrix products, matmul_right_t(): lax.dot_general(left, right, (((1,), (1,)), ((), ())), preferred_element_...  53.5 us
    dot_general x12, matrix products, matmul(): return jnp.dot(left, right, preferred_element_type=jnp.float32)  43.9 us
    slice x12, local copies, waits for them, and re-layouts, in_one_piece(): lax.slice_in_dim(filled, at, at + a.shape[along], axis=along)  41.5 us
  transfers between devices with their start and end apart: 22, of which 9 were waited for; matrix products, arithmetic and copies ran while one was open for 34% of the time, Pallas kernels for 0%

commit v1 on v0

v1 whole, which is shorter than its diff:
```python
import jax
import jax.numpy as jnp
from jax import lax
from jax.experimental import pallas as pl
from jax.experimental.pallas import tpu as pltpu
from jax.sharding import PartitionSpec as P

D = 1088
HEADS = 17
HEAD_DIM = 64
FF = 4352
SHARDS = 16
DROWS = D // SHARDS
PROWS = 72
KPAD = SHARDS * PROWS
LANES = 1152
PAIRS = 9
FROWS = FF // SHARDS
SPLITS = FF // D
SCALE = HEAD_DIM ** (-0.5)

epsilon = 1e-05
bf16 = jnp.bfloat16
f32 = jnp.float32


def xor_pairs(k):
    return [(i, i ^ k) for i in range(SHARDS)]


def moved(value, k):
    return lax.ppermute(value, "fsdp", xor_pairs(k))


def gather_near(x):
    half = x.shape[0] // 2
    blocks = {0: x, 4: moved(x, 4), 12: moved(x, 12), 2: moved(x, 2)}
    blocks[8] = jnp.concatenate([moved(blocks[4][:half], 12), moved(blocks[12][half:], 4)], 0)
    blocks[6] = moved(blocks[2], 4)
    blocks[14] = moved(blocks[2], 12)
    blocks[10] = moved(blocks[8], 2)
    return jnp.stack([blocks[k] for k in range(0, SHARDS, 2)])


def gather_both(x):
    near = gather_near(x)
    return near, moved(near, 1)


def relative_device(me, place):
    return me ^ (2 * (place % 8) + place // 8)


def placing(me, relative):
    column = lax.broadcasted_iota(jnp.int32, (1, KPAD), 1)
    place, row = column // PROWS, column % PROWS
    owner = relative_device(me, place) if relative else place
    source = jnp.where(row < DROWS, owner * DROWS + row, -1)
    return (lax.broadcasted_iota(jnp.int32, (D, KPAD), 0) == source).astype(bf16)


def layer_norm(values, gain_vec, bias_vec):
    average = jnp.mean(values, axis=-1, keepdims=True)
    centred = values - average
    variance = jnp.mean(centred * centred, axis=-1, keepdims=True)
    return centred * lax.rsqrt(variance + epsilon) * gain_vec + bias_vec


def gelu_tanh(values):
    return jax.nn.gelu(values, approximate=True)


def matmul(left, right):
    return jnp.dot(left, right, preferred_element_type=f32)


def contract(left, right, ldim, rdim):
    return lax.dot_general(left, right, (((ldim,), (rdim,)), ((), ())), preferred_element_type=f32)


def split_two(values):
    high = lax.reduce_precision(values, 8, 7)
    return high.astype(bf16), (values - high).astype(bf16)


def unplaced(values, place):
    rows = values.shape[0]
    both = contract(jnp.concatenate(split_two(values), 0), place, 1, 1)
    return both[:rows] + both[rows:]


def two_heads(block):
    lane = lax.broadcasted_iota(jnp.int32, block.shape, 1)
    zero = jnp.zeros_like(block)
    return jnp.concatenate(
        [jnp.where(lane < HEAD_DIM, block, zero), jnp.where(lane < HEAD_DIM, zero, block)], 0
    )


def one_pair(both):
    rows = both.shape[0] // 2
    lane = lax.broadcasted_iota(jnp.int32, (rows, 128), 1)
    return jnp.where(lane < HEAD_DIM, both[:rows], both[rows:])


def rows_of(near_ref, far_ref):
    return jnp.concatenate(
        [near_ref[...].reshape(-1, 128), far_ref[...].reshape(-1, 128)], 0
    )


def forward_kernel(q_ref, kn_ref, kf_ref, vn_ref, vf_ref, bias_ref, out_ref, lse_ref):
    bias = bias_ref[0]
    keys, values = rows_of(kn_ref, kf_ref), rows_of(vn_ref, vf_ref)
    scores = contract(two_heads(q_ref[...]), keys, 1, 1) * SCALE
    scores = scores + jnp.concatenate([bias, bias], 0)
    top = jnp.max(scores, axis=1, keepdims=True)
    shifted = jnp.exp(scores - top)
    total = jnp.sum(shifted, axis=1, keepdims=True)
    probs = (shifted / total).astype(bf16)
    out_ref[...] = one_pair(matmul(probs, values)).astype(bf16)
    lse = top + jnp.log(total)
    lse_ref[0, 0] = jnp.transpose(jnp.broadcast_to(lse, (128, 128)))[:8]


def row_kernel(q_ref, do_ref, lse_ref, kn_ref, kf_ref, vn_ref, vf_ref, bias_ref, dq_ref):
    bias = bias_ref[0]
    keys, values = rows_of(kn_ref, kf_ref), rows_of(vn_ref, vf_ref)
    lse = jnp.transpose(jnp.broadcast_to(lse_ref[0, 0][:1], (128, 128)))[:, :1]
    scores = contract(two_heads(q_ref[...]), keys, 1, 1) * SCALE
    scores = scores + jnp.concatenate([bias, bias], 0)
    probs = jnp.exp(scores - lse)
    grad_probs = contract(two_heads(do_ref[...]), values, 1, 1)
    dots = jnp.sum(grad_probs * probs, axis=1, keepdims=True)
    grad_scores = (probs * (grad_probs - dots)).astype(bf16)
    dq_ref[...] = (one_pair(matmul(grad_scores, keys)) * SCALE).astype(bf16)


def column_kernel(me_ref, k_ref, v_ref, q_ref, a_ref, don_ref, dof_ref, lse_ref, bias_ref, dk_ref, dv_ref):
    me = me_ref[0]

    def ordered(ref):
        return jnp.concatenate(
            [ref[relative_device(me, place), 0, 0] for place in range(SHARDS)], 0
        )

    queries, attended, grads = ordered(q_ref), ordered(a_ref), rows_of(don_ref, dof_ref)
    rows = k_ref.shape[0]
    bias = bias_ref[0]
    lse = lse_ref[0, 0]
    product = attended.astype(f32) * grads.astype(f32)
    sides = (
        lax.broadcasted_iota(jnp.int32, (8, 128), 1) // HEAD_DIM
        == lax.broadcasted_iota(jnp.int32, (8, 128), 0)
    ).astype(bf16)
    high = product.astype(bf16)
    low = (product - high.astype(f32)).astype(bf16)
    dots = contract(sides, high, 1, 1) + contract(sides, low, 1, 1)
    spread = lambda pair: jnp.concatenate(
        [jnp.broadcast_to(pair[:1], (rows, pair.shape[1])), jnp.broadcast_to(pair[1:2], (rows, pair.shape[1]))], 0
    )
    scores = contract(two_heads(k_ref[...]), queries, 1, 1) * SCALE
    probs = jnp.exp(scores + jnp.concatenate([bias, bias], 0) - spread(lse))
    grad_probs = contract(two_heads(v_ref[...]), grads, 1, 1)
    grad_scores = (probs * (grad_probs - spread(dots))).astype(bf16)
    dk_ref[...] = (one_pair(matmul(grad_scores, queries)) * SCALE).astype(bf16)
    dv_ref[...] = one_pair(matmul(probs.astype(bf16), grads)).astype(bf16)


def kernel_call(body, n_matmuls, in_specs, out_specs, out_shape, operands):
    steps = 2 * PAIRS
    return pl.pallas_call(
        body,
        grid=(2, PAIRS),
        in_specs=in_specs,
        out_specs=out_specs,
        out_shape=out_shape,
        compiler_params=pltpu.CompilerParams(vmem_limit_bytes=32 * 1024 * 1024),
        cost_estimate=pl.CostEstimate(
            flops=steps * n_matmuls * 2 * 128 * 128 * 1024 * 4,
            bytes_accessed=steps * 2 * 1024 * 128 * 2,
            transcendentals=steps * 128 * 1024,
        ),
    )(*operands)


def own_spec(rows):
    return pl.BlockSpec((rows, 128), lambda m, h: (m, h))


def all_spec(kind, rows):
    return pl.BlockSpec((8, 1, 1, rows, 128), lambda m, h: (0, kind, m, 0, h))


def shards(
    inputs,
    segment_ids,
    sequence_order,
    ln1_gain,
    ln1_bias,
    w_qkv,
    qv_bias,
    w_out,
    out_bias,
    ln2_gain,
    ln2_bias,
    w_fc,
    fc_bias,
    w_proj,
    proj_bias,
    cotangent,
):
    section_index = lax.axis_index("section")
    me = lax.axis_index("fsdp")
    is_first = section_index == 0
    is_last = section_index == 1
    micro, span = inputs.shape[0], inputs.shape[1]
    tokens = micro * span
    seq_len = segment_ids.shape[1]

    def rows_padded(block):
        return jnp.pad(block, ((0, PROWS - block.shape[0]), (0, 0)))

    later = jnp.concatenate(
        [w_proj[0]]
        + [rows_padded(w_fc[0][:, j * D : (j + 1) * D]) for j in range(SPLITS)]
        + [rows_padded(w_out[0])],
        0,
    )
    later_all = lax.all_gather(later, "fsdp", axis=0, tiled=False)
    vectors = jnp.concatenate(
        [ln1_gain[0], ln1_bias[0], out_bias[0], ln2_gain[0], ln2_bias[0], proj_bias[0], qv_bias[0], fc_bias[0]]
    )
    vector_rows = jnp.pad(vectors[None], ((0, 7), (0, LANES - vectors.shape[0])))
    first = jnp.concatenate(
        [
            jnp.pad(w_qkv[0][:, j * D : (j + 1) * D], ((0, PROWS - DROWS), (0, LANES - D)))
            for j in range(3)
        ]
        + [vector_rows],
        0,
    )
    first_all = jnp.concatenate(gather_both(first), 0)
    weights_q, weights_k, weights_v = [
        first_all[:, j * PROWS : (j + 1) * PROWS].reshape(KPAD, LANES) for j in range(3)
    ]
    place_iota = jnp.arange(SHARDS)
    to_absolute = (relative_device(me, place_iota)[None, :] == place_iota[:, None]).astype(bf16)
    vector_all = matmul(to_absolute, first_all[:, 3 * PROWS])

    def vector(start, size):
        return vector_all[:, start : start + size].reshape(SHARDS * size)

    gain_one, bias_one, out_shift, gain_two, bias_two, proj_shift = [
        vector(j * DROWS, DROWS) for j in range(6)
    ]
    qv_full = vector(6 * DROWS, 2 * DROWS)
    fc_shift = vector(8 * DROWS, FROWS).reshape(SPLITS, 1, D)
    shift_q = jnp.pad(qv_full[:D], (0, LANES - D))
    shift_v = jnp.pad(qv_full[D:], (0, LANES - D))

    full_proj = later_all[:, :FROWS].reshape(SPLITS, D, D)
    full_fc = (
        later_all[:, FROWS : FROWS + SPLITS * PROWS]
        .reshape(SHARDS, SPLITS, PROWS, D)
        .transpose(1, 0, 2, 3)
        .reshape(SPLITS, KPAD, D)
    )
    full_out = later_all[:, FROWS + SPLITS * PROWS :].reshape(KPAD, D)

    place_rel = placing(me, True)
    place_abs = placing(me, False)

    swapped = sequence_order[0, 0] == 1
    ordered_inputs = jnp.where(swapped, inputs[::-1], inputs).reshape(tokens, D)
    ordered_segments = jnp.where(swapped, segment_ids[::-1], segment_ids)
    by_block = ordered_segments.reshape(micro, SHARDS, span)
    rel_devices = relative_device(me, place_iota)
    seg_rel = jnp.take(by_block, rel_devices, axis=1).reshape(micro, 1, seq_len)
    seg_own = lax.dynamic_index_in_dim(by_block, me, 1, keepdims=False)[:, :, None]
    pos_rel = (rel_devices[:, None] * span + jnp.arange(span)[None]).reshape(1, 1, seq_len)
    pos_own = (me * span + jnp.arange(span)).reshape(1, span, 1)
    same = seg_rel == seg_own
    row_bias = jnp.where(same & (pos_rel <= pos_own), 0.0, -1e30).astype(f32)
    column_bias = jnp.where(same & (pos_own <= pos_rel), 0.0, -1e30).astype(f32)

    bias_spec = pl.BlockSpec((1, span, seq_len), lambda m, h: (m, 0, 0))
    lse_spec = pl.BlockSpec((1, 1, 8, 128), lambda m, h: (m, h, 0, 0))
    kv_specs = [all_spec(0, span), all_spec(0, span), all_spec(1, span), all_spec(1, span)]
    token_shape = jax.ShapeDtypeStruct((tokens, LANES), bf16)

    def forward_layer(layer_in):
        layer_wide = layer_in.astype(f32)
        normed_one = layer_norm(layer_wide, gain_one, bias_one).astype(bf16)
        placed_one = matmul(normed_one, place_rel).astype(bf16)
        keys = matmul(placed_one, weights_k).astype(bf16)
        values = (matmul(placed_one, weights_v) + shift_v).astype(bf16)
        kv_near, kv_far = gather_both(jnp.concatenate([keys, values], 0))
        kv_near = kv_near.reshape(8, 2, micro, span, LANES)
        kv_far = kv_far.reshape(8, 2, micro, span, LANES)
        queries = (matmul(placed_one, weights_q) + shift_q).astype(bf16)
        attended, log_total = kernel_call(
            forward_kernel,
            2,
            [own_spec(span)] + kv_specs + [bias_spec],
            [own_spec(span), lse_spec],
            [token_shape, jax.ShapeDtypeStruct((micro, PAIRS, 8, 128), f32)],
            (queries, kv_near, kv_far, kv_near, kv_far, row_bias),
        )
        placed_att = matmul(attended[:, :D], place_abs).astype(bf16)
        hidden = layer_wide + matmul(placed_att, full_out) + out_shift
        normed_two = layer_norm(hidden, gain_two, bias_two).astype(bf16)
        placed_two = matmul(normed_two, place_abs).astype(bf16)
        pre_act = [matmul(placed_two, full_fc[j]) + fc_shift[j] for j in range(SPLITS)]
        total = hidden + proj_shift
        for j in range(SPLITS):
            total = total + matmul(gelu_tanh(pre_act[j]).astype(bf16), full_proj[j])
        out_low = total.astype(bf16)
        return out_low, (
            layer_wide, normed_one, queries, keys, values, kv_near, kv_far,
            attended, log_total, hidden, normed_two, pre_act,
        )

    sent_on, _ = forward_layer(ordered_inputs)
    received = lax.ppermute(sent_on, "section", [(0, 1)])
    layer_in = jnp.where(is_first, ordered_inputs, received)
    out_low, kept = forward_layer(layer_in)
    (
        layer_wide, normed_one, queries, keys, values, kv_near, kv_far,
        attended, log_total, hidden, normed_two, pre_act,
    ) = kept

    lse_own = log_total[:, :, 0]
    part_one = lax.reduce_precision(lse_own, 8, 7)
    part_two = lax.reduce_precision(lse_own - part_one, 8, 7)
    part_three = lse_own - part_one - part_two
    lse_rows = jnp.stack([part_one, part_two, part_three]).astype(bf16).reshape(6, LANES)
    qa_all = lax.all_gather(
        jnp.concatenate([queries, attended, lse_rows, jnp.zeros((2, LANES), bf16)], 0), "fsdp", axis=0
    )
    lse_parts = qa_all[:, 2 * tokens : 2 * tokens + 6].reshape(SHARDS, 3, micro, PAIRS, 2, span).astype(f32)
    lse_all = lse_parts[:, 0] + lse_parts[:, 1] + lse_parts[:, 2]
    lse_all = jnp.take(lse_all, rel_devices, axis=0).transpose(1, 2, 3, 0, 4).reshape(micro, PAIRS, 2, seq_len)
    lse_all = jnp.pad(lse_all, ((0, 0), (0, 0), (0, 6), (0, 0)))
    qa_tokens = qa_all[:, : 2 * tokens].reshape(SHARDS, 2, micro, span, LANES)
    nn_all = lax.all_gather(jnp.concatenate([normed_one, normed_two], 0), "fsdp", axis=0)
    me_scalar = me.astype(jnp.int32).reshape(1)

    def backward_layer(grad_out):
        grad_wide = grad_out.astype(f32)
        grad_pre = []
        grad_placed_two = 0.0
        for j in range(SPLITS):
            grad_act = contract(grad_out, full_proj[j], 1, 1)
            _, gelu_back = jax.vjp(gelu_tanh, pre_act[j])
            grad_pre.append(gelu_back(grad_act)[0].astype(bf16))
            grad_placed_two = grad_placed_two + contract(grad_pre[j], full_fc[j], 1, 1)
        _, norm_two_back = jax.vjp(layer_norm, hidden, gain_two, bias_two)
        grad_hidden_ln, grad_gain_two, grad_bias_two = norm_two_back(unplaced(grad_placed_two, place_abs))
        grad_hidden = grad_wide + grad_hidden_ln
        grad_branch = grad_hidden.astype(bf16)
        grad_att = contract(contract(grad_branch, full_out, 1, 1).astype(bf16), place_abs, 1, 1).astype(bf16)
        grad_att = jnp.pad(grad_att, ((0, 0), (0, LANES - D)))
        do_near, do_far = gather_both(grad_att)
        do_near = do_near.reshape(8, 1, micro, span, LANES)
        do_far = do_far.reshape(8, 1, micro, span, LANES)
        grad_q = kernel_call(
            row_kernel,
            3,
            [own_spec(span), own_spec(span), lse_spec] + kv_specs + [bias_spec],
            own_spec(span),
            token_shape,
            (queries, grad_att, log_total, kv_near, kv_far, kv_near, kv_far, row_bias),
        )
        whole = lambda kind: pl.BlockSpec((SHARDS, 1, 1, span, 128), lambda m, h: (0, kind, m, 0, h))
        grad_k, grad_v = kernel_call(
            column_kernel,
            5,
            [pl.BlockSpec(memory_space=pltpu.SMEM), own_spec(span), own_spec(span), whole(0), whole(1)]
            + [all_spec(0, span), all_spec(0, span)]
            + [pl.BlockSpec((1, 1, 8, seq_len), lambda m, h: (m, h, 0, 0)), bias_spec],
            [own_spec(span), own_spec(span)],
            [token_shape, token_shape],
            (me_scalar, keys, values, qa_tokens, qa_tokens, do_near, do_far, lse_all, column_bias),
        )
        grad_placed_one = (
            contract(grad_q, weights_q, 1, 1) + contract(grad_k, weights_k, 1, 1) + contract(grad_v, weights_v, 1, 1)
        )
        _, norm_one_back = jax.vjp(layer_norm, layer_wide, gain_one, bias_one)
        grad_in_ln, grad_gain_one, grad_bias_one = norm_one_back(unplaced(grad_placed_one, place_rel))
        grad_input = (grad_hidden + grad_in_ln).astype(bf16)
        norm_grads = jnp.stack([grad_gain_one, grad_bias_one, grad_gain_two, grad_bias_two])
        return grad_input, grad_branch, (grad_q, grad_k, grad_v), norm_grads

    own_cotangent = cotangent.reshape(tokens, D)
    sent_back, _, _, _ = backward_layer(own_cotangent)
    received_grad = lax.ppermute(sent_back, "section", [(1, 0)])
    grad_out = jnp.where(is_last, own_cotangent, received_grad)

    go_all = lax.all_gather(grad_out, "fsdp", axis=0).reshape(SHARDS * tokens, D)
    n1_all = nn_all[:, :tokens].reshape(SHARDS * tokens, D)
    n2_all = nn_all[:, tokens:].reshape(SHARDS * tokens, D)
    fc_block = lax.dynamic_index_in_dim(full_fc, me // 4, 0, keepdims=False)
    fc_own = lax.dynamic_slice_in_dim(fc_block, (me % 4) * FROWS, FROWS, 1)
    fc_own = matmul(place_abs, fc_own).astype(bf16)
    pre_own = matmul(n2_all, fc_own) + fc_bias[0].astype(f32)
    activ_own, gelu_own_back = jax.vjp(gelu_tanh, pre_own)
    grad_pre_own = gelu_own_back(contract(go_all, w_proj[0], 1, 1))[0].astype(bf16)
    grad_proj_w = contract(activ_own.astype(bf16), go_all, 0, 0).astype(bf16)
    grad_fc_w = contract(n2_all, grad_pre_own, 0, 0).astype(bf16)
    grad_fc_b = jnp.sum(grad_pre_own.astype(f32), axis=0)
    grad_proj_b = lax.dynamic_slice_in_dim(jnp.sum(go_all.astype(f32), axis=0), me * DROWS, DROWS)
    own_vectors = jnp.concatenate([grad_fc_b, grad_proj_b, jnp.zeros((D - FROWS - DROWS,), f32)]).astype(bf16)
    proj_rows = jnp.concatenate([grad_proj_w, jnp.pad(own_vectors[None], ((0, 7), (0, 0)))], 0)
    proj_total = lax.psum(proj_rows, "replica")

    grad_input, grad_branch, grad_qkv, norm_grads = backward_layer(grad_out)

    wide = jnp.concatenate([g[:, :D] for g in grad_qkv] + [grad_branch], 1)
    columns = lax.all_to_all(
        wide.reshape(tokens, SHARDS, FROWS).transpose(1, 0, 2), "fsdp", 0, 0
    ).reshape(SHARDS * tokens, FROWS)
    att_all = qa_all[:, tokens : 2 * tokens, :D].reshape(SHARDS * tokens, D)
    left = jnp.where(me < 12, n1_all, att_all)
    grad_columns = contract(left, columns, 0, 0).astype(bf16)
    column_sums = jnp.sum(columns.astype(f32), axis=0).astype(bf16)

    rows = jnp.concatenate(
        [
            grad_columns.reshape(SHARDS, DROWS, FROWS),
            grad_fc_w.reshape(SHARDS, DROWS, FROWS),
            norm_grads.astype(bf16).reshape(4, SHARDS, DROWS).transpose(1, 2, 0),
        ],
        2,
    )
    width = 640
    rows = jnp.pad(rows, ((0, 0), (0, 0), (0, width - rows.shape[2])))
    sums_row = jnp.broadcast_to(jnp.pad(column_sums, (0, width - FROWS))[None, None], (SHARDS, 1, width))
    rows = jnp.concatenate([rows, sums_row, jnp.zeros((SHARDS, PROWS - DROWS - 1, width), bf16)], 1)
    got = lax.all_to_all(rows, "fsdp", 0, 0)

    z = lax.axis_index("replica")
    quarter = got.reshape(4, 4, PROWS, width)
    pick = lambda k: lax.dynamic_index_in_dim(quarter, z ^ k, 0, keepdims=False)
    swap = lambda v, k: lax.ppermute(v, "replica", [(j, j ^ k) for j in range(4)])
    total = pick(0).astype(f32)
    for term in [swap(pick(k), k) for k in (1, 3, 2)]:
        total = total + term.astype(f32)
    total = total.astype(bf16)
    finished = jnp.stack([total] + [swap(total, k) for k in (1, 2, 3)])
    finished = jnp.take(finished, z ^ jnp.arange(4), axis=0).reshape(SHARDS, PROWS, width).astype(f32)

    def joined(block):
        return block.transpose(1, 0, 2).reshape(block.shape[1], -1)

    grad_w_qkv = joined(finished[:12, :DROWS, :FROWS])
    grad_w_out = joined(finished[12:, :DROWS, :FROWS])
    grad_w_fc = joined(finished[:, :DROWS, FROWS : 2 * FROWS])
    norm_sums = jnp.sum(finished[:, :DROWS, 2 * FROWS : 2 * FROWS + 4], axis=0)
    sums = finished[:, DROWS, :FROWS].reshape(SHARDS * FROWS)
    qv_sums = jnp.concatenate([sums[:D], sums[2 * D : 3 * D]])
    grad_qv_b = lax.dynamic_slice_in_dim(qv_sums, me * 2 * DROWS, 2 * DROWS)
    grad_out_b = lax.dynamic_slice_in_dim(sums, 3 * D + me * DROWS, DROWS)
    proj_total = proj_total.astype(f32)
    totals = (
        norm_sums[:, 0],
        norm_sums[:, 1],
        grad_w_qkv,
        grad_qv_b,
        grad_w_out,
        grad_out_b,
        norm_sums[:, 2],
        norm_sums[:, 3],
        grad_w_fc,
        proj_total[FROWS, :FROWS],
        proj_total[:FROWS],
        proj_total[FROWS, FROWS : FROWS + DROWS],
    )
    activations = out_low.reshape(1, micro, span, D)
    input_grads = grad_input.reshape(1, micro, span, D)
    return (activations, input_grads) + tuple((total[None] for total in totals))


def solution(mesh):
    return jax.shard_map(
        shards,
        mesh=mesh,
        in_specs=(
            P("replica", "fsdp", None),
            P("replica", None),
            P("replica", None),
            P("section", "fsdp"),
            P("section", "fsdp"),
            P("section", "fsdp", None),
            P("section", "fsdp"),
            P("section", "fsdp", None),
            P("section", "fsdp"),
            P("section", "fsdp"),
            P("section", "fsdp"),
            P("section", "fsdp", None),
            P("section", "fsdp"),
            P("section", "fsdp", None),
            P("section", "fsdp"),
            P("replica", "fsdp", None),
        ),
        out_specs=(
            P("section", "replica", "fsdp", None),
            P("section", "replica", "fsdp", None),
            P("section", "fsdp"),
            P("section", "fsdp"),
            P("section", "fsdp", None),
            P("section", "fsdp"),
            P("section", "fsdp", None),
            P("section", "fsdp"),
            P("section", "fsdp"),
            P("section", "fsdp"),
            P("section", "fsdp", None),
            P("section", "fsdp"),
            P("section", "fsdp", None),
            P("section", "fsdp"),
        ),
        check_vma=False,
    )
```

time: 1540 us -> 836 us (0.54)
  blocking collectives: 475 us -> 0 us
  waiting for transfers between devices: 336 us -> 218 us
  local copies, waits for them, and re-layouts: 341 us -> 231 us
  other arithmetic: 133 us -> 27 us
  Pallas kernels: 0 us -> 89.4 us
  starting transfers between devices: 26.2 us -> 88.1 us
  matrix products: 190 us -> 154 us
    unnamed x3 -> x0, blocking collectives: 387 us -> none
    all_gather x9 -> x4, waiting for transfers between devices: 322 us -> 0.95 us  [the longest x1 0.91 us: shards(): later_all = lax.all_gather(later, 'fsdp', axis=0, tiled=False)]
    ppermute x6 -> x53, waiting for transfers between devices: 13.9 us -> 165 us  [the longest x45 142 us: moved(): return lax.ppermute(value, 'fsdp', xor_pairs(k))]
    slice x50 -> x36, local copies, waits for them, and re-layouts: 174 us -> 79.3 us  [the longest x1 15.3 us: shards(): later_all[:, FROWS:FROWS + SPLITS * PROWS].reshape(SHARDS, SPLITS, PROWS, D)]
    pallas_call x0 -> x6, Pallas kernels: none -> 89.4 us  [kernel_call(): pl.pallas_call(body, grid=(2, PAIRS), in_specs=in_specs, out_specs=out_sp...]
    all_gather x3 -> x0, blocking collectives: 76.7 us -> none  [in_one_piece(): lax.all_gather(both, axis, axis=dim, tiled=True)]
    ppermute x6 -> x53, starting transfers between devices: 13.2 us -> 78.3 us  [the longest x45 65.5 us: moved(): return lax.ppermute(value, 'fsdp', xor_pairs(k))]
    unnamed x84 -> x250, local copies, waits for them, and re-layouts: 35.5 us -> 97.5 us
  transfers between devices with their start and end apart: 22 -> 60, of which waited for: 9 -> 33; matrix products, arithmetic and copies ran while one was open for 34% -> 27% of each run, Pallas kernels for 0% -> 9%
where the time goes in v1:
time: 836 us; the launch traced here: 823 us
  local copies, waits for them, and re-layouts  231 us (28%)
  waiting for transfers between devices  218 us (26%)
  matrix products  154 us (18%)
  Pallas kernels  89.4 us (11%)
  starting transfers between devices  88.1 us (11%)
  other arithmetic  27 us (3%)
  between operations  16.3 us (2%)
    ppermute x45, waiting for transfers between devices, moved(): return lax.ppermute(value, 'fsdp', xor_pairs(k))  142 us
    unnamed x250, local copies, waits for them, and re-layouts  97.5 us
    dot_general x24, matrix products, contract(): lax.dot_general(left, right, (((ldim,), (rdim,)), ((), ())), preferred_el...  91.6 us
    pallas_call x6, Pallas kernels, kernel_call(): pl.pallas_call(body, grid=(2, PAIRS), in_specs=in_specs, out_specs=out_sp...  89.4 us
    ppermute x45, starting transfers between devices, moved(): return lax.ppermute(value, 'fsdp', xor_pairs(k))  65.5 us
    dot_general x26, matrix products, matmul(): return jnp.dot(left, right, preferred_element_type=f32)  62.5 us
    psum x1, waiting for transfers between devices, shards(): proj_total = lax.psum(proj_rows, 'replica')  28.1 us
  transfers between devices with their start and end apart: 60, of which 33 were waited for; matrix products, arithmetic and copies ran while one was open for 27% of the time, Pallas kernels for 9%

profile of v1, /device:TPU:0, one launch (start us, length us, event | category | flops | bytes accessed | tf_op | source)
XLA Modules:
  0.0 823.4 jit_solution(7123082439830017738)
XLA Ops:
  48.1 18.2 %collective-permute-done.2 = bf16[224,1152]{1,0:T(8,128)(2,1)S(1)} collective-permute-done((bf16[224,1152]{1,0:T(8,128)(2,1)S(1)}, bf16[224,1152]{1,0:T(8,128)(2,1)S(1)}, u32[]{:S(2)}, u32[]{:S(2)}) %collective-permute-start.2) | collective-permute-done | bytes 516128 | tf_op jit(solution)/shard_map/ppermute | solution.py:32
  99.6 15.8 %collective-permute-done.10 = bf16[256,1152]{1,0:T(8,128)(2,1)S(1)} collective-permute-done((bf16[256,1152]{1,0:T(8,128)(2,1)S(1)}, bf16[256,1152]{1,0:T(8,128)(2,1)S(1)}, u32[]{:S(2)}, u32[]{:S(2)}) %collective-permute-start.10) | collective-permute-done | bytes 589856 | tf_op jit(solution)/shard_map/ppermute | solution.py:32
  118.3 7.5 collective-permute-done.9
  134.4 8.2 collective-permute-done.11
  144.4 15.7 %collective-permute-done.15 = bf16[256,1152]{1,0:T(8,128)(2,1)S(1)} collective-permute-done((bf16[256,1152]{1,0:T(8,128)(2,1)S(1)}, bf16[256,1152]{1,0:T(8,128)(2,1)S(1)}, u32[]{:S(2)}, u32[]{:S(2)}) %collective-permute-start.15) | collective-permute-done | bytes 589856 | tf_op jit(solution)/shard_map/ppermute | solution.py:32
  171.3 16.5 %shard_map.263 = (bf16[128,1152]{1,0:T(8,128)(2,1)S(1)}, f32[2,9,8,128]{3,2,1,0:T(8,128)}) custom-call(bf16[128,1152]{1,0:T(8,128)(2,1)S(1)} %fusion.43.q_ref, bf16[8,2,2,64,1152]{4,3,2,1,0:T(8,128)(2,1)S(1)} %constant_dynamic-update-slice_fusion.5.kn_ref.vn_ref, bf16[8,2,2,64,1152]{4,3,2,1,0:T(8,128)(2,1)} %bitcast.36.kf_ref.vf_ref, ...), custom_call_target="tpu_custom_call" | custom-call | flops 4831838208 | bytes 9437184 | tf_op jit(solution)/shard_map/pallas_call | solution.py:172
  204.0 15.3 %slice.421 = bf16[16,288,1088]{1,2,0:T(8,128)(2,1)} slice(bf16[16,632,1088]{1,2,0:T(8,128)(2,1)} %all-gather.16.cloned.1.call-done), slice={[0:16], [272:560], [0:1088]} | slice | bytes 20054016 | tf_op jit(solution)/shard_map/slice | solution.py:264
  219.2 15.3 %copy.292 = bf16[16,288,1088]{2,1,0:T(8,128)(2,1)} copy(bf16[16,288,1088]{1,2,0:T(8,128)(2,1)} %slice.421) | data formatting | bytes 20054016
  234.6 7.7 fusion.419
  242.3 9.8 %fusion.418 = (bf16[4,272,1088]{1,2,0:T(8,128)(2,1)}, bf16[4,272,1088]{1,2,0:T(8,128)(2,1)}, bf16[4,272,1088]{1,2,0:T(8,128)(2,1)}, bf16[4,272,1088]{1,2,0:T(8,128)(2,1)}) fusion(bf16[16,632,1088]{1,2,0:T(8,128)(2,1)} %all-gather.16.cloned.1.call-done), kind=kLoop, calls=%fused_computation.708 | loop fusion | bytes 18939904 | tf_op jit(solution)/shard_map/slice | solution.py:317
  308.0 9.8 %collective-permute-done.20 = bf16[256,1152]{1,0:T(8,128)(2,1)S(1)} collective-permute-done((bf16[256,1152]{1,0:T(8,128)(2,1)S(1)}, bf16[256,1152]{1,0:T(8,128)(2,1)S(1)}, u32[]{:S(2)}, u32[]{:S(2)}) %collective-permute-start.20) | collective-permute-done | bytes 589856 | tf_op jit(solution)/shard_map/ppermute | solution.py:32
  351.6 13.2 %shard_map.264 = (bf16[128,1152]{1,0:T(8,128)(2,1)S(1)}, f32[2,9,8,128]{3,2,1,0:T(8,128)S(1)}) custom-call(bf16[128,1152]{1,0:T(8,128)(2,1)S(1)} %fusion.46.q_ref, bf16[8,2,2,64,1152]{4,3,2,1,0:T(8,128)(2,1)S(1)} %constant_dynamic-update-slice_fusion.15.kn_ref.vn_ref, bf16[8,2,2,64,1152]{4,3,2,1,0:T(8,128)(2,1)S(1)} %bitcast.369, ...), custom_call_target="tpu_custom_call" | custom-call | flops 4831838208 | bytes 9437184 | tf_op jit(solution)/shard_map/pallas_call | solution.py:172
  367.5 9.4 %copy.271 = bf16[4,16,72,1088]{3,2,1,0:T(8,128)(2,1)} copy(bf16[4,16,72,1088]{3,2,0,1:T(8,128)(2,1)} %bitcast.389) | data formatting | bytes 20054016 | tf_op jit(solution)/shard_map/transpose | solution.py:266
  400.8 7.1 convolution_add_fusion.16
  442.2 12.6 %shard_map.265 = bf16[128,1152]{1,0:T(8,128)(2,1)S(1)} custom-call(bf16[128,1152]{1,0:T(8,128)(2,1)S(1)} %fusion.46.q_ref, bf16[128,1152]{1,0:T(8,128)(2,1)S(1)} %pad.71.do_ref, f32[2,9,8,128]{3,2,1,0:T(8,128)S(1)} %get-tuple-element.23.lse_ref, bf16[8,2,2,64,1152]{4,3,2,1,0:T(8,128)(2,1)S(1)} %bitcast.368, bf16[8,2,2,64,1152]{4,3,2,1,0:T(8,128)(2,1)S(1)} %bitcast.373, ...), custom_call_target="tpu_custom_call" | custom-call | flops 7247757312 | bytes 9437184 | tf_op jit(solution)/shard_map/pallas_call | solution.py:172
  466.5 8.3 %collective-permute-done.30 = bf16[128,1152]{1,0:T(8,128)(2,1)S(1)} collective-permute-done((bf16[128,1152]{1,0:T(8,128)(2,1)S(1)}, bf16[128,1152]{1,0:T(8,128)(2,1)S(1)}, u32[]{:S(2)}, u32[]{:S(2)}) %collective-permute-start.30) | collective-permute-done | bytes 294944 | tf_op jit(solution)/shard_map/ppermute | solution.py:32
  483.3 8.3 %slice.438 = bf16[16,256,1152]{2,1,0:T(8,128)(2,1)} slice(bf16[16,264,1152]{2,1,0:T(8,128)(2,1)} %bitcast.435), slice={[0:16], [0:256], [0:1152]} | slice | bytes 18874368 | tf_op jit(solution)/shard_map/slice | solution.py:345
  509.2 17.3 %shard_map.266 = (bf16[128,1152]{1,0:T(8,128)(2,1)S(1)}, bf16[128,1152]{1,0:T(8,128)(2,1)S(1)}) custom-call(s32[1]{0:T(128)} %bitcast.79.me_ref, bf16[128,1152]{1,0:T(8,128)(2,1)S(1)} %convolution_convert_fusion.4.k_ref, bf16[128,1152]{1,0:T(8,128)(2,1)S(1)} %fusion.47.v_ref, bf16[16,2,2,64,1152]{4,3,2,1,0:T(8,128)(2,1)S(1)} %bitcast.377, ...), custom_call_target="tpu_custom_call" | custom-call | flops 12079595520 | bytes 9437184 | tf_op jit(solution)/shard_map/pallas_call | solution.py:172
  534.7 8.6 %fusion.420 = (bf16[16,128,1088]{2,1,0:T(8,128)(2,1)}, bf16[16,128,1088]{2,1,0:T(8,128)(2,1)}) fusion(bf16[16,256,1088]{2,1,0:T(8,128)(2,1)} %bitcast.438), kind=kLoop, calls=%fused_computation.710 | loop fusion | bytes 17825792 | tf_op jit(solution)/shard_map/slice | solution.py:401
  636.4 12.6 %shard_map.267 = bf16[128,1152]{1,0:T(8,128)(2,1)S(1)} custom-call(bf16[128,1152]{1,0:T(8,128)(2,1)S(1)} %fusion.46.q_ref, bf16[128,1152]{1,0:T(8,128)(2,1)S(1)} %pad.73.do_ref, f32[2,9,8,128]{3,2,1,0:T(8,128)S(1)} %get-tuple-element.23.lse_ref, bf16[8,2,2,64,1152]{4,3,2,1,0:T(8,128)(2,1)S(1)} %copy-done.1, bf16[8,2,2,64,1152]{4,3,2,1,0:T(8,128)(2,1)S(1)} %bitcast.375, ...), custom_call_target="tpu_custom_call" | custom-call | flops 7247757312 | bytes 9437184 | tf_op jit(solution)/shard_map/pallas_call | solution.py:172
  650.5 17.3 %shard_map.268 = (bf16[128,1152]{1,0:T(8,128)(2,1)S(1)}, bf16[128,1152]{1,0:T(8,128)(2,1)S(1)}) custom-call(s32[1]{0:T(128)} %bitcast.79.me_ref, bf16[128,1152]{1,0:T(8,128)(2,1)S(1)} %convolution_convert_fusion.4.k_ref, bf16[128,1152]{1,0:T(8,128)(2,1)S(1)} %fusion.47.v_ref, bf16[16,2,2,64,1152]{4,3,2,1,0:T(8,128)(2,1)S(1)} %bitcast.381, ...), custom_call_target="tpu_custom_call" | custom-call | flops 12079595520 | bytes 9437184 | tf_op jit(solution)/shard_map/pallas_call | solution.py:172
  685.7 10.9 %all-to-all-done = bf16[16,128,272]{1,2,0:T(8,128)(2,1)} async-done(((bf16[16,128,272]{1,2,0:T(8,128)(2,1)}), bf16[16,128,272]{1,2,0:T(8,128)(2,1)}, u32[]{:S(2)}, u32[]{:S(2)}) %all-to-all-start) | async-done | bytes 1114144 | tf_op jit(solution)/shard_map/all_to_all | solution.py:420
  731.1 13.1 %all-to-all-done.1 = bf16[16,72,640]{2,1,0:T(8,128)(2,1)S(1)} async-done(((bf16[16,72,640]{2,1,0:T(8,128)(2,1)}), bf16[16,72,640]{2,1,0:T(8,128)(2,1)S(1)}, u32[]{:S(2)}, u32[]{:S(2)}) %all-to-all-start.1) | async-done | bytes 1474592 | tf_op jit(solution)/shard_map/all_to_all | solution.py:440
  750.3 28.1 %all-reduce.19.cloned.1.call-done = bf16[280,1088]{1,0:T(8,128)(2,1)} async-done(((bf16[280,1088]{1,0:T(8,128)(2,1)}), bf16[280,1088]{1,0:T(8,128)(2,1)}) %all-reduce.19.cloned.1.call-update) | async-done | bytes 609296 | tf_op jit(solution)/shard_map/psum | solution.py:415
  (618 shorter events, 500.7 us)
Async XLA Ops:
  7.2 181.4 %all-gather.16.cloned.1.call-start = ((), (), s32[]{:S(2)}) async-start(), calls=%async_computation.6 | async-start | bytes 23674880 | tf_op jit(solution)/shard_map/all_gather | solution.py:230
  13.0 468.6 %all-gather.10.cloned.1.call-start = ((), (), s32[]{:S(2)}) async-start(), calls=%async_computation.3 | async-start | bytes 10340352 | tf_op jit(solution)/shard_map/all_gather | solution.py:338
  36.5 29.8 %collective-permute-start.2 = (bf16[224,1152]{1,0:T(8,128)(2,1)S(1)}, bf16[224,1152]{1,0:T(8,128)(2,1)S(1)}, u32[]{:S(2)}, u32[]{:S(2)}) collective-permute-start(bf16[224,1152]{1,0:T(8,128)(2,1)S(1)} %collective-permute-done), channel_id=1, source_target_pairs={{0,16},{4,20},{8,24},{12,28},{16,0},{20,4},{24,8},{28,12},{32,48},... | collective-permute-start | bytes 1548296 | tf_op jit(solution)/shard_map/ppermute | solution.py:32
  36.5 34.0 %collective-permute-start.7 = (bf16[224,1152]{1,0:T(8,128)(2,1)S(1)}, bf16[224,1152]{1,0:T(8,128)(2,1)S(1)}, u32[]{:S(2)}, u32[]{:S(2)}) collective-permute-start(bf16[224,1152]{1,0:T(8,128)(2,1)S(1)} %collective-permute-done), channel_id=1, source_target_pairs={{0,48},{4,52},{8,56},{12,60},{16,32},{20,36},{24,40},{28,44},{32,1... | collective-permute-start | bytes 1548296 | tf_op jit(solution)/shard_map/ppermute | solution.py:32
  45.0 23.4 %collective-permute-start.6 = (bf16[224,1152]{1,0:T(8,128)(2,1)S(1)}, bf16[224,1152]{1,0:T(8,128)(2,1)S(1)}, u32[]{:S(2)}, u32[]{:S(2)}) collective-permute-start(bf16[224,1152]{1,0:T(8,128)(2,1)S(1)} %constant_dynamic-update-slice_fusion), channel_id=1, source_target_pairs={{0,8},{4,12},{8,0},{12,4},{16,24},{20,28},{24,16},{28,20},{32,40},... | collective-permute-start | bytes 1548296 | tf_op jit(solution)/shard_map/ppermute | solution.py:32
  94.1 23.5 %collective-permute-start.13 = (bf16[256,1152]{1,0:T(8,128)(2,1)S(1)}, bf16[256,1152]{1,0:T(8,128)(2,1)S(1)}, u32[]{:S(2)}, u32[]{:S(2)}) collective-permute-start(bf16[256,1152]{1,0:T(8,128)(2,1)S(1)} %pad_maximum_fusion.1), channel_id=1, source_target_pairs={{0,48},{4,52},{8,56},{12,60},{16,32},{20,36},{24,40},{28,44},{32,1... | collective-permute-start | bytes 1769480 | tf_op jit(solution)/shard_map/ppermute | solution.py:32
  95.9 29.9 %collective-permute-start.9 = (bf16[256,1152]{1,0:T(8,128)(2,1)S(1)}, bf16[256,1152]{1,0:T(8,128)(2,1)S(1)}, u32[]{:S(2)}, u32[]{:S(2)}) collective-permute-start(bf16[256,1152]{1,0:T(8,128)(2,1)S(1)} %pad_maximum_fusion.1), channel_id=1, source_target_pairs={{0,8},{4,12},{8,0},{12,4},{16,24},{20,28},{24,16},{28,20},{32,40},... | collective-permute-start | bytes 1769480 | tf_op jit(solution)/shard_map/ppermute | solution.py:32
  127.1 34.9 %collective-permute-start.16 = (bf16[256,1152]{1,0:T(8,128)(2,1)S(1)}, bf16[256,1152]{1,0:T(8,128)(2,1)S(1)}, u32[]{:S(2)}, u32[]{:S(2)}) collective-permute-start(bf16[256,1152]{1,0:T(8,128)(2,1)S(1)} %collective-permute-done.9), channel_id=1, source_target_pairs={{0,48},{4,52},{8,56},{12,60},{16,32},{20,36},{24,40},{28,44},{32,1... | collective-permute-start | bytes 1769480 | tf_op jit(solution)/shard_map/ppermute | solution.py:32
  130.3 29.8 %collective-permute-start.15 = (bf16[256,1152]{1,0:T(8,128)(2,1)S(1)}, bf16[256,1152]{1,0:T(8,128)(2,1)S(1)}, u32[]{:S(2)}, u32[]{:S(2)}) collective-permute-start(bf16[256,1152]{1,0:T(8,128)(2,1)S(1)} %constant_dynamic-update-slice_fusion.3), channel_id=1, source_target_pairs={{0,8},{4,12},{8,0},{12,4},{16,24},{20,28},{24,16},{28,20},{32,40},... | collective-permute-start | bytes 1769480 | tf_op jit(solution)/shard_map/ppermute | solution.py:32
  366.0 168.7 %all-gather.12.cloned.1.call-start = ((), (), s32[]{:S(2)}) async-start(), calls=%async_computation.4 | async-start | bytes 10027008 | tf_op jit(solution)/shard_map/all_gather | solution.py:346
  388.6 314.5 %all-gather.14.cloned.1.call-start = ((), (), s32[]{:S(2)}) async-start(), calls=%async_computation.5 | async-start | bytes 5013504 | tf_op jit(solution)/shard_map/all_gather | solution.py:400
  429.8 29.6 %collective-permute-start.28 = (bf16[128,1152]{1,0:T(8,128)(2,1)S(1)}, bf16[128,1152]{1,0:T(8,128)(2,1)S(1)}, u32[]{:S(2)}, u32[]{:S(2)}) collective-permute-start(bf16[128,1152]{1,0:T(8,128)(2,1)S(1)} %pad.71.do_ref), channel_id=1, source_target_pairs={{0,8},{4,12},{8,0},{12,4},{16,24},{20,28},{24,16},{28,20},{32,40},... | collective-permute-start | bytes 884744 | tf_op jit(solution)/shard_map/ppermute | solution.py:32
  433.2 23.1 %collective-permute-start.29 = (bf16[128,1152]{1,0:T(8,128)(2,1)S(1)}, bf16[128,1152]{1,0:T(8,128)(2,1)S(1)}, u32[]{:S(2)}, u32[]{:S(2)}) collective-permute-start(bf16[128,1152]{1,0:T(8,128)(2,1)S(1)} %pad.71.do_ref), channel_id=1, source_target_pairs={{0,16},{4,20},{8,24},{12,28},{16,0},{20,4},{24,8},{28,12},{32,48},... | collective-permute-start | bytes 884744 | tf_op jit(solution)/shard_map/ppermute | solution.py:32
  433.2 25.3 %collective-permute-start.32 = (bf16[128,1152]{1,0:T(8,128)(2,1)S(1)}, bf16[128,1152]{1,0:T(8,128)(2,1)S(1)}, u32[]{:S(2)}, u32[]{:S(2)}) collective-permute-start(bf16[128,1152]{1,0:T(8,128)(2,1)S(1)} %pad.71.do_ref), channel_id=1, source_target_pairs={{0,48},{4,52},{8,56},{12,60},{16,32},{20,36},{24,40},{28,44},{32,1... | collective-permute-start | bytes 884744 | tf_op jit(solution)/shard_map/ppermute | solution.py:32
  480.1 23.6 %collective-permute-start.36 = (bf16[8,128,1152]{2,1,0:T(8,128)(2,1)}, bf16[8,128,1152]{2,1,0:T(8,128)(2,1)}, u32[]{:S(2)}, u32[]{:S(2)}) collective-permute-start(bf16[8,128,1152]{2,1,0:T(8,128)(2,1)} %bitcast_dynamic-update-slice_fusion.40), channel_id=1, source_target_pairs={{0,4},{4,0},{8,12},{12,8},{16,20},{20,16},{24,28},{28,24},{32,36},... | collective-permute-start | bytes 7077896 | tf_op jit(solution)/shard_map/ppermute | solution.py:32
  577.1 31.5 %collective-permute-start.38 = (bf16[128,1152]{1,0:T(8,128)(2,1)S(1)}, bf16[128,1152]{1,0:T(8,128)(2,1)}, u32[]{:S(2)}, u32[]{:S(2)}) collective-permute-start(bf16[128,1152]{1,0:T(8,128)(2,1)S(1)} %pad.73.do_ref), channel_id=1, source_target_pairs={{0,8},{4,12},{8,0},{12,4},{16,24},{20,28},{24,16},{28,20},{32,40},... | collective-permute-start | bytes 884744 | tf_op jit(solution)/shard_map/ppermute | solution.py:32
  577.4 29.6 %collective-permute-start.39 = (bf16[128,1152]{1,0:T(8,128)(2,1)S(1)}, bf16[128,1152]{1,0:T(8,128)(2,1)S(1)}, u32[]{:S(2)}, u32[]{:S(2)}) collective-permute-start(bf16[128,1152]{1,0:T(8,128)(2,1)S(1)} %pad.73.do_ref), channel_id=1, source_target_pairs={{0,16},{4,20},{8,24},{12,28},{16,0},{20,4},{24,8},{28,12},{32,48},... | collective-permute-start | bytes 884744 | tf_op jit(solution)/shard_map/ppermute | solution.py:32
  579.1 29.4 %collective-permute-start.42 = (bf16[128,1152]{1,0:T(8,128)(2,1)S(1)}, bf16[128,1152]{1,0:T(8,128)(2,1)S(1)}, u32[]{:S(2)}, u32[]{:S(2)}) collective-permute-start(bf16[128,1152]{1,0:T(8,128)(2,1)S(1)} %pad.73.do_ref), channel_id=1, source_target_pairs={{0,48},{4,52},{8,56},{12,60},{16,32},{20,36},{24,40},{28,44},{32,1... | collective-permute-start | bytes 884744 | tf_op jit(solution)/shard_map/ppermute | solution.py:32
  672.3 24.3 %all-to-all-start = ((bf16[16,128,272]{1,2,0:T(8,128)(2,1)}), bf16[16,128,272]{1,2,0:T(8,128)(2,1)}, u32[]{:S(2)}, u32[]{:S(2)}) async-start(bf16[16,128,272]{1,2,0:T(8,128)(2,1)} %bitcast.445), calls=%async_computation | async-start | bytes 2228224 | tf_op jit(solution)/shard_map/all_to_all | solution.py:420
  717.9 26.3 %all-to-all-start.1 = ((bf16[16,72,640]{2,1,0:T(8,128)(2,1)}), bf16[16,72,640]{2,1,0:T(8,128)(2,1)S(1)}, u32[]{:S(2)}, u32[]{:S(2)}) async-start(bf16[16,72,640]{2,1,0:T(8,128)(2,1)} %maximum_maximum_fusion), calls=%async_computation.1 | async-start | bytes 2949120 | tf_op jit(solution)/shard_map/all_to_all | solution.py:440
  721.6 56.8 %all-reduce.19.cloned.1.call-start = ((), (), s32[]{:S(2)}) async-start(), calls=%async_computation.2 | async-start | bytes 1290240 | tf_op jit(solution)/shard_map/psum | solution.py:415
  745.2 36.9 %collective-permute-start.47 = (bf16[4,72,640]{2,1,0:T(8,128)(2,1)}, bf16[4,72,640]{2,1,0:T(8,128)(2,1)}, u32[]{:S(2)}, u32[]{:S(2)}) collective-permute-start(bf16[4,72,640]{2,1,0:T(8,128)(2,1)} %get-tuple-element.140), channel_id=1, source_target_pairs={{0,1},{1,0},{2,3},{3,2},{4,5},{5,4},{6,7},{7,6},{8,9},{9,8},{10,11... | collective-permute-start | bytes 1105928 | tf_op jit(solution)/shard_map/ppermute | solution.py:445
  745.5 36.5 %collective-permute-start.48 = (bf16[4,72,640]{2,1,0:T(8,128)(2,1)}, bf16[4,72,640]{2,1,0:T(8,128)(2,1)}, u32[]{:S(2)}, u32[]{:S(2)}) collective-permute-start(bf16[4,72,640]{2,1,0:T(8,128)(2,1)} %get-tuple-element.142), channel_id=1, source_target_pairs={{0,3},{1,2},{2,1},{3,0},{4,7},{5,6},{6,5},{7,4},{8,11},{9,10},{10,... | collective-permute-start | bytes 1105928 | tf_op jit(solution)/shard_map/ppermute | solution.py:445
  747.7 34.4 %collective-permute-start.49 = (bf16[4,72,640]{2,1,0:T(8,128)(2,1)}, bf16[4,72,640]{2,1,0:T(8,128)(2,1)}, u32[]{:S(2)}, u32[]{:S(2)}) collective-permute-start(bf16[4,72,640]{2,1,0:T(8,128)(2,1)} %get-tuple-element.141), channel_id=1, source_target_pairs={{0,2},{1,3},{2,0},{3,1},{4,6},{5,7},{6,4},{7,5},{8,10},{9,11},{10,... | collective-permute-start | bytes 1105928 | tf_op jit(solution)/shard_map/ppermute | solution.py:445
  (123 other events, 1511.6 us)
Sparse Core Ops, SparseCore 0:
  13.2 175.4 all-gather.15
  366.1 84.3 all-gather.9
  452.9 80.5 all-gather.11
  606.4 58.1 all-gather.13
  731.2 47.1 all-reduce.18

commit v2 on v1

v2 whole, which is shorter than its diff:
```python
import jax
import jax.numpy as jnp
from jax import lax
from jax.experimental import pallas as pl
from jax.experimental.pallas import tpu as pltpu
from jax.sharding import PartitionSpec as P

D = 1088
HEADS = 17
HEAD_DIM = 64
FF = 4352
SHARDS = 16
DROWS = D // SHARDS
PROWS = 80
KPAD = SHARDS * PROWS
LANES = 1152
PAIRS = 9
FROWS = FF // SHARDS
SPLITS = FF // D
SCALE = HEAD_DIM ** (-0.5)

HALF = KPAD // 2
OUT_AT = SPLITS * PROWS
PROJ_AT = OUT_AT + PROWS
GELU_C = 0.7978845608028654
GELU_A = 0.044715

epsilon = 1e-05
bf16 = jnp.bfloat16
f32 = jnp.float32


def xor_pairs(k):
    return [(i, i ^ k) for i in range(SHARDS)]


def moved(value, k):
    return lax.ppermute(value, "fsdp", xor_pairs(k))


def gather_near(x, beside=None):
    half = x.shape[0] // 2
    blocks = {0: x, 4: moved(x, 4), 12: moved(x, 12), 2: moved(x, 2)}
    result = None
    if beside is not None:
        blocks[4], blocks[12], blocks[2], result = lax.optimization_barrier(
            (blocks[4], blocks[12], blocks[2], beside())
        )
    blocks[8] = jnp.concatenate([moved(blocks[4][:half], 12), moved(blocks[12][half:], 4)], 0)
    blocks[6] = moved(blocks[2], 4)
    blocks[14] = moved(blocks[2], 12)
    blocks[10] = moved(blocks[8], 2)
    return jnp.stack([blocks[k] for k in range(0, SHARDS, 2)]), result


def gather_both(x):
    near, _ = gather_near(x)
    return near, moved(near, 1)


def relative_device(me, place):
    return me ^ (2 * (place % 8) + place // 8)


def placing(me, relative):
    column = lax.broadcasted_iota(jnp.int32, (1, KPAD), 1)
    place, row = column // PROWS, column % PROWS
    owner = relative_device(me, place) if relative else place
    source = jnp.where(row < DROWS, owner * DROWS + row, -1)
    return (lax.broadcasted_iota(jnp.int32, (D, KPAD), 0) == source).astype(bf16)


def matmul(left, right):
    return jnp.dot(left, right, preferred_element_type=f32)


def contract(left, right, ldim, rdim):
    return lax.dot_general(left, right, (((ldim,), (rdim,)), ((), ())), preferred_element_type=f32)


def split_two(values):
    high = lax.reduce_precision(values, 8, 7)
    return high.astype(bf16), (values - high).astype(bf16)


def unplaced(values, place):
    rows = values.shape[0]
    both = contract(jnp.concatenate(split_two(values), 0), place, 1, 1)
    return both[:rows] + both[rows:]


def two_heads(block):
    lane = lax.broadcasted_iota(jnp.int32, block.shape, 1)
    zero = jnp.zeros_like(block)
    return jnp.concatenate(
        [jnp.where(lane < HEAD_DIM, block, zero), jnp.where(lane < HEAD_DIM, zero, block)], 0
    )


def one_pair(both):
    rows = both.shape[0] // 2
    lane = lax.broadcasted_iota(jnp.int32, (rows, 128), 1)
    return jnp.where(lane < HEAD_DIM, both[:rows], both[rows:])


def rows_of(near_ref, far_ref):
    return jnp.concatenate(
        [near_ref[...].reshape(-1, 128), far_ref[...].reshape(-1, 128)], 0
    )


def forward_kernel(q_ref, kn_ref, kf_ref, vn_ref, vf_ref, bias_ref, out_ref, lse_ref):
    bias = bias_ref[0]
    keys, values = rows_of(kn_ref, kf_ref), rows_of(vn_ref, vf_ref)
    scores = contract(two_heads(q_ref[...]), keys, 1, 1) * SCALE
    scores = scores + jnp.concatenate([bias, bias], 0)
    top = jnp.max(scores, axis=1, keepdims=True)
    shifted = jnp.exp(scores - top)
    total = jnp.sum(shifted, axis=1, keepdims=True)
    probs = (shifted / total).astype(bf16)
    out_ref[...] = one_pair(matmul(probs, values)).astype(bf16)
    lse = top + jnp.log(total)
    lse_ref[0, 0] = jnp.transpose(jnp.broadcast_to(lse, (128, 128)))[:8]


def row_kernel(q_ref, do_ref, lse_ref, kn_ref, kf_ref, vn_ref, vf_ref, bias_ref, dq_ref):
    bias = bias_ref[0]
    keys, values = rows_of(kn_ref, kf_ref), rows_of(vn_ref, vf_ref)
    lse = jnp.transpose(jnp.broadcast_to(lse_ref[0, 0][:1], (128, 128)))[:, :1]
    scores = contract(two_heads(q_ref[...]), keys, 1, 1) * SCALE
    scores = scores + jnp.concatenate([bias, bias], 0)
    probs = jnp.exp(scores - lse)
    grad_probs = contract(two_heads(do_ref[...]), values, 1, 1)
    dots = jnp.sum(grad_probs * probs, axis=1, keepdims=True)
    grad_scores = (probs * (grad_probs - dots)).astype(bf16)
    dq_ref[...] = (one_pair(matmul(grad_scores, keys)) * SCALE).astype(bf16)


def normalized(values):
    centred = values - jnp.mean(values, axis=1, keepdims=True)
    scale = lax.rsqrt(jnp.mean(centred * centred, axis=1, keepdims=True) + epsilon)
    return centred * scale, scale


def norm_back(values, gain, grad):
    z, scale = normalized(values)
    weighted = grad * gain
    by_values = scale * (
        weighted
        - jnp.mean(weighted, axis=1, keepdims=True)
        - z * jnp.mean(weighted * z, axis=1, keepdims=True)
    )
    row = lax.broadcasted_iota(jnp.int32, (8, D), 0)
    gain_sum = jnp.sum(grad * z, axis=0, keepdims=True)
    bias_sum = jnp.sum(grad, axis=0, keepdims=True)
    return by_values, jnp.where(row == 0, gain_sum, jnp.where(row == 1, bias_sum, 0.0))


def gelu_parts(v):
    t = jnp.tanh(GELU_C * (v + GELU_A * v * v * v))
    return 0.5 * v * (1.0 + t), t


def gelu_slope(v, t):
    return 0.5 * (1.0 + t) + 0.5 * v * (1.0 - t * t) * (GELU_C * (1.0 + 3.0 * GELU_A * v * v))


def unplaced(values, place):
    rows = values.shape[0]
    high = values.astype(bf16)
    low = (values - high.astype(f32)).astype(bf16)
    both = contract(jnp.concatenate([high, low], 0), place, 1, 1)
    return both[:rows] + both[rows:]


def input_weight(near_ref, far_ref, j):
    rows = slice(j * PROWS, (j + 1) * PROWS)
    return near_ref[:, rows, :].reshape(HALF, LANES), far_ref[:, rows, :].reshape(HALF, LANES)


def qkv_kernel(x_ref, near_ref, far_ref, place_ref, gain_ref, bias_ref, sq_ref, sv_ref, n1_ref, q_ref, kv_ref):
    z, _ = normalized(x_ref[...].astype(f32))
    normed = (z * gain_ref[...] + bias_ref[...]).astype(bf16)
    n1_ref[...] = normed
    placed = matmul(normed, place_ref[...]).astype(bf16)
    rows = placed.shape[0]

    def product(j):
        near, far = input_weight(near_ref, far_ref, j)
        return matmul(placed[:, :HALF], near) + matmul(placed[:, HALF:], far)

    kv_ref[:rows] = product(1).astype(bf16)
    kv_ref[rows:] = (product(2) + sv_ref[...]).astype(bf16)
    q_ref[...] = (product(0) + sq_ref[...]).astype(bf16)


def qkv_back_kernel(dq_ref, dk_ref, dv_ref, near_ref, far_ref, place_ref, x_ref, gain_ref, gh_ref, gin_ref, sums_ref):
    near_sum, far_sum = 0.0, 0.0
    for j, ref in enumerate((dq_ref, dk_ref, dv_ref)):
        near, far = input_weight(near_ref, far_ref, j)
        near_sum = near_sum + contract(ref[...], near, 1, 1)
        far_sum = far_sum + contract(ref[...], far, 1, 1)
    grad = unplaced(jnp.concatenate([near_sum, far_sum], 1), place_ref[...])
    by_input, sums_ref[...] = norm_back(x_ref[...].astype(f32), gain_ref[...], grad)
    gin_ref[...] = (gh_ref[...] + by_input).astype(bf16)


def weight_copies(all_ref, fc_buf, out_buf, proj_buf, sems):
    out_copy = pltpu.make_async_copy(all_ref.at[:, pl.ds(OUT_AT, PROWS), :], out_buf, sems.at[0])
    fc = [
        pltpu.make_async_copy(all_ref.at[:, pl.ds(j * PROWS, PROWS), :], fc_buf.at[j], sems.at[1 + j])
        for j in range(SPLITS)
    ]
    proj = [
        pltpu.make_async_copy(
            all_ref.at[pl.ds(4 * j, 4), pl.ds(PROJ_AT, FROWS), :], proj_buf.at[j], sems.at[1 + SPLITS + j]
        )
        for j in range(SPLITS)
    ]
    return out_copy, fc, proj


def ffn_kernel(
    att_ref, x_ref, place_ref, os_ref, gain_ref, bias_ref, ps_ref, fs_ref, all_ref,
    hidden_ref, n2_ref, pre_ref, out_ref, fc_buf, out_buf, proj_buf, sems,
):
    out_copy, fc, proj = weight_copies(all_ref, fc_buf, out_buf, proj_buf, sems)
    out_copy.start()
    for j in range(SPLITS):
        fc[j].start()
        proj[j].start()
    place = place_ref[...]
    placed = matmul(att_ref[:, :D], place).astype(bf16)
    out_copy.wait()
    hidden = x_ref[...].astype(f32) + matmul(placed, out_buf[...].reshape(KPAD, D)) + os_ref[...]
    hidden_ref[...] = hidden
    z, _ = normalized(hidden)
    normed = (z * gain_ref[...] + bias_ref[...]).astype(bf16)
    n2_ref[...] = normed
    placed = matmul(normed, place).astype(bf16)
    total = hidden + ps_ref[...]
    for j in range(SPLITS):
        fc[j].wait()
        pre = matmul(placed, fc_buf[j].reshape(KPAD, D)) + fs_ref[j : j + 1]
        pre_ref[j] = pre
        activ, _ = gelu_parts(pre)
        proj[j].wait()
        total = total + matmul(activ.astype(bf16), proj_buf[j].reshape(D, D))
    out_ref[...] = total.astype(bf16)


def ffn_back_kernel(
    go_ref, pre_ref, hidden_ref, place_ref, gain_ref, all_ref,
    gh_ref, gb_ref, ga_ref, sums_ref, fc_buf, out_buf, proj_buf, sems,
):
    out_copy, fc, proj = weight_copies(all_ref, fc_buf, out_buf, proj_buf, sems)
    for j in range(SPLITS):
        proj[j].start()
        fc[j].start()
    out_copy.start()
    grad_out = go_ref[...]
    placed = 0.0
    for j in range(SPLITS):
        pre = pre_ref[j]
        _, t = gelu_parts(pre)
        slope = gelu_slope(pre, t)
        proj[j].wait()
        grad_pre = (contract(grad_out, proj_buf[j].reshape(D, D), 1, 1) * slope).astype(bf16)
        fc[j].wait()
        placed = placed + contract(grad_pre, fc_buf[j].reshape(KPAD, D), 1, 1)
    place = place_ref[...]
    by_hidden, sums_ref[...] = norm_back(hidden_ref[...], gain_ref[...], unplaced(placed, place))
    grad_hidden = grad_out.astype(f32) + by_hidden
    gh_ref[...] = grad_hidden
    branch = grad_hidden.astype(bf16)
    gb_ref[...] = branch
    out_copy.wait()
    grad_att = contract(branch, out_buf[...].reshape(KPAD, D), 1, 1).astype(bf16)
    ga_ref[...] = jnp.zeros_like(ga_ref)
    ga_ref[:, :D] = contract(grad_att, place, 1, 1).astype(bf16)


def column_kernel(me_ref, k_ref, v_ref, q_ref, a_ref, lse_ref, don_ref, dof_ref, bias_ref, dk_ref, dv_ref):
    me = me_ref[0]
    owners = [relative_device(me, place) for place in range(SHARDS)]
    queries = jnp.concatenate([q_ref[owner] for owner in owners], 0)
    attended = jnp.concatenate([a_ref[owner] for owner in owners], 0)
    grads = rows_of(don_ref, dof_ref)
    rows = k_ref.shape[0]
    span = q_ref.shape[1]
    bias = bias_ref[0]
    micro = pl.program_id(0)
    term_row = lax.broadcasted_iota(jnp.int32, (16, 128), 0)
    place_of = (
        lax.broadcasted_iota(jnp.int32, (SHARDS, SHARDS * span), 1) // span
        == lax.broadcasted_iota(jnp.int32, (SHARDS, SHARDS * span), 0)
    ).astype(bf16)
    spread_lse = 0.0
    for term in range(3):
        picked = [
            jnp.sum(jnp.where(term_row == 2 * term + micro, lse_ref[owner].astype(f32), 0.0), axis=0, keepdims=True)
            for owner in owners
        ]
        spread_lse = spread_lse + contract(jnp.concatenate(picked, 0).astype(bf16), place_of, 0, 0)
    on_diagonal = (
        lax.broadcasted_iota(jnp.int32, spread_lse.shape, 0) % span
        == lax.broadcasted_iota(jnp.int32, spread_lse.shape, 1) % span
    )
    spread_lse = jnp.where(on_diagonal, spread_lse, 0.0)
    lse_a = jnp.sum(spread_lse[:span], axis=0, keepdims=True)
    lse_b = jnp.sum(spread_lse[span:], axis=0, keepdims=True)
    product = attended.astype(f32) * grads.astype(f32)
    sides = (
        lax.broadcasted_iota(jnp.int32, (8, 128), 1) // HEAD_DIM
        == lax.broadcasted_iota(jnp.int32, (8, 128), 0)
    ).astype(bf16)
    high = product.astype(bf16)
    low = (product - high.astype(f32)).astype(bf16)
    dots = contract(sides, high, 1, 1) + contract(sides, low, 1, 1)

    def spread(row_a, row_b):
        return jnp.concatenate(
            [jnp.broadcast_to(row_a, (rows, row_a.shape[1])), jnp.broadcast_to(row_b, (rows, row_b.shape[1]))], 0
        )

    scores = contract(two_heads(k_ref[...]), queries, 1, 1) * SCALE
    probs = jnp.exp(scores + jnp.concatenate([bias, bias], 0) - spread(lse_a, lse_b))
    grad_probs = contract(two_heads(v_ref[...]), grads, 1, 1)
    grad_scores = (probs * (grad_probs - spread(dots[:1], dots[1:2]))).astype(bf16)
    dk_ref[...] = (one_pair(matmul(grad_scores, queries)) * SCALE).astype(bf16)
    dv_ref[...] = one_pair(matmul(probs.astype(bf16), grads)).astype(bf16)


def hidden_units_kernel(n2_ref, go_ref, fc_ref, fb_ref, proj_ref, gp_ref, gf_out_ref, bsum_ref, osum_ref):
    step = pl.program_id(0)

    @pl.when(step == 0)
    def _():
        for ref in (gp_ref, gf_out_ref, bsum_ref, osum_ref):
            ref[...] = jnp.zeros_like(ref)

    n2 = n2_ref[...].reshape(-1, D)
    go = go_ref[...].reshape(-1, D)
    pre = matmul(n2, fc_ref[...]) + fb_ref[...]
    activ, t = gelu_parts(pre)
    grad_pre = (contract(go, proj_ref[...], 1, 1) * gelu_slope(pre, t)).astype(bf16)
    gp_ref[...] += contract(activ.astype(bf16), go, 0, 0)
    gf_out_ref[...] += contract(n2, grad_pre, 0, 0)
    bsum_ref[...] += jnp.broadcast_to(jnp.sum(grad_pre.astype(f32), axis=0, keepdims=True), bsum_ref.shape)
    osum_ref[...] += jnp.broadcast_to(jnp.sum(go.astype(f32), axis=0, keepdims=True), osum_ref.shape)


def columns_kernel(me_ref, n1_ref, a_ref, cols_ref, grad_ref, sums_ref):
    step = pl.program_id(0)

    @pl.when(step == 0)
    def _():
        grad_ref[...] = jnp.zeros_like(grad_ref)
        sums_ref[...] = jnp.zeros_like(sums_ref)

    att = a_ref[...].reshape(-1, LANES)[:, :D]
    left = jnp.where(me_ref[0] < 12, n1_ref[...].reshape(-1, D), att)
    cols = cols_ref[...].reshape(-1, FROWS)
    grad_ref[...] += contract(left, cols, 0, 0)
    sums_ref[...] += jnp.broadcast_to(jnp.sum(cols.astype(f32), axis=0, keepdims=True), sums_ref.shape)


def params(flops, bytes_accessed, transcendentals=0, vmem=32):
    return dict(
        compiler_params=pltpu.CompilerParams(vmem_limit_bytes=vmem * 1024 * 1024),
        cost_estimate=pl.CostEstimate(
            flops=flops, bytes_accessed=bytes_accessed, transcendentals=transcendentals
        ),
    )


def shape(*dims, dtype=bf16):
    return jax.ShapeDtypeStruct(dims, dtype)


def whole_call(body, out_shape, operands, in_hbm=(), scratch=(), flops=0, bytes_accessed=0, vmem=56):
    vm, hbm = pl.BlockSpec(memory_space=pltpu.VMEM), pl.BlockSpec(memory_space=pl.ANY)
    return pl.pallas_call(
        body,
        in_specs=[hbm if i in in_hbm else vm for i in range(len(operands))],
        out_specs=[vm] * len(out_shape),
        out_shape=out_shape,
        scratch_shapes=list(scratch),
        **params(flops, bytes_accessed, 0, vmem),
    )(*operands)


def pair_call(body, n_matmuls, in_specs, out_specs, out_shape, operands):
    steps = 2 * PAIRS
    return pl.pallas_call(
        body,
        grid=(2, PAIRS),
        in_specs=in_specs,
        out_specs=out_specs,
        out_shape=out_shape,
        **params(
            steps * n_matmuls * 2 * 128 * 128 * 1024 * 4, steps * 2 * 1024 * 128 * 2, steps * 128 * 1024
        ),
    )(*operands)


def own_spec(rows):
    return pl.BlockSpec((rows, 128), lambda m, h: (m, h))


def all_spec(kind, rows):
    return pl.BlockSpec((8, 1, 1, rows, 128), lambda m, h: (0, kind, m, 0, h))


def shards(
    inputs,
    segment_ids,
    sequence_order,
    ln1_gain,
    ln1_bias,
    w_qkv,
    qv_bias,
    w_out,
    out_bias,
    ln2_gain,
    ln2_bias,
    w_fc,
    fc_bias,
    w_proj,
    proj_bias,
    cotangent,
):
    section_index = lax.axis_index("section")
    me = lax.axis_index("fsdp")
    is_first = section_index == 0
    is_last = section_index == 1
    micro, span = inputs.shape[0], inputs.shape[1]
    tokens = micro * span
    seq_len = segment_ids.shape[1]

    def rows_padded(block):
        return jnp.pad(block, ((0, PROWS - block.shape[0]), (0, 0)))

    later = jnp.concatenate(
        [rows_padded(w_fc[0][:, j * D : (j + 1) * D]) for j in range(SPLITS)]
        + [rows_padded(w_out[0]), w_proj[0]],
        0,
    )
    later_all = lax.all_gather(later, "fsdp", axis=0, tiled=False)
    vectors = jnp.concatenate(
        [ln1_gain[0], ln1_bias[0], out_bias[0], ln2_gain[0], ln2_bias[0], proj_bias[0], qv_bias[0], fc_bias[0]]
    )
    vector_rows = jnp.pad(vectors[None], ((0, 15), (0, LANES - vectors.shape[0])))
    first = jnp.concatenate(
        [
            jnp.pad(w_qkv[0][:, j * D : (j + 1) * D], ((0, PROWS - DROWS), (0, LANES - D)))
            for j in range(3)
        ]
        + [vector_rows],
        0,
    )
    first_near, first_far = gather_both(first)
    place_iota = jnp.arange(SHARDS)
    to_absolute = (relative_device(me, place_iota)[None, :] == place_iota[:, None]).astype(bf16)
    vector_rel = jnp.concatenate([first_near[:, 3 * PROWS], first_far[:, 3 * PROWS]], 0)
    vector_all = matmul(to_absolute, vector_rel)

    def vector(start, size):
        return vector_all[:, start : start + size].reshape(1, SHARDS * size)

    gain_one, bias_one, out_shift, gain_two, bias_two, proj_shift = [
        vector(j * DROWS, DROWS) for j in range(6)
    ]
    qv_full = vector(6 * DROWS, 2 * DROWS)
    fc_shift = vector(8 * DROWS, FROWS).reshape(SPLITS, D)
    shift_q = jnp.pad(qv_full[:, :D], ((0, 0), (0, LANES - D)))
    shift_v = jnp.pad(qv_full[:, D:], ((0, 0), (0, LANES - D)))

    place_rel = placing(me, True)
    place_abs = placing(me, False)

    swapped = sequence_order[0, 0] == 1
    ordered_inputs = jnp.where(swapped, inputs[::-1], inputs).reshape(tokens, D)
    ordered_segments = jnp.where(swapped, segment_ids[::-1], segment_ids)
    by_block = ordered_segments.reshape(micro, SHARDS, span)
    rel_devices = relative_device(me, place_iota)
    seg_rel = jnp.take(by_block, rel_devices, axis=1).reshape(micro, 1, seq_len)
    seg_own = lax.dynamic_index_in_dim(by_block, me, 1, keepdims=False)[:, :, None]
    pos_rel = (rel_devices[:, None] * span + jnp.arange(span)[None]).reshape(1, 1, seq_len)
    pos_own = (me * span + jnp.arange(span)).reshape(1, span, 1)
    same = seg_rel == seg_own
    row_bias = jnp.where(same & (pos_rel <= pos_own), 0.0, -1e30).astype(f32)
    column_bias = jnp.where(same & (pos_own <= pos_rel), 0.0, -1e30).astype(f32)
    me_scalar = me.astype(jnp.int32).reshape(1)

    bias_spec = pl.BlockSpec((1, span, seq_len), lambda m, h: (m, 0, 0))
    lse_spec = pl.BlockSpec((1, 1, 8, 128), lambda m, h: (m, h, 0, 0))
    kv_specs = [all_spec(0, span), all_spec(0, span), all_spec(1, span), all_spec(1, span)]
    token_shape = shape(tokens, LANES)
    buffers = [
        pltpu.VMEM((SPLITS, SHARDS, PROWS, D), bf16),
        pltpu.VMEM((SHARDS, PROWS, D), bf16),
        pltpu.VMEM((SPLITS, 4, FROWS, D), bf16),
        pltpu.SemaphoreType.DMA((1 + 2 * SPLITS,)),
    ]
    ffn_cost = dict(flops=4 * 2 * tokens * D * FF, bytes_accessed=2 * SHARDS * 672 * D, scratch=buffers)
    qkv_cost = dict(flops=4 * 2 * tokens * D * 3 * D, bytes_accessed=2 * SHARDS * 256 * LANES)

    def by_kind(block):
        return block.reshape(8, -1, micro, span, LANES)

    def forward_layer(layer_in):
        normed_one, queries, keys_values = whole_call(
            qkv_kernel,
            [shape(tokens, D), token_shape, shape(2 * tokens, LANES)],
            (layer_in, first_near, first_far, place_rel, gain_one, bias_one, shift_q, shift_v),
            **qkv_cost,
        )
        kv_near, kv_far = [by_kind(b) for b in gather_both(keys_values)]
        attended, log_total = pair_call(
            forward_kernel,
            2,
            [own_spec(span)] + kv_specs + [bias_spec],
            [own_spec(span), lse_spec],
            [token_shape, shape(micro, PAIRS, 8, 128, dtype=f32)],
            (queries, kv_near, kv_far, kv_near, kv_far, row_bias),
        )
        hidden, normed_two, pre_act, out_low = whole_call(
            ffn_kernel,
            [shape(tokens, D, dtype=f32), shape(tokens, D), shape(SPLITS, tokens, D, dtype=f32), shape(tokens, D)],
            (attended, layer_in, place_abs, out_shift, gain_two, bias_two, proj_shift, fc_shift, later_all),
            in_hbm=(8,),
            **ffn_cost,
        )
        return out_low, (normed_one, queries, keys_values, kv_near, kv_far, attended, log_total, hidden, normed_two, pre_act)

    sent_on, _ = forward_layer(ordered_inputs)
    received = lax.ppermute(sent_on, "section", [(0, 1)])
    layer_in = jnp.where(is_first, ordered_inputs, received)
    out_low, kept = forward_layer(layer_in)
    normed_one, queries, keys_values, kv_near, kv_far, attended, log_total, hidden, normed_two, pre_act = kept

    lse_own = log_total[:, :, 0]
    part_one = lax.reduce_precision(lse_own, 8, 7)
    part_two = lax.reduce_precision(lse_own - part_one, 8, 7)
    part_three = lse_own - part_one - part_two
    lse_rows = jnp.stack([part_one, part_two, part_three]).astype(bf16).reshape(6, LANES)
    qa_all = lax.all_gather(
        jnp.concatenate([queries, attended, lse_rows, jnp.zeros((10, LANES), bf16)], 0), "fsdp", axis=0
    )
    nn_all = lax.all_gather(jnp.concatenate([normed_one, normed_two], 0), "fsdp", axis=0)

    def backward_layer(grad_out):
        grad_hidden, grad_branch, grad_att, sums_two = whole_call(
            ffn_back_kernel,
            [shape(tokens, D, dtype=f32), shape(tokens, D), token_shape, shape(8, D, dtype=f32)],
            (grad_out, pre_act, hidden, place_abs, gain_two, later_all),
            in_hbm=(5,),
            **ffn_cost,
        )
        def row_part():
            return pair_call(
                row_kernel,
                3,
                [own_spec(span), own_spec(span), lse_spec] + kv_specs + [bias_spec],
                own_spec(span),
                token_shape,
                (queries, grad_att, log_total, kv_near, kv_far, kv_near, kv_far, row_bias),
            )

        near, grad_q = gather_near(grad_att, row_part)
        do_near, do_far = by_kind(near), by_kind(moved(near, 1))
        own_half = lambda half: pl.BlockSpec((span, 128), lambda m, h: (2 * half + m, h))
        grad_k, grad_v = pair_call(
            column_kernel,
            5,
            [
                pl.BlockSpec(memory_space=pltpu.SMEM),
                own_half(0),
                own_half(1),
                pl.BlockSpec((SHARDS, span, 128), lambda m, h: (0, m, h)),
                pl.BlockSpec((SHARDS, span, 128), lambda m, h: (0, 2 + m, h)),
                pl.BlockSpec((SHARDS, 16, 128), lambda m, h: (0, 16, h)),
            ]
            + [all_spec(0, span), all_spec(0, span), bias_spec],
            [own_spec(span), own_spec(span)],
            [token_shape, token_shape],
            (
                me_scalar, keys_values, keys_values, qa_all, qa_all, qa_all, do_near, do_far, column_bias,
            ),
        )
        grad_input, sums_one = whole_call(
            qkv_back_kernel,
            [shape(tokens, D), shape(8, D, dtype=f32)],
            (grad_q, grad_k, grad_v, first_near, first_far, place_rel, layer_in, gain_one, grad_hidden),
            **qkv_cost,
        )
        norm_grads = jnp.concatenate([sums_one[:2], sums_two[:2]], 0)
        return grad_input, grad_branch, (grad_q, grad_k, grad_v), norm_grads

    own_cotangent = cotangent.reshape(tokens, D)
    sent_back, _, _, _ = backward_layer(own_cotangent)
    received_grad = lax.ppermute(sent_back, "section", [(1, 0)])
    grad_out = jnp.where(is_last, own_cotangent, received_grad)
    go_all = lax.all_gather(grad_out, "fsdp", axis=0)
    grad_input, grad_branch, grad_qkv, norm_grads = backward_layer(grad_out)

    fc_own = lax.dynamic_slice(later_all, (0, (me // 4) * PROWS, (me % 4) * FROWS), (SHARDS, PROWS, FROWS))
    fc_own = fc_own[:, :DROWS].reshape(D, FROWS)
    fixed = lambda *dims: pl.BlockSpec(dims, lambda s: (0,) * len(dims))
    chip = lambda kind, width: pl.BlockSpec((2, tokens, width), lambda s: (s, kind, 0))
    grad_proj_w, grad_fc_w, grad_fc_b, out_sums = pl.pallas_call(
        hidden_units_kernel,
        grid=(8,),
        in_specs=[chip(1, D), chip(0, D), fixed(D, FROWS), fixed(1, FROWS), fixed(FROWS, D)],
        out_specs=[fixed(FROWS, D), fixed(D, FROWS), fixed(8, FROWS), fixed(8, D)],
        out_shape=[shape(FROWS, D, dtype=f32), shape(D, FROWS, dtype=f32), shape(8, FROWS, dtype=f32), shape(8, D, dtype=f32)],
        **params(4 * 4 * 2 * SHARDS * tokens * D * FROWS, 3 * 2 * SHARDS * tokens * D),
    )(nn_all, go_all, fc_own, fc_bias.astype(f32), w_proj[0])
    grad_proj_b = lax.dynamic_slice_in_dim(out_sums[0], me * DROWS, DROWS)
    wide = jnp.concatenate([g[:, :D] for g in grad_qkv] + [grad_branch], 1)
    wide = wide.reshape(tokens, SHARDS, FROWS).transpose(1, 0, 2)
    columns = lax.all_to_all(wide, "fsdp", 0, 0)
    grad_columns, column_sums = pl.pallas_call(
        columns_kernel,
        grid=(8,),
        in_specs=[pl.BlockSpec(memory_space=pltpu.SMEM), chip(0, D), chip(1, LANES), chip(0, FROWS)],
        out_specs=[fixed(D, FROWS), fixed(8, FROWS)],
        out_shape=[shape(D, FROWS, dtype=f32), shape(8, FROWS, dtype=f32)],
        **params(4 * 2 * SHARDS * tokens * D * FROWS, 4 * 2 * SHARDS * tokens * D),
    )(me_scalar, nn_all, qa_all, columns)

    rows = jnp.concatenate(
        [
            grad_columns.astype(bf16).reshape(SHARDS, DROWS, FROWS),
            grad_fc_w.astype(bf16).reshape(SHARDS, DROWS, FROWS),
            norm_grads.astype(bf16).reshape(4, SHARDS, DROWS).transpose(1, 2, 0),
        ],
        2,
    )
    width, height = 640, 72
    rows = jnp.pad(rows, ((0, 0), (0, 0), (0, width - rows.shape[2])))
    sums_row = jnp.broadcast_to(
        jnp.pad(column_sums[0].astype(bf16), (0, width - FROWS))[None, None], (SHARDS, 1, width)
    )
    rows = jnp.concatenate([rows, sums_row, jnp.zeros((SHARDS, height - DROWS - 1, width), bf16)], 1)
    got = lax.all_to_all(rows, "fsdp", 0, 0)

    z = lax.axis_index("replica")
    own_vectors = jnp.concatenate([grad_fc_b[0], grad_proj_b, jnp.zeros((2 * width - FROWS - DROWS,), f32)])
    proj_part = jnp.pad(grad_proj_w.reshape(4, DROWS, D), ((0, 0), (0, 0), (0, 2 * width - D)))
    own_part = jnp.broadcast_to(own_vectors[None, None], (4, height - DROWS, 2 * width))
    proj_part = jnp.concatenate([proj_part, own_part], 1).astype(bf16)
    quarter = jnp.concatenate(
        [got.reshape(4, 4, height, width), proj_part[:, None, :, :width], proj_part[:, None, :, width:]], 1
    )
    pick = lambda k: lax.dynamic_index_in_dim(quarter, z ^ k, 0, keepdims=False)
    swap = lambda v, k: lax.ppermute(v, "replica", [(j, j ^ k) for j in range(4)])
    total = pick(0).astype(f32)
    for term in [swap(pick(k), k) for k in (1, 3, 2)]:
        total = total + term.astype(f32)
    total = total.astype(bf16)
    finished = jnp.stack([total] + [swap(total, k) for k in (1, 2, 3)])
    finished = jnp.take(finished, z ^ jnp.arange(4), axis=0).astype(f32)
    proj_total = jnp.concatenate([finished[:, 4], finished[:, 5]], 2)
    finished = finished[:, :4].reshape(SHARDS, height, width)

    def joined(block):
        return block.transpose(1, 0, 2).reshape(block.shape[1], -1)

    grad_w_qkv = joined(finished[:12, :DROWS, :FROWS])
    grad_w_out = joined(finished[12:, :DROWS, :FROWS])
    grad_w_fc = joined(finished[:, :DROWS, FROWS : 2 * FROWS])
    norm_sums = jnp.sum(finished[:, :DROWS, 2 * FROWS : 2 * FROWS + 4], axis=0)
    sums = finished[:, DROWS, :FROWS].reshape(SHARDS * FROWS)
    qv_sums = jnp.concatenate([sums[:D], sums[2 * D : 3 * D]])
    grad_qv_b = lax.dynamic_slice_in_dim(qv_sums, me * 2 * DROWS, 2 * DROWS)
    grad_out_b = lax.dynamic_slice_in_dim(sums, 3 * D + me * DROWS, DROWS)
    totals = (
        norm_sums[:, 0],
        norm_sums[:, 1],
        grad_w_qkv,
        grad_qv_b,
        grad_w_out,
        grad_out_b,
        norm_sums[:, 2],
        norm_sums[:, 3],
        grad_w_fc,
        proj_total[0, DROWS, :FROWS],
        proj_total[:, :DROWS, :D].reshape(FROWS, D),
        proj_total[0, DROWS, FROWS : FROWS + DROWS],
    )
    activations = out_low.reshape(1, micro, span, D)
    input_grads = grad_input.reshape(1, micro, span, D)
    return (activations, input_grads) + tuple((total[None] for total in totals))


def solution(mesh):
    return jax.shard_map(
        shards,
        mesh=mesh,
        in_specs=(
            P("replica", "fsdp", None),
            P("replica", None),
            P("replica", None),
            P("section", "fsdp"),
            P("section", "fsdp"),
            P("section", "fsdp", None),
            P("section", "fsdp"),
            P("section", "fsdp", None),
            P("section", "fsdp"),
            P("section", "fsdp"),
            P("section", "fsdp"),
            P("section", "fsdp", None),
            P("section", "fsdp"),
            P("section", "fsdp", None),
            P("section", "fsdp"),
            P("replica", "fsdp", None),
        ),
        out_specs=(
            P("section", "replica", "fsdp", None),
            P("section", "replica", "fsdp", None),
            P("section", "fsdp"),
            P("section", "fsdp"),
            P("section", "fsdp", None),
            P("section", "fsdp"),
            P("section", "fsdp", None),
            P("section", "fsdp"),
            P("section", "fsdp"),
            P("section", "fsdp"),
            P("section", "fsdp", None),
            P("section", "fsdp"),
            P("section", "fsdp", None),
            P("section", "fsdp"),
        ),
        check_vma=False,
    )
```

time: 836 us -> 723 us (0.86)
  matrix products: 154 us -> 0.13 us
  Pallas kernels: 89.4 us -> 213 us
  local copies, waits for them, and re-layouts: 231 us -> 111 us
  waiting for transfers between devices: 218 us -> 264 us
    pallas_call x6 -> x16, Pallas kernels: 89.4 us -> 213 us  [the longest x6 98.6 us: pair_call(): pl.pallas_call(body, grid=(2, PAIRS), in_specs=in_specs, out_specs=out_sp...]
    dot_general x24 -> x0, matrix products: 91.6 us -> none  [contract(): lax.dot_general(left, right, (((ldim,), (rdim,)), ((), ())), preferred_el...]
    slice x19 -> x13, local copies, waits for them, and re-layouts: 78 us -> 6.13 us  [the longest x1 2.11 us: shards(): fc_own = fc_own[:, :DROWS].reshape(D, FROWS)]
    dot_general x26 -> x1, matrix products: 62.5 us -> 0.13 us  [matmul(): return jnp.dot(left, right, preferred_element_type=f32)]
    unnamed x250 -> x207, local copies, waits for them, and re-layouts: 97.5 us -> 61.8 us
    ppermute x6, waiting for transfers between devices: 14.8 us -> 47.1 us  [shards(): lax.ppermute(v, 'replica', [(j, j ^ k) for j in range(4)])]
    psum x1 -> x0, waiting for transfers between devices: 28.1 us -> none  [shards(): proj_total = lax.psum(proj_rows, 'replica')]
    ppermute x45, waiting for transfers between devices: 142 us -> 166 us  [moved(): return lax.ppermute(value, 'fsdp', xor_pairs(k))]
  transfers between devices with their start and end apart: 60 -> 59, of which waited for: 33 -> 36; matrix products, arithmetic and copies ran while one was open for 27% -> 9% of each run, Pallas kernels for 9% -> 23%
where the time goes in v2:
time: 723 us; the launch traced here: 713 us
  waiting for transfers between devices  264 us (37%)
  Pallas kernels  213 us (29%)
  local copies, waits for them, and re-layouts  111 us (15%)
  starting transfers between devices  84.5 us (12%)
  other arithmetic  24.9 us (3%)
  between operations  15.8 us (2%)
    ppermute x45, waiting for transfers between devices, moved(): return lax.ppermute(value, 'fsdp', xor_pairs(k))  166 us
    pallas_call x6, Pallas kernels, pair_call(): pl.pallas_call(body, grid=(2, PAIRS), in_specs=in_specs, out_specs=out_sp...  98.6 us
    pallas_call x8, Pallas kernels, whole_call(): pl.pallas_call(body, in_specs=[hbm if i in in_hbm else vm for i in range(...  97.4 us
    ppermute x45, starting transfers between devices, moved(): return lax.ppermute(value, 'fsdp', xor_pairs(k))  62.1 us
    unnamed x207, local copies, waits for them, and re-layouts  61.8 us
    ppermute x6, waiting for transfers between devices, shards(): lax.ppermute(v, 'replica', [(j, j ^ k) for j in range(4)])  47.1 us
    all_to_all x1, waiting for transfers between devices, shards(): got = lax.all_to_all(rows, 'fsdp', 0, 0)  22 us
    ppermute x1, waiting for transfers between devices, shards(): received_grad = lax.ppermute(sent_back, 'section', [(1, 0)])  16.3 us
  transfers between devices with their start and end apart: 59, of which 36 were waited for; matrix products, arithmetic and copies ran while one was open for 9% of the time, Pallas kernels for 23%

profile of v2, /device:TPU:0, one launch (start us, length us, event | category | flops | bytes accessed | tf_op | source)
XLA Modules:
  0.0 713.4 jit_solution(4435189883034856967)
XLA Ops:
  51.8 19.6 %collective-permute-done.2 = bf16[256,1152]{1,0:T(8,128)(2,1)S(1)} collective-permute-done((bf16[256,1152]{1,0:T(8,128)(2,1)S(1)}, bf16[256,1152]{1,0:T(8,128)(2,1)S(1)}, u32[]{:S(2)}, u32[]{:S(2)}) %collective-permute-start.2) | collective-permute-done | bytes 589856 | tf_op jit(solution)/shard_map/ppermute | solution.py:38
  104.8 17.7 %collective-permute-done.10 = bf16[256,1152]{1,0:T(8,128)(2,1)S(1)} collective-permute-done((bf16[256,1152]{1,0:T(8,128)(2,1)}, bf16[256,1152]{1,0:T(8,128)(2,1)S(1)}, u32[]{:S(2)}, u32[]{:S(2)}) %collective-permute-start.10) | collective-permute-done | bytes 589856 | tf_op jit(solution)/shard_map/ppermute | solution.py:38
  139.8 10.3 %collective-permute-done.11 = bf16[256,1152]{1,0:T(8,128)(2,1)S(1)} collective-permute-done((bf16[256,1152]{1,0:T(8,128)(2,1)S(1)}, bf16[256,1152]{1,0:T(8,128)(2,1)S(1)}, u32[]{:S(2)}, u32[]{:S(2)}) %collective-permute-start.11) | collective-permute-done | bytes 589856 | tf_op jit(solution)/shard_map/ppermute | solution.py:38
  151.9 13.0 %collective-permute-done.15 = bf16[256,1152]{1,0:T(8,128)(2,1)S(1)} collective-permute-done((bf16[256,1152]{1,0:T(8,128)(2,1)S(1)}, bf16[256,1152]{1,0:T(8,128)(2,1)S(1)}, u32[]{:S(2)}, u32[]{:S(2)}) %collective-permute-start.15) | collective-permute-done | bytes 589856 | tf_op jit(solution)/shard_map/ppermute | solution.py:38
  182.3 16.5 %shard_map.264 = (bf16[128,1152]{1,0:T(8,128)(2,1)S(1)}, f32[2,9,8,128]{3,2,1,0:T(8,128)}) custom-call(bf16[128,1152]{1,0:T(8,128)(2,1)S(1)} %copy-done.24, bf16[8,2,2,64,1152]{4,3,2,1,0:T(8,128)(2,1)S(1)} %constant_dynamic-update-slice_fusion.4.kn_ref.vn_ref, bf16[8,2,2,64,1152]{4,3,2,1,0:T(8,128)(2,1)} %bitcast.33.kf_ref.vf_ref, ...), custom_call_target="tpu_custom_call" | custom-call | flops 4831838208 | bytes 9437184 | tf_op jit(solution)/shard_map/pallas_call | solution.py:395
  201.8 12.1 %shard_map.265 = (f32[128,1088]{1,0:T(8,128)}, bf16[128,1088]{1,0:T(8,128)(2,1)}, f32[4,128,1088]{2,1,0:T(8,128)}, bf16[128,1088]{1,0:T(8,128)(2,1)}) custom-call(bf16[128,1152]{1,0:T(8,128)(2,1)} %copy-done.25, bf16[128,1088]{1,0:T(8,128)(2,1)} %bitcast.264, bf16[1088,1280]{1,0:T(8,128)(2,1)} %fusion.1.place_ref, f32[1,1088]{1,0:T(1,128)} %reshape.552.os_ref, ...), custom_call_target="tpu_custom_call" | custom-call | flops 4848615424 | bytes 23396352 | tf_op jit(solution)/shard_map/pallas_call | solution.py:383
  237.3 9.9 %collective-permute-done.20 = bf16[256,1152]{1,0:T(8,128)(2,1)S(1)} collective-permute-done((bf16[256,1152]{1,0:T(8,128)(2,1)}, bf16[256,1152]{1,0:T(8,128)(2,1)S(1)}, u32[]{:S(2)}, u32[]{:S(2)}) %collective-permute-start.20) | collective-permute-done | bytes 589856 | tf_op jit(solution)/shard_map/ppermute | solution.py:38
  279.0 13.2 %shard_map.267 = (bf16[128,1152]{1,0:T(8,128)(2,1)S(1)}, f32[2,9,8,128]{3,2,1,0:T(8,128)S(1)}) custom-call(bf16[128,1152]{1,0:T(8,128)(2,1)S(1)} %copy-done.16, bf16[8,2,2,64,1152]{4,3,2,1,0:T(8,128)(2,1)S(1)} %constant_dynamic-update-slice_fusion.15.kn_ref.vn_ref, bf16[8,2,2,64,1152]{4,3,2,1,0:T(8,128)(2,1)S(1)} %bitcast.221, ...), custom_call_target="tpu_custom_call" | custom-call | flops 4831838208 | bytes 9437184 | tf_op jit(solution)/shard_map/pallas_call | solution.py:395
  293.5 12.3 %shard_map.268 = (f32[128,1088]{1,0:T(8,128)}, bf16[128,1088]{1,0:T(8,128)(2,1)}, f32[4,128,1088]{2,1,0:T(8,128)}, bf16[128,1088]{1,0:T(8,128)(2,1)}) custom-call(bf16[128,1152]{1,0:T(8,128)(2,1)} %copy-done.17, bf16[128,1088]{1,0:T(8,128)(2,1)} %broadcast_select_fusion.1.x_ref, bf16[1088,1280]{1,0:T(8,128)(2,1)} %fusion.1.place_ref, ...), custom_call_target="tpu_custom_call" | custom-call | flops 4848615424 | bytes 23396352 | tf_op jit(solution)/shard_map/pallas_call | solution.py:383
  308.0 18.7 %shard_map.269 = (f32[128,1088]{1,0:T(8,128)}, bf16[128,1088]{1,0:T(8,128)(2,1)}, bf16[128,1152]{1,0:T(8,128)(2,1)}, f32[8,1088]{1,0:T(8,128)}) custom-call(bf16[128,1088]{1,0:T(8,128)(2,1)} %bitcast.288, f32[4,128,1088]{2,1,0:T(8,128)} %get-tuple-element.62.pre_ref, f32[128,1088]{1,0:T(8,128)} %get-tuple-element.63.hidden_ref, ...), custom_call_target="tpu_custom_call" | custom-call | flops 4848615424 | bytes 23396352 | tf_op jit(solution)/shard_map/pallas_call | solution.py:383
  334.2 12.6 %shard_map.270.dq_ref = bf16[128,1152]{1,0:T(8,128)(2,1)S(1)} custom-call(bf16[128,1152]{1,0:T(8,128)(2,1)S(1)} %copy-done.16, bf16[128,1152]{1,0:T(8,128)(2,1)S(1)} %copy-done.15, f32[2,9,8,128]{3,2,1,0:T(8,128)S(1)} %get-tuple-element.65.lse_ref, bf16[8,2,2,64,1152]{4,3,2,1,0:T(8,128)(2,1)S(1)} %bitcast.218, bf16[8,2,2,64,1152]{4,3,2,1,0:T(8,128)(2,1)S(1)} %bitcast.223, ...), custom_call_target="tpu_custom_call" | custom-call | flops 7247757312 | bytes 9437184 | tf_op jit(solution)/shard_map/pallas_call | solution.py:395
  351.9 12.1 %collective-permute-done.32 = bf16[64,1152]{1,0:T(8,128)(2,1)S(1)} collective-permute-done((bf16[64,1152]{1,0:T(8,128)(2,1)S(1)}, bf16[64,1152]{1,0:T(8,128)(2,1)S(1)}, u32[]{:S(2)}, u32[]{:S(2)}) %collective-permute-start.32) | collective-permute-done | bytes 147488 | tf_op jit(solution)/shard_map/ppermute | solution.py:38
  386.5 21.9 %shard_map.271 = (bf16[128,1152]{1,0:T(8,128)(2,1)S(1)}, bf16[128,1152]{1,0:T(8,128)(2,1)S(1)}) custom-call(s32[1]{0:T(128)} %bitcast.60.me_ref, bf16[256,1152]{1,0:T(8,128)(2,1)S(1)} %copy-done.9, bf16[256,1152]{1,0:T(8,128)(2,1)S(1)} %copy-done.9, bf16[16,272,1152]{2,1,0:T(8,128)(2,1)S(1)} %bitcast.227, bf16[16,272,1152]{2,1,0:T(8,128)(2,1)S(1)} %bitcast.228, ...), custom_call_target="tpu_custom_call" | custom-call | flops 12079595520 | bytes 9437184 | tf_op jit(solution)/shard_map/pallas_call | solution.py:395
  409.8 9.5 %shard_map.272 = (bf16[128,1088]{1,0:T(8,128)(2,1)}, f32[8,1088]{1,0:T(8,128)}) custom-call(bf16[128,1152]{1,0:T(8,128)(2,1)} %copy-done.21, bf16[128,1152]{1,0:T(8,128)(2,1)} %copy-done.22, bf16[128,1152]{1,0:T(8,128)(2,1)} %copy-done.23, bf16[8,256,1152]{2,1,0:T(8,128)(2,1)} %bitcast_dynamic-update-slice_fusion.16.near_ref, ...), custom_call_target="tpu_custom_call" | custom-call | flops 3636461568 | bytes 9437184 | tf_op jit(solution)/shard_map/pallas_call | solution.py:383
  421.0 16.3 %collective-permute-done.37 = bf16[128,1088]{1,0:T(8,128)(2,1)S(1)} collective-permute-done((bf16[128,1088]{1,0:T(8,128)(2,1)}, bf16[128,1088]{1,0:T(8,128)(2,1)S(1)}, u32[]{:S(2)}, u32[]{:S(2)}) %collective-permute-start.37) | collective-permute-done | bytes 278560 | tf_op jit(solution)/shard_map/ppermute | solution.py:603
  438.1 18.8 %shard_map.273 = (f32[128,1088]{1,0:T(8,128)}, bf16[128,1088]{1,0:T(8,128)(2,1)}, bf16[128,1152]{1,0:T(8,128)(2,1)}, f32[8,1088]{1,0:T(8,128)}) custom-call(bf16[128,1088]{1,0:T(8,128)(2,1)} %broadcast_select_fusion.go_ref, f32[4,128,1088]{2,1,0:T(8,128)} %get-tuple-element.62.pre_ref, f32[128,1088]{1,0:T(8,128)} %get-tuple-element.63.hidden_ref, ...), custom_call_target="tpu_custom_call" | custom-call | flops 4848615424 | bytes 23396352 | tf_op jit(solution)/shard_map/pallas_call | solution.py:383
  465.1 12.6 %shard_map.274.dq_ref = bf16[128,1152]{1,0:T(8,128)(2,1)S(1)} custom-call(bf16[128,1152]{1,0:T(8,128)(2,1)S(1)} %copy-done.16, bf16[128,1152]{1,0:T(8,128)(2,1)S(1)} %copy-done.13, f32[2,9,8,128]{3,2,1,0:T(8,128)S(1)} %get-tuple-element.65.lse_ref, bf16[8,2,2,64,1152]{4,3,2,1,0:T(8,128)(2,1)S(1)} %bitcast.220, bf16[8,2,2,64,1152]{4,3,2,1,0:T(8,128)(2,1)S(1)} %bitcast.225, ...), custom_call_target="tpu_custom_call" | custom-call | flops 7247757312 | bytes 9437184 | tf_op jit(solution)/shard_map/pallas_call | solution.py:395
  506.8 21.9 %shard_map.275 = (bf16[128,1152]{1,0:T(8,128)(2,1)S(1)}, bf16[128,1152]{1,0:T(8,128)(2,1)S(1)}) custom-call(s32[1]{0:T(128)} %bitcast.60.me_ref, bf16[256,1152]{1,0:T(8,128)(2,1)S(1)} %copy-done.9, bf16[256,1152]{1,0:T(8,128)(2,1)S(1)} %copy-done.9, bf16[16,272,1152]{2,1,0:T(8,128)(2,1)S(1)} %bitcast.230, bf16[16,272,1152]{2,1,0:T(8,128)(2,1)S(1)} %bitcast.231, ...), custom_call_target="tpu_custom_call" | custom-call | flops 12079595520 | bytes 9437184 | tf_op jit(solution)/shard_map/pallas_call | solution.py:395
  541.1 9.5 %shard_map.276 = (bf16[128,1088]{1,0:T(8,128)(2,1)}, f32[8,1088]{1,0:T(8,128)}) custom-call(bf16[128,1152]{1,0:T(8,128)(2,1)} %copy-done.10, bf16[128,1152]{1,0:T(8,128)(2,1)} %copy-done.11, bf16[128,1152]{1,0:T(8,128)(2,1)} %copy-done.12, bf16[8,256,1152]{2,1,0:T(8,128)(2,1)} %bitcast_dynamic-update-slice_fusion.16.near_ref, ...), custom_call_target="tpu_custom_call" | custom-call | flops 3636461568 | bytes 9437184 | tf_op jit(solution)/shard_map/pallas_call | solution.py:383
  578.0 11.8 %shard_map.278 = (f32[272,1088]{1,0:T(8,128)S(1)}, f32[1088,272]{1,0:T(8,128)S(1)}, f32[8,272]{1,0:T(8,128)S(1)}, f32[8,1088]{1,0:T(8,128)S(1)}) custom-call(bf16[16,256,1088]{2,1,0:T(8,128)(2,1)S(1)} %bitcast.235, bf16[16,128,1088]{2,1,0:T(8,128)(2,1)S(1)} %bitcast.243, bf16[1088,272]{1,0:T(8,128)(2,1)S(1)} %reshape.565.fc_ref, ...), custom_call_target="tpu_custom_call" | custom-call | flops 19394461696 | bytes 13369344 | tf_op jit(solution)/shard_map/pallas_call | solution.py:612
  600.7 22.0 %all-to-all-done.1 = bf16[16,72,640]{2,1,0:T(8,128)(2,1)} async-done(((bf16[16,72,640]{2,1,0:T(8,128)(2,1)}), bf16[16,72,640]{2,1,0:T(8,128)(2,1)}, u32[]{:S(2)}, u32[]{:S(2)}) %all-to-all-start.1) | async-done | bytes 1474592 | tf_op jit(solution)/shard_map/all_to_all | solution.py:647
  629.8 11.5 %collective-permute-done.47 = bf16[6,72,640]{2,1,0:T(8,128)(2,1)S(1)} collective-permute-done((bf16[6,72,640]{2,1,0:T(8,128)(2,1)}, bf16[6,72,640]{2,1,0:T(8,128)(2,1)S(1)}, u32[]{:S(2)}, u32[]{:S(2)}) %collective-permute-start.47) | collective-permute-done | bytes 552992 | tf_op jit(solution)/shard_map/ppermute | solution.py:658
  641.3 13.1 %collective-permute-done.48 = bf16[6,72,640]{2,1,0:T(8,128)(2,1)} collective-permute-done((bf16[6,72,640]{2,1,0:T(8,128)(2,1)}, bf16[6,72,640]{2,1,0:T(8,128)(2,1)}, u32[]{:S(2)}, u32[]{:S(2)}) %collective-permute-start.48) | collective-permute-done | bytes 552992 | tf_op jit(solution)/shard_map/ppermute | solution.py:658
  660.8 10.7 %collective-permute-done.50 = bf16[6,72,640]{2,1,0:T(8,128)(2,1)S(1)} collective-permute-done((bf16[6,72,640]{2,1,0:T(8,128)(2,1)S(1)}, bf16[6,72,640]{2,1,0:T(8,128)(2,1)S(1)}, u32[]{:S(2)}, u32[]{:S(2)}) %collective-permute-start.50) | collective-permute-done | bytes 552992 | tf_op jit(solution)/shard_map/ppermute | solution.py:658
  (473 shorter events, 349.9 us)
Async XLA Ops:
  7.2 194.6 %all-gather.9.cloned.1.call-start = ((), (), s32[]{:S(2)}) async-start(), calls=%async_computation.2 | async-start | bytes 26320896 | tf_op jit(solution)/shard_map/all_gather | solution.py:449
  10.2 369.2 %all-gather.11.cloned.1.call-start = ((), (), s32[]{:S(2)}) async-start(), calls=%async_computation.3 | async-start | bytes 10653696 | tf_op jit(solution)/shard_map/all_gather | solution.py:548
  15.6 22.9 %collective-permute-start = (bf16[256,1152]{1,0:T(8,128)(2,1)S(1)}, bf16[256,1152]{1,0:T(8,128)(2,1)S(1)}, u32[]{:S(2)}, u32[]{:S(2)}) collective-permute-start(bf16[256,1152]{1,0:T(8,128)(2,1)S(1)} %fusion.19), channel_id=1, source_target_pairs={{0,8},{4,12},{8,0},{12,4},{16,24},{20,28},{24,16},{28,20},{32,40},... | collective-permute-start | bytes 1769480 | tf_op jit(solution)/shard_map/ppermute | solution.py:38
  38.6 32.9 %collective-permute-start.2 = (bf16[256,1152]{1,0:T(8,128)(2,1)S(1)}, bf16[256,1152]{1,0:T(8,128)(2,1)S(1)}, u32[]{:S(2)}, u32[]{:S(2)}) collective-permute-start(bf16[256,1152]{1,0:T(8,128)(2,1)S(1)} %collective-permute-done), channel_id=1, source_target_pairs={{0,16},{4,20},{8,24},{12,28},{16,0},{20,4},{24,8},{28,12},{32,48},... | collective-permute-start | bytes 1769480 | tf_op jit(solution)/shard_map/ppermute | solution.py:38
  38.6 36.4 %collective-permute-start.7 = (bf16[256,1152]{1,0:T(8,128)(2,1)S(1)}, bf16[256,1152]{1,0:T(8,128)(2,1)S(1)}, u32[]{:S(2)}, u32[]{:S(2)}) collective-permute-start(bf16[256,1152]{1,0:T(8,128)(2,1)S(1)} %collective-permute-done), channel_id=1, source_target_pairs={{0,48},{4,52},{8,56},{12,60},{16,32},{20,36},{24,40},{28,44},{32,1... | collective-permute-start | bytes 1769480 | tf_op jit(solution)/shard_map/ppermute | solution.py:38
  49.0 24.2 %collective-permute-start.6 = (bf16[256,1152]{1,0:T(8,128)(2,1)S(1)}, bf16[256,1152]{1,0:T(8,128)(2,1)S(1)}, u32[]{:S(2)}, u32[]{:S(2)}) collective-permute-start(bf16[256,1152]{1,0:T(8,128)(2,1)S(1)} %constant_dynamic-update-slice_fusion), channel_id=1, source_target_pairs={{0,8},{4,12},{8,0},{12,4},{16,24},{20,28},{24,16},{28,20},{32,40},... | collective-permute-start | bytes 1769480 | tf_op jit(solution)/shard_map/ppermute | solution.py:38
  96.5 30.3 %collective-permute-start.9 = (bf16[256,1152]{1,0:T(8,128)(2,1)}, bf16[256,1152]{1,0:T(8,128)(2,1)S(1)}, u32[]{:S(2)}, u32[]{:S(2)}) collective-permute-start(bf16[256,1152]{1,0:T(8,128)(2,1)} %get-tuple-element.55), channel_id=1, source_target_pairs={{0,8},{4,12},{8,0},{12,4},{16,24},{20,28},{24,16},{28,20},{32,40},... | collective-permute-start | bytes 1769480 | tf_op jit(solution)/shard_map/ppermute | solution.py:38
  99.5 23.1 %collective-permute-start.10 = (bf16[256,1152]{1,0:T(8,128)(2,1)}, bf16[256,1152]{1,0:T(8,128)(2,1)S(1)}, u32[]{:S(2)}, u32[]{:S(2)}) collective-permute-start(bf16[256,1152]{1,0:T(8,128)(2,1)} %get-tuple-element.55), channel_id=1, source_target_pairs={{0,16},{4,20},{8,24},{12,28},{16,0},{20,4},{24,8},{28,12},{32,48},... | collective-permute-start | bytes 1769480 | tf_op jit(solution)/shard_map/ppermute | solution.py:38
  100.5 24.2 %collective-permute-start.13 = (bf16[256,1152]{1,0:T(8,128)(2,1)}, bf16[256,1152]{1,0:T(8,128)(2,1)S(1)}, u32[]{:S(2)}, u32[]{:S(2)}) collective-permute-start(bf16[256,1152]{1,0:T(8,128)(2,1)} %get-tuple-element.55), channel_id=1, source_target_pairs={{0,48},{4,52},{8,56},{12,60},{16,32},{20,36},{24,40},{28,44},{32,1... | collective-permute-start | bytes 1769480 | tf_op jit(solution)/shard_map/ppermute | solution.py:38
  126.7 23.4 %collective-permute-start.11 = (bf16[256,1152]{1,0:T(8,128)(2,1)S(1)}, bf16[256,1152]{1,0:T(8,128)(2,1)S(1)}, u32[]{:S(2)}, u32[]{:S(2)}) collective-permute-start(bf16[256,1152]{1,0:T(8,128)(2,1)S(1)} %collective-permute-done.9), channel_id=1, source_target_pairs={{0,16},{4,20},{8,24},{12,28},{16,0},{20,4},{24,8},{28,12},{32,48},... | collective-permute-start | bytes 1769480 | tf_op jit(solution)/shard_map/ppermute | solution.py:38
  127.7 39.0 %collective-permute-start.16 = (bf16[256,1152]{1,0:T(8,128)(2,1)S(1)}, bf16[256,1152]{1,0:T(8,128)(2,1)S(1)}, u32[]{:S(2)}, u32[]{:S(2)}) collective-permute-start(bf16[256,1152]{1,0:T(8,128)(2,1)S(1)} %collective-permute-done.9), channel_id=1, source_target_pairs={{0,48},{4,52},{8,56},{12,60},{16,32},{20,36},{24,40},{28,44},{32,1... | collective-permute-start | bytes 1769480 | tf_op jit(solution)/shard_map/ppermute | solution.py:38
  134.8 30.1 %collective-permute-start.15 = (bf16[256,1152]{1,0:T(8,128)(2,1)S(1)}, bf16[256,1152]{1,0:T(8,128)(2,1)S(1)}, u32[]{:S(2)}, u32[]{:S(2)}) collective-permute-start(bf16[256,1152]{1,0:T(8,128)(2,1)S(1)} %constant_dynamic-update-slice_fusion.2), channel_id=1, source_target_pairs={{0,8},{4,12},{8,0},{12,4},{16,24},{20,28},{24,16},{28,20},{32,40},... | collective-permute-start | bytes 1769480 | tf_op jit(solution)/shard_map/ppermute | solution.py:38
  250.7 20.3 %collective-permute-start.26 = (bf16[256,1152]{1,0:T(8,128)(2,1)S(1)}, bf16[256,1152]{1,0:T(8,128)(2,1)S(1)}, u32[]{:S(2)}, u32[]{:S(2)}) collective-permute-start(bf16[256,1152]{1,0:T(8,128)(2,1)S(1)} %collective-permute-done.19), channel_id=1, source_target_pairs={{0,48},{4,52},{8,56},{12,60},{16,32},{20,36},{24,40},{28,44},{32,1... | collective-permute-start | bytes 1769480 | tf_op jit(solution)/shard_map/ppermute | solution.py:38
  293.4 264.8 %all-gather.13.cloned.1.call-start = ((), (), s32[]{:S(2)}) async-start(), calls=%async_computation.4 | async-start | bytes 10027008 | tf_op jit(solution)/shard_map/all_gather | solution.py:551
  307.8 264.2 %all-gather.15.cloned.1.call-start = ((), (), s32[]{:S(2)}) async-start(), calls=%async_computation.5 | async-start | bytes 5013504 | tf_op jit(solution)/shard_map/all_gather | solution.py:605
  348.4 24.1 %collective-permute-start.35 = (bf16[128,1152]{1,0:T(8,128)(2,1)S(1)}, bf16[128,1152]{1,0:T(8,128)(2,1)S(1)}, u32[]{:S(2)}, u32[]{:S(2)}) collective-permute-start(bf16[128,1152]{1,0:T(8,128)(2,1)S(1)} %collective-permute-done.30), channel_id=1, source_target_pairs={{0,48},{4,52},{8,56},{12,60},{16,32},{20,36},{24,40},{28,44},{32,1... | collective-permute-start | bytes 884744 | tf_op jit(solution)/shard_map/ppermute | solution.py:38
  456.9 20.8 %collective-permute-start.38 = (bf16[128,1152]{1,0:T(8,128)(2,1)}, bf16[128,1152]{1,0:T(8,128)(2,1)}, u32[]{:S(2)}, u32[]{:S(2)}) collective-permute-start(bf16[128,1152]{1,0:T(8,128)(2,1)} %get-tuple-element.74.do_ref), channel_id=1, source_target_pairs={{0,16},{4,20},{8,24},{12,28},{16,0},{20,4},{24,8},{28,12},{32,48},... | collective-permute-start | bytes 884744 | tf_op jit(solution)/shard_map/ppermute | solution.py:38
  478.9 22.2 %collective-permute-start.45 = (bf16[128,1152]{1,0:T(8,128)(2,1)}, bf16[128,1152]{1,0:T(8,128)(2,1)S(1)}, u32[]{:S(2)}, u32[]{:S(2)}) collective-permute-start(bf16[128,1152]{1,0:T(8,128)(2,1)} %collective-permute-done.40), channel_id=1, source_target_pairs={{0,48},{4,52},{8,56},{12,60},{16,32},{20,36},{24,40},{28,44},{32,1... | collective-permute-start | bytes 884744 | tf_op jit(solution)/shard_map/ppermute | solution.py:38
  533.3 23.1 %all-to-all-start = ((bf16[16,128,272]{1,2,0:T(8,128)(2,1)}), bf16[16,128,272]{1,2,0:T(8,128)(2,1)}, u32[]{:S(2)}, u32[]{:S(2)}) async-start(bf16[16,128,272]{1,2,0:T(8,128)(2,1)} %bitcast.100), calls=%async_computation | async-start | bytes 2228224 | tf_op jit(solution)/shard_map/all_to_all | solution.py:623
  595.5 27.3 %all-to-all-start.1 = ((bf16[16,72,640]{2,1,0:T(8,128)(2,1)}), bf16[16,72,640]{2,1,0:T(8,128)(2,1)}, u32[]{:S(2)}, u32[]{:S(2)}) async-start(bf16[16,72,640]{2,1,0:T(8,128)(2,1)} %maximum_maximum_fusion), calls=%async_computation.1 | async-start | bytes 2949120 | tf_op jit(solution)/shard_map/all_to_all | solution.py:647
  627.3 27.1 %collective-permute-start.48 = (bf16[6,72,640]{2,1,0:T(8,128)(2,1)}, bf16[6,72,640]{2,1,0:T(8,128)(2,1)}, u32[]{:S(2)}, u32[]{:S(2)}) collective-permute-start(bf16[6,72,640]{2,1,0:T(8,128)(2,1)} %get-tuple-element.160), channel_id=1, source_target_pairs={{0,3},{1,2},{2,1},{3,0},{4,7},{5,6},{6,5},{7,4},{8,11},{9,10},{10,... | collective-permute-start | bytes 1658888 | tf_op jit(solution)/shard_map/ppermute | solution.py:658
  629.0 25.4 %collective-permute-start.49 = (bf16[6,72,640]{2,1,0:T(8,128)(2,1)S(1)}, bf16[6,72,640]{2,1,0:T(8,128)(2,1)}, u32[]{:S(2)}, u32[]{:S(2)}) collective-permute-start(bf16[6,72,640]{2,1,0:T(8,128)(2,1)S(1)} %get-tuple-element.159), channel_id=1, source_target_pairs={{0,2},{1,3},{2,0},{3,1},{4,6},{5,7},{6,4},{7,5},{8,10},{9,11},{10,... | collective-permute-start | bytes 1658888 | tf_op jit(solution)/shard_map/ppermute | solution.py:658
  656.0 24.6 %collective-permute-start.51 = (bf16[6,72,640]{2,1,0:T(8,128)(2,1)S(1)}, bf16[6,72,640]{2,1,0:T(8,128)(2,1)S(1)}, u32[]{:S(2)}, u32[]{:S(2)}) collective-permute-start(bf16[6,72,640]{2,1,0:T(8,128)(2,1)S(1)} %fusion.16), channel_id=1, source_target_pairs={{0,2},{1,3},{2,0},{3,1},{4,6},{5,7},{6,4},{7,5},{8,10},{9,11},{10,... | collective-permute-start | bytes 1658888 | tf_op jit(solution)/shard_map/ppermute | solution.py:658
  659.2 24.0 %collective-permute-start.52 = (bf16[6,72,640]{2,1,0:T(8,128)(2,1)S(1)}, bf16[6,72,640]{2,1,0:T(8,128)(2,1)S(1)}, u32[]{:S(2)}, u32[]{:S(2)}) collective-permute-start(bf16[6,72,640]{2,1,0:T(8,128)(2,1)S(1)} %fusion.16), channel_id=1, source_target_pairs={{0,3},{1,2},{2,1},{3,0},{4,7},{5,6},{6,5},{7,4},{8,11},{9,10},{10,... | collective-permute-start | bytes 1658888 | tf_op jit(solution)/shard_map/ppermute | solution.py:658
  (101 other events, 1248.1 us)
Sparse Core Ops, SparseCore 0:
  10.5 191.2 all-gather.8
  293.5 85.7 all-gather.10
  381.8 77.6 all-gather.12
  477.8 57.6 all-gather.14

commit v3 on v2

--- a/solution.py
+++ b/solution.py
@@ -390,7 +390,7 @@
     )(*operands)
 
 
-def pair_call(body, n_matmuls, in_specs, out_specs, out_shape, operands):
+def pair_call(body, n_matmuls, in_specs, out_specs, out_shape, operands, vmem=32):
     steps = 2 * PAIRS
     return pl.pallas_call(
         body,
@@ -399,7 +399,7 @@
         out_specs=out_specs,
         out_shape=out_shape,
         **params(
-            steps * n_matmuls * 2 * 128 * 128 * 1024 * 4, steps * 2 * 1024 * 128 * 2, steps * 128 * 1024
+            steps * n_matmuls * 2 * 128 * 128 * 1024 * 4, steps * 2 * 1024 * 128 * 2, steps * 128 * 1024, vmem
         ),
     )(*operands)
 
@@ -588,6 +588,7 @@
             (
                 me_scalar, keys_values, keys_values, qa_all, qa_all, qa_all, do_near, do_far, column_bias,
             ),
+            vmem=60,
         )
         grad_input, sums_one = whole_call(
             qkv_back_kernel,
@@ -615,63 +616,71 @@
         in_specs=[chip(1, D), chip(0, D), fixed(D, FROWS), fixed(1, FROWS), fixed(FROWS, D)],
         out_specs=[fixed(FROWS, D), fixed(D, FROWS), fixed(8, FROWS), fixed(8, D)],
         out_shape=[shape(FROWS, D, dtype=f32), shape(D, FROWS, dtype=f32), shape(8, FROWS, dtype=f32), shape(8, D, dtype=f32)],
-        **params(4 * 4 * 2 * SHARDS * tokens * D * FROWS, 3 * 2 * SHARDS * tokens * D),
+        **params(4 * 4 * 2 * SHARDS * tokens * D * FROWS, 3 * 2 * SHARDS * tokens * D, vmem=60),
     )(nn_all, go_all, fc_own, fc_bias.astype(f32), w_proj[0])
     grad_proj_b = lax.dynamic_slice_in_dim(out_sums[0], me * DROWS, DROWS)
     wide = jnp.concatenate([g[:, :D] for g in grad_qkv] + [grad_branch], 1)
     wide = wide.reshape(tokens, SHARDS, FROWS).transpose(1, 0, 2)
     columns = lax.all_to_all(wide, "fsdp", 0, 0)
+    columns, grad_fc_w, grad_proj_w = lax.optimization_barrier((columns, grad_fc_w, grad_proj_w))
     grad_columns, column_sums = pl.pallas_call(
         columns_kernel,
         grid=(8,),
         in_specs=[pl.BlockSpec(memory_space=pltpu.SMEM), chip(0, D), chip(1, LANES), chip(0, FROWS)],
         out_specs=[fixed(D, FROWS), fixed(8, FROWS)],
         out_shape=[shape(D, FROWS, dtype=f32), shape(8, FROWS, dtype=f32)],
-        **params(4 * 2 * SHARDS * tokens * D * FROWS, 4 * 2 * SHARDS * tokens * D),
+        **params(4 * 2 * SHARDS * tokens * D * FROWS, 4 * 2 * SHARDS * tokens * D, vmem=60),
     )(me_scalar, nn_all, qa_all, columns)
+
+    width, height = 384, 72
+    z = lax.axis_index("replica")
+
+    def to_owners(columns_of_rows):
+        pads = ((0, 0), (0, height - columns_of_rows.shape[1]), (0, width - columns_of_rows.shape[2]))
+        return lax.all_to_all(jnp.pad(columns_of_rows, pads), "fsdp", 0, 0)
+
+    def over_replicas(quarter):
+        pick = lambda k: lax.dynamic_index_in_dim(quarter, z ^ k, 0, keepdims=False)
+        swap = lambda v, k: lax.ppermute(v, "replica", [(j, j ^ k) for j in range(4)])
+        total = pick(0).astype(f32)
+        for term in [swap(pick(k), k) for k in (1, 3, 2)]:
+            total = total + term.astype(f32)
+        total = total.astype(bf16)
+        finished = jnp.stack([total] + [swap(total, k) for k in (1, 2, 3)])
+        return jnp.take(finished, z ^ jnp.arange(4), axis=0)
+
+    got_fc = to_owners(grad_fc_w.astype(bf16).reshape(SHARDS, DROWS, FROWS)).reshape(4, 4, height, width)
+    own_vectors = jnp.concatenate([grad_fc_b[0], grad_proj_b, jnp.zeros((3 * width - FROWS - DROWS,), f32)])
+    proj_part = jnp.pad(grad_proj_w.reshape(4, DROWS, D), ((0, 0), (0, 0), (0, 3 * width - D)))
+    own_part = jnp.broadcast_to(own_vectors[None, None], (4, height - DROWS, 3 * width))
+    proj_part = jnp.concatenate([proj_part, own_part], 1).astype(bf16)
+    proj_parts = [proj_part[:, None, :, j * width : (j + 1) * width] for j in range(3)]
+    ffn_total = over_replicas(jnp.concatenate([got_fc] + proj_parts, 1))
 
     rows = jnp.concatenate(
         [
             grad_columns.astype(bf16).reshape(SHARDS, DROWS, FROWS),
-            grad_fc_w.astype(bf16).reshape(SHARDS, DROWS, FROWS),
             norm_grads.astype(bf16).reshape(4, SHARDS, DROWS).transpose(1, 2, 0),
         ],
         2,
     )
-    width, height = 640, 72
     rows = jnp.pad(rows, ((0, 0), (0, 0), (0, width - rows.shape[2])))
     sums_row = jnp.broadcast_to(
         jnp.pad(column_sums[0].astype(bf16), (0, width - FROWS))[None, None], (SHARDS, 1, width)
     )
-    rows = jnp.concatenate([rows, sums_row, jnp.zeros((SHARDS, height - DROWS - 1, width), bf16)], 1)
-    got = lax.all_to_all(rows, "fsdp", 0, 0)
-
-    z = lax.axis_index("replica")
-    own_vectors = jnp.concatenate([grad_fc_b[0], grad_proj_b, jnp.zeros((2 * width - FROWS - DROWS,), f32)])
-    proj_part = jnp.pad(grad_proj_w.reshape(4, DROWS, D), ((0, 0), (0, 0), (0, 2 * width - D)))
-    own_part = jnp.broadcast_to(own_vectors[None, None], (4, height - DROWS, 2 * width))
-    proj_part = jnp.concatenate([proj_part, own_part], 1).astype(bf16)
-    quarter = jnp.concatenate(
-        [got.reshape(4, 4, height, width), proj_part[:, None, :, :width], proj_part[:, None, :, width:]], 1
-    )
-    pick = lambda k: lax.dynamic_index_in_dim(quarter, z ^ k, 0, keepdims=False)
-    swap = lambda v, k: lax.ppermute(v, "replica", [(j, j ^ k) for j in range(4)])
-    total = pick(0).astype(f32)
-    for term in [swap(pick(k), k) for k in (1, 3, 2)]:
-        total = total + term.astype(f32)
-    total = total.astype(bf16)
-    finished = jnp.stack([total] + [swap(total, k) for k in (1, 2, 3)])
-    finished = jnp.take(finished, z ^ jnp.arange(4), axis=0).astype(f32)
-    proj_total = jnp.concatenate([finished[:, 4], finished[:, 5]], 2)
-    finished = finished[:, :4].reshape(SHARDS, height, width)
+    got = to_owners(jnp.concatenate([rows, sums_row], 1))
+    got, ffn_total = lax.optimization_barrier((got, ffn_total))
+    finished = over_replicas(got.reshape(4, 4, height, width)).reshape(SHARDS, height, width).astype(f32)
+    proj_total = jnp.concatenate([ffn_total[:, 4], ffn_total[:, 5], ffn_total[:, 6]], 2).astype(f32)
+    fc_total = ffn_total[:, :4].reshape(SHARDS, height, width).astype(f32)
 
     def joined(block):
         return block.transpose(1, 0, 2).reshape(block.shape[1], -1)
 
     grad_w_qkv = joined(finished[:12, :DROWS, :FROWS])
     grad_w_out = joined(finished[12:, :DROWS, :FROWS])
-    grad_w_fc = joined(finished[:, :DROWS, FROWS : 2 * FROWS])
-    norm_sums = jnp.sum(finished[:, :DROWS, 2 * FROWS : 2 * FROWS + 4], axis=0)
+    grad_w_fc = joined(fc_total[:, :DROWS, :FROWS])
+    norm_sums = jnp.sum(finished[:, :DROWS, FROWS : FROWS + 4], axis=0)
     sums = finished[:, DROWS, :FROWS].reshape(SHARDS * FROWS)
     qv_sums = jnp.concatenate([sums[:D], sums[2 * D : 3 * D]])
     grad_qv_b = lax.dynamic_slice_in_dim(qv_sums, me * 2 * DROWS, 2 * DROWS)

time: 723 us -> 682 us (0.943)
  waiting for transfers between devices: 264 us -> 231 us
  local copies, waits for them, and re-layouts: 111 us -> 82.9 us
  starting transfers between devices: 84.5 us -> 95.9 us
    unnamed x207 -> x169, local copies, waits for them, and re-layouts: 61.8 us -> 38.2 us
    ppermute x6 -> x12, waiting for transfers between devices: 47.1 us -> 27.4 us  [over_replicas(): lax.ppermute(v, 'replica', [(j, j ^ k) for j in range(4)])]
    ppermute x6 -> x12, starting transfers between devices: 8.9 us -> 17.1 us  [over_replicas(): lax.ppermute(v, 'replica', [(j, j ^ k) for j in range(4)])]
    all_to_all x1 -> x2, waiting for transfers between devices: 22 us -> 13.8 us  [to_owners(): return lax.all_to_all(jnp.pad(columns_of_rows, pads), 'fsdp', 0, 0)]
  transfers between devices with their start and end apart: 59 -> 66, of which waited for: 36 -> 40; matrix products, arithmetic and copies ran while one was open for 9% -> 11% of each run, Pallas kernels for 23% -> 28%
where the time goes in v3:
time: 682 us; the launch traced here: 671 us
  waiting for transfers between devices  231 us (34%)
  Pallas kernels  219 us (32%)
  starting transfers between devices  95.9 us (14%)
  local copies, waits for them, and re-layouts  82.9 us (12%)
  other arithmetic  26.8 us (4%)
  between operations  15.7 us (2%)
    ppermute x45, waiting for transfers between devices, moved(): return lax.ppermute(value, 'fsdp', xor_pairs(k))  165 us
    pallas_call x6, Pallas kernels, pair_call(): pl.pallas_call(body, grid=(2, PAIRS), in_specs=in_specs, out_specs=out_sp...  98.1 us
    pallas_call x8, Pallas kernels, whole_call(): pl.pallas_call(body, in_specs=[hbm if i in in_hbm else vm for i in range(...  97 us
    ppermute x45, starting transfers between devices, moved(): return lax.ppermute(value, 'fsdp', xor_pairs(k))  58.4 us
    unnamed x169, local copies, waits for them, and re-layouts  38.2 us
    ppermute x12, waiting for transfers between devices, over_replicas(): lax.ppermute(v, 'replica', [(j, j ^ k) for j in range(4)])  27.4 us
    ppermute x12, starting transfers between devices, over_replicas(): lax.ppermute(v, 'replica', [(j, j ^ k) for j in range(4)])  17.1 us
    pallas_call x1, Pallas kernels, shards(): pl.pallas_call(hidden_units_kernel, grid=(8,), in_specs=[chip(1, D), chip...  14.6 us
  transfers between devices with their start and end apart: 66, of which 40 were waited for; matrix products, arithmetic and copies ran while one was open for 11% of the time, Pallas kernels for 28%

profile of v3, /device:TPU:0, one launch (start us, length us, event | category | flops | bytes accessed | tf_op | source)
XLA Modules:
  0.0 671.1 jit_solution(5052312145068002076)
XLA Ops:
  50.6 20.8 %collective-permute-done.2 = bf16[256,1152]{1,0:T(8,128)(2,1)S(1)} collective-permute-done((bf16[256,1152]{1,0:T(8,128)(2,1)S(1)}, bf16[256,1152]{1,0:T(8,128)(2,1)S(1)}, u32[]{:S(2)}, u32[]{:S(2)}) %collective-permute-start.2) | collective-permute-done | bytes 589856 | tf_op jit(solution)/shard_map/ppermute | solution.py:38
  88.1 8.4 %shard_map.263 = (bf16[128,1088]{1,0:T(8,128)(2,1)}, bf16[128,1152]{1,0:T(8,128)(2,1)}, bf16[256,1152]{1,0:T(8,128)(2,1)}) custom-call(bf16[128,1088]{1,0:T(8,128)(2,1)} %bitcast.278, bf16[8,256,1152]{2,1,0:T(8,128)(2,1)} %bitcast_dynamic-update-slice_fusion.16.near_ref, bf16[8,256,1152]{2,1,0:T(8,128)(2,1)} %collective-permute-done.8.far_ref, ...), custom_call_target="tpu_custom_call" | custom-call | flops 3636461568 | bytes 9437184 | tf_op jit(solution)/shard_map/pallas_call | solution.py:383
  104.7 17.3 %collective-permute-done.10 = bf16[256,1152]{1,0:T(8,128)(2,1)S(1)} collective-permute-done((bf16[256,1152]{1,0:T(8,128)(2,1)}, bf16[256,1152]{1,0:T(8,128)(2,1)S(1)}, u32[]{:S(2)}, u32[]{:S(2)}) %collective-permute-start.10) | collective-permute-done | bytes 589856 | tf_op jit(solution)/shard_map/ppermute | solution.py:38
  139.2 10.4 %collective-permute-done.11 = bf16[256,1152]{1,0:T(8,128)(2,1)S(1)} collective-permute-done((bf16[256,1152]{1,0:T(8,128)(2,1)S(1)}, bf16[256,1152]{1,0:T(8,128)(2,1)S(1)}, u32[]{:S(2)}, u32[]{:S(2)}) %collective-permute-start.11) | collective-permute-done | bytes 589856 | tf_op jit(solution)/shard_map/ppermute | solution.py:38
  151.3 13.0 %collective-permute-done.15 = bf16[256,1152]{1,0:T(8,128)(2,1)S(1)} collective-permute-done((bf16[256,1152]{1,0:T(8,128)(2,1)S(1)}, bf16[256,1152]{1,0:T(8,128)(2,1)S(1)}, u32[]{:S(2)}, u32[]{:S(2)}) %collective-permute-start.15) | collective-permute-done | bytes 589856 | tf_op jit(solution)/shard_map/ppermute | solution.py:38
  179.5 16.5 %shard_map.264 = (bf16[128,1152]{1,0:T(8,128)(2,1)S(1)}, f32[2,9,8,128]{3,2,1,0:T(8,128)}) custom-call(bf16[128,1152]{1,0:T(8,128)(2,1)S(1)} %copy-done.12, bf16[8,2,2,64,1152]{4,3,2,1,0:T(8,128)(2,1)S(1)} %constant_dynamic-update-slice_fusion.4.kn_ref.vn_ref, bf16[8,2,2,64,1152]{4,3,2,1,0:T(8,128)(2,1)} %bitcast.33.kf_ref.vf_ref, ...), custom_call_target="tpu_custom_call" | custom-call | flops 4831838208 | bytes 9437184 | tf_op jit(solution)/shard_map/pallas_call | solution.py:395
  201.3 12.1 %shard_map.265 = (f32[128,1088]{1,0:T(8,128)}, bf16[128,1088]{1,0:T(8,128)(2,1)}, f32[4,128,1088]{2,1,0:T(8,128)}, bf16[128,1088]{1,0:T(8,128)(2,1)}) custom-call(bf16[128,1152]{1,0:T(8,128)(2,1)} %copy-done.13, bf16[128,1088]{1,0:T(8,128)(2,1)} %bitcast.279, bf16[1088,1280]{1,0:T(8,128)(2,1)} %fusion.1.place_ref, f32[1,1088]{1,0:T(1,128)} %reshape.560.os_ref, ...), custom_call_target="tpu_custom_call" | custom-call | flops 4848615424 | bytes 23396352 | tf_op jit(solution)/shard_map/pallas_call | solution.py:383
  236.7 9.9 %collective-permute-done.20 = bf16[256,1152]{1,0:T(8,128)(2,1)S(1)} collective-permute-done((bf16[256,1152]{1,0:T(8,128)(2,1)}, bf16[256,1152]{1,0:T(8,128)(2,1)S(1)}, u32[]{:S(2)}, u32[]{:S(2)}) %collective-permute-start.20) | collective-permute-done | bytes 589856 | tf_op jit(solution)/shard_map/ppermute | solution.py:38
  278.5 13.2 %shard_map.267 = (bf16[128,1152]{1,0:T(8,128)(2,1)S(1)}, f32[2,9,8,128]{3,2,1,0:T(8,128)S(1)}) custom-call(bf16[128,1152]{1,0:T(8,128)(2,1)S(1)} %copy-done.9, bf16[8,2,2,64,1152]{4,3,2,1,0:T(8,128)(2,1)S(1)} %constant_dynamic-update-slice_fusion.15.kn_ref.vn_ref, bf16[8,2,2,64,1152]{4,3,2,1,0:T(8,128)(2,1)S(1)} %bitcast.245, ...), custom_call_target="tpu_custom_call" | custom-call | flops 4831838208 | bytes 9437184 | tf_op jit(solution)/shard_map/pallas_call | solution.py:395
  293.0 12.3 %shard_map.268 = (f32[128,1088]{1,0:T(8,128)}, bf16[128,1088]{1,0:T(8,128)(2,1)}, f32[4,128,1088]{2,1,0:T(8,128)}, bf16[128,1088]{1,0:T(8,128)(2,1)}) custom-call(bf16[128,1152]{1,0:T(8,128)(2,1)} %copy-done.10, bf16[128,1088]{1,0:T(8,128)(2,1)} %broadcast_select_fusion.2.x_ref, bf16[1088,1280]{1,0:T(8,128)(2,1)} %fusion.1.place_ref, ...), custom_call_target="tpu_custom_call" | custom-call | flops 4848615424 | bytes 23396352 | tf_op jit(solution)/shard_map/pallas_call | solution.py:383
  307.5 18.7 %shard_map.269 = (f32[128,1088]{1,0:T(8,128)}, bf16[128,1088]{1,0:T(8,128)(2,1)}, bf16[128,1152]{1,0:T(8,128)(2,1)}, f32[8,1088]{1,0:T(8,128)}) custom-call(bf16[128,1088]{1,0:T(8,128)(2,1)} %bitcast.308, f32[4,128,1088]{2,1,0:T(8,128)} %get-tuple-element.67.pre_ref, f32[128,1088]{1,0:T(8,128)} %get-tuple-element.68.hidden_ref, ...), custom_call_target="tpu_custom_call" | custom-call | flops 4848615424 | bytes 23396352 | tf_op jit(solution)/shard_map/pallas_call | solution.py:383
  333.7 12.6 %shard_map.270.dq_ref = bf16[128,1152]{1,0:T(8,128)(2,1)S(1)} custom-call(bf16[128,1152]{1,0:T(8,128)(2,1)S(1)} %copy-done.9, bf16[128,1152]{1,0:T(8,128)(2,1)S(1)} %copy-done.8, f32[2,9,8,128]{3,2,1,0:T(8,128)S(1)} %get-tuple-element.70.lse_ref, bf16[8,2,2,64,1152]{4,3,2,1,0:T(8,128)(2,1)S(1)} %bitcast.244, bf16[8,2,2,64,1152]{4,3,2,1,0:T(8,128)(2,1)S(1)} %bitcast.247, ...), custom_call_target="tpu_custom_call" | custom-call | flops 7247757312 | bytes 9437184 | tf_op jit(solution)/shard_map/pallas_call | solution.py:395
  351.4 12.1 %collective-permute-done.32 = bf16[64,1152]{1,0:T(8,128)(2,1)S(1)} collective-permute-done((bf16[64,1152]{1,0:T(8,128)(2,1)S(1)}, bf16[64,1152]{1,0:T(8,128)(2,1)S(1)}, u32[]{:S(2)}, u32[]{:S(2)}) %collective-permute-start.32) | collective-permute-done | bytes 147488 | tf_op jit(solution)/shard_map/ppermute | solution.py:38
  378.7 21.6 %shard_map.271 = (bf16[128,1152]{1,0:T(8,128)(2,1)}, bf16[128,1152]{1,0:T(8,128)(2,1)}) custom-call(s32[1]{0:T(128)} %bitcast.60.me_ref, bf16[256,1152]{1,0:T(8,128)(2,1)} %get-tuple-element.64.k_ref.v_ref, bf16[256,1152]{1,0:T(8,128)(2,1)} %get-tuple-element.64.k_ref.v_ref, bf16[16,272,1152]{2,1,0:T(8,128)(2,1)} %bitcast.259, ...), custom_call_target="tpu_custom_call" | custom-call | flops 12079595520 | bytes 9437184 | tf_op jit(solution)/shard_map/pallas_call | solution.py:395
  400.3 9.6 %shard_map.272 = (bf16[128,1088]{1,0:T(8,128)(2,1)}, f32[8,1088]{1,0:T(8,128)}) custom-call(bf16[128,1152]{1,0:T(8,128)(2,1)} %copy-done.11, bf16[128,1152]{1,0:T(8,128)(2,1)} %get-tuple-element.75.dk_ref, bf16[128,1152]{1,0:T(8,128)(2,1)} %get-tuple-element.76.dv_ref, bf16[8,256,1152]{2,1,0:T(8,128)(2,1)} %bitcast_dynamic-update-slice_fusion.16.near_ref, ...), custom_call_target="tpu_custom_call" | custom-call | flops 3636461568 | bytes 9437184 | tf_op jit(solution)/shard_map/pallas_call | solution.py:383
  411.5 11.5 %collective-permute-done.37 = bf16[128,1088]{1,0:T(8,128)(2,1)S(1)} collective-permute-done((bf16[128,1088]{1,0:T(8,128)(2,1)}, bf16[128,1088]{1,0:T(8,128)(2,1)S(1)}, u32[]{:S(2)}, u32[]{:S(2)}) %collective-permute-start.37) | collective-permute-done | bytes 278560 | tf_op jit(solution)/shard_map/ppermute | solution.py:604
  423.8 18.3 %shard_map.273 = (f32[128,1088]{1,0:T(8,128)}, bf16[128,1088]{1,0:T(8,128)(2,1)}, bf16[128,1152]{1,0:T(8,128)(2,1)}, f32[8,1088]{1,0:T(8,128)}) custom-call(bf16[128,1088]{1,0:T(8,128)(2,1)} %broadcast_select_fusion.1.go_ref, f32[4,128,1088]{2,1,0:T(8,128)} %get-tuple-element.67.pre_ref, f32[128,1088]{1,0:T(8,128)} %get-tuple-element.68.hidden_ref, ...), custom_call_target="tpu_custom_call" | custom-call | flops 4848615424 | bytes 23396352 | tf_op jit(solution)/shard_map/pallas_call | solution.py:383
  451.2 12.6 %shard_map.274.dq_ref = bf16[128,1152]{1,0:T(8,128)(2,1)S(1)} custom-call(bf16[128,1152]{1,0:T(8,128)(2,1)S(1)} %copy-done.9, bf16[128,1152]{1,0:T(8,128)(2,1)S(1)} %copy-done.6, f32[2,9,8,128]{3,2,1,0:T(8,128)S(1)} %get-tuple-element.70.lse_ref, bf16[8,2,2,64,1152]{4,3,2,1,0:T(8,128)(2,1)S(1)} %copy-done.1, bf16[8,2,2,64,1152]{4,3,2,1,0:T(8,128)(2,1)S(1)} %bitcast.249, ...), custom_call_target="tpu_custom_call" | custom-call | flops 7247757312 | bytes 9437184 | tf_op jit(solution)/shard_map/pallas_call | solution.py:395
  495.4 21.7 %shard_map.275 = (bf16[128,1152]{1,0:T(8,128)(2,1)}, bf16[128,1152]{1,0:T(8,128)(2,1)}) custom-call(s32[1]{0:T(128)} %bitcast.60.me_ref, bf16[256,1152]{1,0:T(8,128)(2,1)} %get-tuple-element.64.k_ref.v_ref, bf16[256,1152]{1,0:T(8,128)(2,1)} %get-tuple-element.64.k_ref.v_ref, bf16[16,272,1152]{2,1,0:T(8,128)(2,1)} %bitcast.262, ...), custom_call_target="tpu_custom_call" | custom-call | flops 12079595520 | bytes 9437184 | tf_op jit(solution)/shard_map/pallas_call | solution.py:395
  525.3 9.5 %shard_map.276 = (bf16[128,1088]{1,0:T(8,128)(2,1)}, f32[8,1088]{1,0:T(8,128)}) custom-call(bf16[128,1152]{1,0:T(8,128)(2,1)} %copy-done.5, bf16[128,1152]{1,0:T(8,128)(2,1)} %get-tuple-element.84.dk_ref, bf16[128,1152]{1,0:T(8,128)(2,1)} %get-tuple-element.85.dv_ref, bf16[8,256,1152]{2,1,0:T(8,128)(2,1)} %bitcast_dynamic-update-slice_fusion.16.near_ref, ...), custom_call_target="tpu_custom_call" | custom-call | flops 3636461568 | bytes 9437184 | tf_op jit(solution)/shard_map/pallas_call | solution.py:383
  535.7 14.6 %shard_map.277 = (f32[272,1088]{1,0:T(8,128)}, f32[1088,272]{1,0:T(8,128)}, f32[8,272]{1,0:T(8,128)}, f32[8,1088]{1,0:T(8,128)}) custom-call(bf16[16,256,1088]{2,1,0:T(8,128)(2,1)} %bitcast.266, bf16[16,128,1088]{2,1,0:T(8,128)(2,1)} %bitcast.337, bf16[1088,272]{1,0:T(8,128)(2,1)} %reshape.572.fc_ref, f32[1,272]{1,0:T(1,128)} %get-tuple-element.197.fb_ref, ...), custom_call_target="tpu_custom_call" | custom-call | flops 19394461696 | bytes 13369344 | tf_op jit(solution)/shard_map/pallas_call | solution.py:613
  566.2 10.4 %all-to-all-done.2 = bf16[16,72,384]{2,1,0:T(8,128)(2,1)S(1)} async-done(((bf16[16,72,384]{2,1,0:T(8,128)(2,1)}), bf16[16,72,384]{2,1,0:T(8,128)(2,1)S(1)}, u32[]{:S(2)}, u32[]{:S(2)}) %all-to-all-start.2) | async-done | bytes 884768 | tf_op jit(solution)/shard_map/all_to_all | solution.py:640
  582.2 9.3 %shard_map.278 = (f32[1088,272]{1,0:T(8,128)}, f32[8,272]{1,0:T(8,128)}) custom-call(s32[1]{0:T(128)} %bitcast.60.me_ref, bf16[16,256,1088]{2,1,0:T(8,128)(2,1)} %bitcast.267, bf16[16,272,1152]{2,1,0:T(8,128)(2,1)} %bitcast.265, bf16[16,128,272]{2,1,0:T(8,128)(2,1)} %copy.93.cols_ref), custom_call_target="tpu_custom_call" | custom-call | flops 4848615424 | bytes 17825792 | tf_op jit(solution)/shard_map/pallas_call | solution.py:626
  609.9 10.5 %collective-permute-done.52 = bf16[7,72,384]{2,1,0:T(8,128)(2,1)S(1)} collective-permute-done((bf16[7,72,384]{2,1,0:T(8,128)(2,1)S(1)}, bf16[7,72,384]{2,1,0:T(8,128)(2,1)S(1)}, u32[]{:S(2)}, u32[]{:S(2)}) %collective-permute-start.52) | collective-permute-done | bytes 387104 | tf_op jit(solution)/shard_map/ppermute | solution.py:644
  (453 shorter events, 328.8 us)
Async XLA Ops:
  7.2 194.1 %all-gather.9.cloned.1.call-start = ((), (), s32[]{:S(2)}) async-start(), calls=%async_computation.3 | async-start | bytes 26320896 | tf_op jit(solution)/shard_map/all_gather | solution.py:449
  10.2 368.5 %all-gather.11.cloned.1.call-start = ((), (), s32[]{:S(2)}) async-start(), calls=%async_computation.4 | async-start | bytes 10653696 | tf_op jit(solution)/shard_map/all_gather | solution.py:548
  15.1 22.4 %collective-permute-start = (bf16[256,1152]{1,0:T(8,128)(2,1)S(1)}, bf16[256,1152]{1,0:T(8,128)(2,1)S(1)}, u32[]{:S(2)}, u32[]{:S(2)}) collective-permute-start(bf16[256,1152]{1,0:T(8,128)(2,1)S(1)} %fusion.21), channel_id=1, source_target_pairs={{0,8},{4,12},{8,0},{12,4},{16,24},{20,28},{24,16},{28,20},{32,40},... | collective-permute-start | bytes 1769480 | tf_op jit(solution)/shard_map/ppermute | solution.py:38
  37.5 33.9 %collective-permute-start.2 = (bf16[256,1152]{1,0:T(8,128)(2,1)S(1)}, bf16[256,1152]{1,0:T(8,128)(2,1)S(1)}, u32[]{:S(2)}, u32[]{:S(2)}) collective-permute-start(bf16[256,1152]{1,0:T(8,128)(2,1)S(1)} %collective-permute-done), channel_id=1, source_target_pairs={{0,16},{4,20},{8,24},{12,28},{16,0},{20,4},{24,8},{28,12},{32,48},... | collective-permute-start | bytes 1769480 | tf_op jit(solution)/shard_map/ppermute | solution.py:38
  37.5 37.4 %collective-permute-start.7 = (bf16[256,1152]{1,0:T(8,128)(2,1)S(1)}, bf16[256,1152]{1,0:T(8,128)(2,1)S(1)}, u32[]{:S(2)}, u32[]{:S(2)}) collective-permute-start(bf16[256,1152]{1,0:T(8,128)(2,1)S(1)} %collective-permute-done), channel_id=1, source_target_pairs={{0,48},{4,52},{8,56},{12,60},{16,32},{20,36},{24,40},{28,44},{32,1... | collective-permute-start | bytes 1769480 | tf_op jit(solution)/shard_map/ppermute | solution.py:38
  47.8 25.4 %collective-permute-start.6 = (bf16[256,1152]{1,0:T(8,128)(2,1)S(1)}, bf16[256,1152]{1,0:T(8,128)(2,1)S(1)}, u32[]{:S(2)}, u32[]{:S(2)}) collective-permute-start(bf16[256,1152]{1,0:T(8,128)(2,1)S(1)} %constant_dynamic-update-slice_fusion), channel_id=1, source_target_pairs={{0,8},{4,12},{8,0},{12,4},{16,24},{20,28},{24,16},{28,20},{32,40},... | collective-permute-start | bytes 1769480 | tf_op jit(solution)/shard_map/ppermute | solution.py:38
  96.5 30.3 %collective-permute-start.9 = (bf16[256,1152]{1,0:T(8,128)(2,1)}, bf16[256,1152]{1,0:T(8,128)(2,1)S(1)}, u32[]{:S(2)}, u32[]{:S(2)}) collective-permute-start(bf16[256,1152]{1,0:T(8,128)(2,1)} %get-tuple-element.60), channel_id=1, source_target_pairs={{0,8},{4,12},{8,0},{12,4},{16,24},{20,28},{24,16},{28,20},{32,40},... | collective-permute-start | bytes 1769480 | tf_op jit(solution)/shard_map/ppermute | solution.py:38
  99.4 22.6 %collective-permute-start.10 = (bf16[256,1152]{1,0:T(8,128)(2,1)}, bf16[256,1152]{1,0:T(8,128)(2,1)S(1)}, u32[]{:S(2)}, u32[]{:S(2)}) collective-permute-start(bf16[256,1152]{1,0:T(8,128)(2,1)} %get-tuple-element.60), channel_id=1, source_target_pairs={{0,16},{4,20},{8,24},{12,28},{16,0},{20,4},{24,8},{28,12},{32,48},... | collective-permute-start | bytes 1769480 | tf_op jit(solution)/shard_map/ppermute | solution.py:38
  99.9 24.3 %collective-permute-start.13 = (bf16[256,1152]{1,0:T(8,128)(2,1)}, bf16[256,1152]{1,0:T(8,128)(2,1)S(1)}, u32[]{:S(2)}, u32[]{:S(2)}) collective-permute-start(bf16[256,1152]{1,0:T(8,128)(2,1)} %get-tuple-element.60), channel_id=1, source_target_pairs={{0,48},{4,52},{8,56},{12,60},{16,32},{20,36},{24,40},{28,44},{32,1... | collective-permute-start | bytes 1769480 | tf_op jit(solution)/shard_map/ppermute | solution.py:38
  126.8 22.8 %collective-permute-start.11 = (bf16[256,1152]{1,0:T(8,128)(2,1)S(1)}, bf16[256,1152]{1,0:T(8,128)(2,1)S(1)}, u32[]{:S(2)}, u32[]{:S(2)}) collective-permute-start(bf16[256,1152]{1,0:T(8,128)(2,1)S(1)} %collective-permute-done.9), channel_id=1, source_target_pairs={{0,16},{4,20},{8,24},{12,28},{16,0},{20,4},{24,8},{28,12},{32,48},... | collective-permute-start | bytes 1769480 | tf_op jit(solution)/shard_map/ppermute | solution.py:38
  127.1 39.1 %collective-permute-start.16 = (bf16[256,1152]{1,0:T(8,128)(2,1)S(1)}, bf16[256,1152]{1,0:T(8,128)(2,1)S(1)}, u32[]{:S(2)}, u32[]{:S(2)}) collective-permute-start(bf16[256,1152]{1,0:T(8,128)(2,1)S(1)} %collective-permute-done.9), channel_id=1, source_target_pairs={{0,48},{4,52},{8,56},{12,60},{16,32},{20,36},{24,40},{28,44},{32,1... | collective-permute-start | bytes 1769480 | tf_op jit(solution)/shard_map/ppermute | solution.py:38
  134.3 30.1 %collective-permute-start.15 = (bf16[256,1152]{1,0:T(8,128)(2,1)S(1)}, bf16[256,1152]{1,0:T(8,128)(2,1)S(1)}, u32[]{:S(2)}, u32[]{:S(2)}) collective-permute-start(bf16[256,1152]{1,0:T(8,128)(2,1)S(1)} %constant_dynamic-update-slice_fusion.2), channel_id=1, source_target_pairs={{0,8},{4,12},{8,0},{12,4},{16,24},{20,28},{24,16},{28,20},{32,40},... | collective-permute-start | bytes 1769480 | tf_op jit(solution)/shard_map/ppermute | solution.py:38
  250.1 20.3 %collective-permute-start.26 = (bf16[256,1152]{1,0:T(8,128)(2,1)S(1)}, bf16[256,1152]{1,0:T(8,128)(2,1)S(1)}, u32[]{:S(2)}, u32[]{:S(2)}) collective-permute-start(bf16[256,1152]{1,0:T(8,128)(2,1)S(1)} %collective-permute-done.19), channel_id=1, source_target_pairs={{0,48},{4,52},{8,56},{12,60},{16,32},{20,36},{24,40},{28,44},{32,1... | collective-permute-start | bytes 1769480 | tf_op jit(solution)/shard_map/ppermute | solution.py:38
  292.9 242.8 %all-gather.13.cloned.1.call-start = ((), (), s32[]{:S(2)}) async-start(), calls=%async_computation.5 | async-start | bytes 10027008 | tf_op jit(solution)/shard_map/all_gather | solution.py:551
  307.3 228.5 %all-gather.15.cloned.1.call-start = ((), (), s32[]{:S(2)}) async-start(), calls=%async_computation.6 | async-start | bytes 5013504 | tf_op jit(solution)/shard_map/all_gather | solution.py:606
  347.9 24.1 %collective-permute-start.35 = (bf16[128,1152]{1,0:T(8,128)(2,1)S(1)}, bf16[128,1152]{1,0:T(8,128)(2,1)S(1)}, u32[]{:S(2)}, u32[]{:S(2)}) collective-permute-start(bf16[128,1152]{1,0:T(8,128)(2,1)S(1)} %collective-permute-done.30), channel_id=1, source_target_pairs={{0,48},{4,52},{8,56},{12,60},{16,32},{20,36},{24,40},{28,44},{32,1... | collective-permute-start | bytes 884744 | tf_op jit(solution)/shard_map/ppermute | solution.py:38
  442.2 22.4 %collective-permute-start.38 = (bf16[128,1152]{1,0:T(8,128)(2,1)}, bf16[128,1152]{1,0:T(8,128)(2,1)S(1)}, u32[]{:S(2)}, u32[]{:S(2)}) collective-permute-start(bf16[128,1152]{1,0:T(8,128)(2,1)} %get-tuple-element.79.do_ref), channel_id=1, source_target_pairs={{0,16},{4,20},{8,24},{12,28},{16,0},{20,4},{24,8},{28,12},{32,48},... | collective-permute-start | bytes 884744 | tf_op jit(solution)/shard_map/ppermute | solution.py:38
  442.8 21.8 %collective-permute-start.39 = (bf16[128,1152]{1,0:T(8,128)(2,1)}, bf16[128,1152]{1,0:T(8,128)(2,1)S(1)}, u32[]{:S(2)}, u32[]{:S(2)}) collective-permute-start(bf16[128,1152]{1,0:T(8,128)(2,1)} %get-tuple-element.79.do_ref), channel_id=1, source_target_pairs={{0,48},{4,52},{8,56},{12,60},{16,32},{20,36},{24,40},{28,44},{32,1... | collective-permute-start | bytes 884744 | tf_op jit(solution)/shard_map/ppermute | solution.py:38
  442.9 21.7 %collective-permute-start.40 = (bf16[128,1152]{1,0:T(8,128)(2,1)}, bf16[128,1152]{1,0:T(8,128)(2,1)S(1)}, u32[]{:S(2)}, u32[]{:S(2)}) collective-permute-start(bf16[128,1152]{1,0:T(8,128)(2,1)} %get-tuple-element.79.do_ref), channel_id=1, source_target_pairs={{0,8},{4,12},{8,0},{12,4},{16,24},{20,28},{24,16},{28,20},{32,40},... | collective-permute-start | bytes 884744 | tf_op jit(solution)/shard_map/ppermute | solution.py:38
  465.5 23.1 %collective-permute-start.45 = (bf16[128,1152]{1,0:T(8,128)(2,1)S(1)}, bf16[128,1152]{1,0:T(8,128)(2,1)S(1)}, u32[]{:S(2)}, u32[]{:S(2)}) collective-permute-start(bf16[128,1152]{1,0:T(8,128)(2,1)S(1)} %collective-permute-done.40), channel_id=1, source_target_pairs={{0,48},{4,52},{8,56},{12,60},{16,32},{20,36},{24,40},{28,44},{32,1... | collective-permute-start | bytes 884744 | tf_op jit(solution)/shard_map/ppermute | solution.py:38
  521.0 29.3 %all-to-all-start = ((bf16[16,128,272]{1,2,0:T(8,128)(2,1)}), bf16[16,128,272]{1,2,0:T(8,128)(2,1)S(1)}, u32[]{:S(2)}, u32[]{:S(2)}) async-start(bf16[16,128,272]{1,2,0:T(8,128)(2,1)} %bitcast.100), calls=%async_computation | async-start | bytes 2228224 | tf_op jit(solution)/shard_map/all_to_all | solution.py:624
  553.1 23.5 %all-to-all-start.2 = ((bf16[16,72,384]{2,1,0:T(8,128)(2,1)}), bf16[16,72,384]{2,1,0:T(8,128)(2,1)S(1)}, u32[]{:S(2)}, u32[]{:S(2)}) async-start(bf16[16,72,384]{2,1,0:T(8,128)(2,1)} %pad.72), calls=%async_computation.2 | async-start | bytes 1769472 | tf_op jit(solution)/shard_map/all_to_all | solution.py:640
  600.2 20.3 %collective-permute-start.52 = (bf16[7,72,384]{2,1,0:T(8,128)(2,1)S(1)}, bf16[7,72,384]{2,1,0:T(8,128)(2,1)S(1)}, u32[]{:S(2)}, u32[]{:S(2)}) collective-permute-start(bf16[7,72,384]{2,1,0:T(8,128)(2,1)S(1)} %fusion.18), channel_id=1, source_target_pairs={{0,3},{1,2},{2,1},{3,0},{4,7},{5,6},{6,5},{7,4},{8,11},{9,10},{10,... | collective-permute-start | bytes 1161224 | tf_op jit(solution)/shard_map/ppermute | solution.py:644
  605.4 20.6 %all-to-all-start.1 = ((bf16[16,72,384]{2,1,0:T(8,128)(2,1)}), bf16[16,72,384]{2,1,0:T(8,128)(2,1)}, u32[]{:S(2)}, u32[]{:S(2)}) async-start(bf16[16,72,384]{2,1,0:T(8,128)(2,1)} %fusion.14), calls=%async_computation.1 | async-start | bytes 1769472 | tf_op jit(solution)/shard_map/all_to_all | solution.py:640
  (89 other events, 947.1 us)
Sparse Core Ops, SparseCore 0:
  10.5 190.6 all-gather.8
  293.0 85.6 all-gather.10
  381.2 79.2 all-gather.12
  462.8 57.4 all-gather.14

commit v4 on v3

--- a/solution.py
+++ b/solution.py
@@ -97,6 +97,10 @@
     )
 
 
+def scaled(block):
+    return (block.astype(f32) * SCALE).astype(bf16)
+
+
 def one_pair(both):
     rows = both.shape[0] // 2
     lane = lax.broadcasted_iota(jnp.int32, (rows, 128), 1)
@@ -112,8 +116,7 @@
 def forward_kernel(q_ref, kn_ref, kf_ref, vn_ref, vf_ref, bias_ref, out_ref, lse_ref):
     bias = bias_ref[0]
     keys, values = rows_of(kn_ref, kf_ref), rows_of(vn_ref, vf_ref)
-    scores = contract(two_heads(q_ref[...]), keys, 1, 1) * SCALE
-    scores = scores + jnp.concatenate([bias, bias], 0)
+    scores = contract(two_heads(scaled(q_ref[...])), keys, 1, 1) + jnp.concatenate([bias, bias], 0)
     top = jnp.max(scores, axis=1, keepdims=True)
     shifted = jnp.exp(scores - top)
     total = jnp.sum(shifted, axis=1, keepdims=True)
@@ -127,8 +130,7 @@
     bias = bias_ref[0]
     keys, values = rows_of(kn_ref, kf_ref), rows_of(vn_ref, vf_ref)
     lse = jnp.transpose(jnp.broadcast_to(lse_ref[0, 0][:1], (128, 128)))[:, :1]
-    scores = contract(two_heads(q_ref[...]), keys, 1, 1) * SCALE
-    scores = scores + jnp.concatenate([bias, bias], 0)
+    scores = contract(two_heads(scaled(q_ref[...])), keys, 1, 1) + jnp.concatenate([bias, bias], 0)
     probs = jnp.exp(scores - lse)
     grad_probs = contract(two_heads(do_ref[...]), values, 1, 1)
     dots = jnp.sum(grad_probs * probs, axis=1, keepdims=True)
@@ -192,6 +194,27 @@
     kv_ref[:rows] = product(1).astype(bf16)
     kv_ref[rows:] = (product(2) + sv_ref[...]).astype(bf16)
     q_ref[...] = (product(0) + sq_ref[...]).astype(bf16)
+
+
+def kv_all_kernel(xn_ref, xf_ref, near_ref, far_ref, place_ref, gain_ref, bias_ref, sq_ref, sv_ref, q_ref, kn_ref, kf_ref):
+    rows = xn_ref.shape[1]
+    x = jnp.concatenate([xn_ref[0], xf_ref[0]], 0)[:, :D]
+    z, _ = normalized(x.astype(f32))
+    normed = (z * gain_ref[...] + bias_ref[...]).astype(bf16)
+    placed = matmul(normed, place_ref[...]).astype(bf16)
+
+    def product(left, j):
+        near, far = input_weight(near_ref, far_ref, j)
+        return matmul(left[:, :HALF], near) + matmul(left[:, HALF:], far)
+
+    keys = product(placed, 1).astype(bf16)
+    values = (product(placed, 2) + sv_ref[...]).astype(bf16)
+    kn_ref[0, 0], kn_ref[0, 1] = keys[:rows], values[:rows]
+    kf_ref[0, 0], kf_ref[0, 1] = keys[rows:], values[rows:]
+
+    @pl.when(pl.program_id(0) == 0)
+    def _():
+        q_ref[...] = (product(placed[:rows], 0) + sq_ref[...]).astype(bf16)
 
 
 def qkv_back_kernel(dq_ref, dk_ref, dv_ref, near_ref, far_ref, place_ref, x_ref, gain_ref, gh_ref, gin_ref, sums_ref):
@@ -220,7 +243,7 @@
     return out_copy, fc, proj
 
 
-def ffn_kernel(
+def ffn_forward(
     att_ref, x_ref, place_ref, os_ref, gain_ref, bias_ref, ps_ref, fs_ref, all_ref,
     hidden_ref, n2_ref, pre_ref, out_ref, fc_buf, out_buf, proj_buf, sems,
 ):
@@ -249,6 +272,32 @@
     out_ref[...] = total.astype(bf16)
 
 
+def ffn_backward(
+    go_ref, pre_ref, hidden_ref, place_ref, gain_ref, ready,
+    gh_ref, gb_ref, ga_ref, sums_ref, fc_buf, out_buf, proj_buf,
+):
+    grad_out = go_ref[...]
+    placed = 0.0
+    for j in range(SPLITS):
+        pre = pre_ref[j]
+        _, t = gelu_parts(pre)
+        slope = gelu_slope(pre, t)
+        ready("proj", j)
+        grad_pre = (contract(grad_out, proj_buf[j].reshape(D, D), 1, 1) * slope).astype(bf16)
+        ready("fc", j)
+        placed = placed + contract(grad_pre, fc_buf[j].reshape(KPAD, D), 1, 1)
+    place = place_ref[...]
+    by_hidden, sums_ref[...] = norm_back(hidden_ref[...], gain_ref[...], unplaced(placed, place))
+    grad_hidden = grad_out.astype(f32) + by_hidden
+    gh_ref[...] = grad_hidden
+    branch = grad_hidden.astype(bf16)
+    gb_ref[...] = branch
+    ready("out", 0)
+    grad_att = contract(branch, out_buf[...].reshape(KPAD, D), 1, 1).astype(bf16)
+    ga_ref[...] = jnp.zeros_like(ga_ref)
+    ga_ref[:, :D] = contract(grad_att, place, 1, 1).astype(bf16)
+
+
 def ffn_back_kernel(
     go_ref, pre_ref, hidden_ref, place_ref, gain_ref, all_ref,
     gh_ref, gb_ref, ga_ref, sums_ref, fc_buf, out_buf, proj_buf, sems,
@@ -258,26 +307,25 @@
         proj[j].start()
         fc[j].start()
     out_copy.start()
-    grad_out = go_ref[...]
-    placed = 0.0
-    for j in range(SPLITS):
-        pre = pre_ref[j]
-        _, t = gelu_parts(pre)
-        slope = gelu_slope(pre, t)
-        proj[j].wait()
-        grad_pre = (contract(grad_out, proj_buf[j].reshape(D, D), 1, 1) * slope).astype(bf16)
-        fc[j].wait()
-        placed = placed + contract(grad_pre, fc_buf[j].reshape(KPAD, D), 1, 1)
-    place = place_ref[...]
-    by_hidden, sums_ref[...] = norm_back(hidden_ref[...], gain_ref[...], unplaced(placed, place))
-    grad_hidden = grad_out.astype(f32) + by_hidden
-    gh_ref[...] = grad_hidden
-    branch = grad_hidden.astype(bf16)
-    gb_ref[...] = branch
-    out_copy.wait()
-    grad_att = contract(branch, out_buf[...].reshape(KPAD, D), 1, 1).astype(bf16)
-    ga_ref[...] = jnp.zeros_like(ga_ref)
-    ga_ref[:, :D] = contract(grad_att, place, 1, 1).astype(bf16)
+    copies = {"proj": proj, "fc": fc, "out": [out_copy]}
+    ffn_backward(
+        go_ref, pre_ref, hidden_ref, place_ref, gain_ref, lambda kind, j: copies[kind][j].wait(),
+        gh_ref, gb_ref, ga_ref, sums_ref, fc_buf, out_buf, proj_buf,
+    )
+
+
+def ffn_both_kernel(
+    att_ref, x_ref, place_ref, os_ref, gain_ref, bias_ref, ps_ref, fs_ref, all_ref, go_ref,
+    hidden_ref, n2_ref, pre_ref, out_ref, gh_ref, gb_ref, ga_ref, sums_ref, fc_buf, out_buf, proj_buf, sems,
+):
+    ffn_forward(
+        att_ref, x_ref, place_ref, os_ref, gain_ref, bias_ref, ps_ref, fs_ref, all_ref,
+        hidden_ref, n2_ref, pre_ref, out_ref, fc_buf, out_buf, proj_buf, sems,
+    )
+    ffn_backward(
+        go_ref, pre_ref, hidden_ref, place_ref, gain_ref, lambda kind, j: None,
+        gh_ref, gb_ref, ga_ref, sums_ref, fc_buf, out_buf, proj_buf,
+    )
 
 
 def column_kernel(me_ref, k_ref, v_ref, q_ref, a_ref, lse_ref, don_ref, dof_ref, bias_ref, dk_ref, dv_ref):
@@ -291,17 +339,16 @@
     bias = bias_ref[0]
     micro = pl.program_id(0)
     term_row = lax.broadcasted_iota(jnp.int32, (16, 128), 0)
+    terms = (3 * SHARDS, SHARDS * span)
     place_of = (
-        lax.broadcasted_iota(jnp.int32, (SHARDS, SHARDS * span), 1) // span
-        == lax.broadcasted_iota(jnp.int32, (SHARDS, SHARDS * span), 0)
+        lax.broadcasted_iota(jnp.int32, terms, 1) // span == lax.broadcasted_iota(jnp.int32, terms, 0) % SHARDS
     ).astype(bf16)
-    spread_lse = 0.0
-    for term in range(3):
-        picked = [
-            jnp.sum(jnp.where(term_row == 2 * term + micro, lse_ref[owner].astype(f32), 0.0), axis=0, keepdims=True)
-            for owner in owners
-        ]
-        spread_lse = spread_lse + contract(jnp.concatenate(picked, 0).astype(bf16), place_of, 0, 0)
+    picked = [
+        jnp.sum(jnp.where(term_row == 2 * term + micro, lse_ref[owner].astype(f32), 0.0), axis=0, keepdims=True)
+        for term in range(3)
+        for owner in owners
+    ]
+    spread_lse = contract(jnp.concatenate(picked, 0).astype(bf16), place_of, 0, 0)
     on_diagonal = (
         lax.broadcasted_iota(jnp.int32, spread_lse.shape, 0) % span
         == lax.broadcasted_iota(jnp.int32, spread_lse.shape, 1) % span
@@ -311,19 +358,19 @@
     lse_b = jnp.sum(spread_lse[span:], axis=0, keepdims=True)
     product = attended.astype(f32) * grads.astype(f32)
     sides = (
-        lax.broadcasted_iota(jnp.int32, (8, 128), 1) // HEAD_DIM
-        == lax.broadcasted_iota(jnp.int32, (8, 128), 0)
+        lax.broadcasted_iota(jnp.int32, (8, 256), 1) % 128 // HEAD_DIM
+        == lax.broadcasted_iota(jnp.int32, (8, 256), 0)
     ).astype(bf16)
     high = product.astype(bf16)
     low = (product - high.astype(f32)).astype(bf16)
-    dots = contract(sides, high, 1, 1) + contract(sides, low, 1, 1)
+    dots = contract(sides, jnp.concatenate([high, low], 1), 1, 1)
 
     def spread(row_a, row_b):
         return jnp.concatenate(
             [jnp.broadcast_to(row_a, (rows, row_a.shape[1])), jnp.broadcast_to(row_b, (rows, row_b.shape[1]))], 0
         )
 
-    scores = contract(two_heads(k_ref[...]), queries, 1, 1) * SCALE
+    scores = contract(two_heads(scaled(k_ref[...])), queries, 1, 1)
     probs = jnp.exp(scores + jnp.concatenate([bias, bias], 0) - spread(lse_a, lse_b))
     grad_probs = contract(two_heads(v_ref[...]), grads, 1, 1)
     grad_scores = (probs * (grad_probs - spread(dots[:1], dots[1:2]))).astype(bf16)
@@ -378,11 +425,15 @@
     return jax.ShapeDtypeStruct(dims, dtype)
 
 
-def whole_call(body, out_shape, operands, in_hbm=(), scratch=(), flops=0, bytes_accessed=0, vmem=56):
+def whole_call(body, out_shape, operands, in_hbm=(), first_rows=(), scratch=(), flops=0, bytes_accessed=0, vmem=56):
     vm, hbm = pl.BlockSpec(memory_space=pltpu.VMEM), pl.BlockSpec(memory_space=pl.ANY)
+    weight = pl.BlockSpec((8, 256, LANES), lambda s: (0, 0, 0))
     return pl.pallas_call(
         body,
-        in_specs=[hbm if i in in_hbm else vm for i in range(len(operands))],
+        grid=(1,) if first_rows else (),
+        in_specs=[
+            hbm if i in in_hbm else weight if i in first_rows else vm for i in range(len(operands))
+        ],
         out_specs=[vm] * len(out_shape),
         out_shape=out_shape,
         scratch_shapes=list(scratch),
@@ -441,6 +492,9 @@
     def rows_padded(block):
         return jnp.pad(block, ((0, PROWS - block.shape[0]), (0, 0)))
 
+    swapped = sequence_order[0, 0] == 1
+    ordered_inputs = jnp.where(swapped, inputs[::-1], inputs).reshape(tokens, D)
+
     later = jnp.concatenate(
         [rows_padded(w_fc[0][:, j * D : (j + 1) * D]) for j in range(SPLITS)]
         + [rows_padded(w_out[0]), w_proj[0]],
@@ -456,7 +510,7 @@
             jnp.pad(w_qkv[0][:, j * D : (j + 1) * D], ((0, PROWS - DROWS), (0, LANES - D)))
             for j in range(3)
         ]
-        + [vector_rows],
+        + [vector_rows, jnp.pad(ordered_inputs, ((0, 0), (0, LANES - D)))],
         0,
     )
     first_near, first_far = gather_both(first)
@@ -479,8 +533,6 @@
     place_rel = placing(me, True)
     place_abs = placing(me, False)
 
-    swapped = sequence_order[0, 0] == 1
-    ordered_inputs = jnp.where(swapped, inputs[::-1], inputs).reshape(tokens, D)
     ordered_segments = jnp.where(swapped, segment_ids[::-1], segment_ids)
     by_block = ordered_segments.reshape(micro, SHARDS, span)
     rel_devices = relative_device(me, place_iota)
@@ -509,15 +561,8 @@
     def by_kind(block):
         return block.reshape(8, -1, micro, span, LANES)
 
-    def forward_layer(layer_in):
-        normed_one, queries, keys_values = whole_call(
-            qkv_kernel,
-            [shape(tokens, D), token_shape, shape(2 * tokens, LANES)],
-            (layer_in, first_near, first_far, place_rel, gain_one, bias_one, shift_q, shift_v),
-            **qkv_cost,
-        )
-        kv_near, kv_far = [by_kind(b) for b in gather_both(keys_values)]
-        attended, log_total = pair_call(
+    def attention(queries, kv_near, kv_far):
+        return pair_call(
             forward_kernel,
             2,
             [own_spec(span)] + kv_specs + [bias_spec],
@@ -525,20 +570,51 @@
             [token_shape, shape(micro, PAIRS, 8, 128, dtype=f32)],
             (queries, kv_near, kv_far, kv_near, kv_far, row_bias),
         )
-        hidden, normed_two, pre_act, out_low = whole_call(
-            ffn_kernel,
-            [shape(tokens, D, dtype=f32), shape(tokens, D), shape(SPLITS, tokens, D, dtype=f32), shape(tokens, D)],
-            (attended, layer_in, place_abs, out_shift, gain_two, bias_two, proj_shift, fc_shift, later_all),
-            in_hbm=(8,),
-            **ffn_cost,
-        )
-        return out_low, (normed_one, queries, keys_values, kv_near, kv_far, attended, log_total, hidden, normed_two, pre_act)
-
-    sent_on, _ = forward_layer(ordered_inputs)
+
+    ffn_shapes = [shape(tokens, D, dtype=f32), shape(tokens, D), shape(SPLITS, tokens, D, dtype=f32), shape(tokens, D)]
+    back_shapes = [shape(tokens, D, dtype=f32), shape(tokens, D), token_shape, shape(8, D, dtype=f32)]
+    vectors_two = (out_shift, gain_two, bias_two, proj_shift, fc_shift)
+
+    step_fixed = lambda *dims: pl.BlockSpec(dims, lambda s: (0,) * len(dims))
+    x_spec = pl.BlockSpec((1, tokens, LANES), lambda s: (s, 2, 0))
+    kv_out = pl.BlockSpec((1, 2, tokens, LANES), lambda s: (s, 0, 0, 0))
+    queries, kv_near, kv_far = pl.pallas_call(
+        kv_all_kernel,
+        grid=(8,),
+        in_specs=[x_spec, x_spec, step_fixed(8, 256, LANES), step_fixed(8, 256, LANES), step_fixed(D, KPAD)]
+        + [step_fixed(1, D), step_fixed(1, D), step_fixed(1, LANES), step_fixed(1, LANES)],
+        out_specs=[step_fixed(tokens, LANES), kv_out, kv_out],
+        out_shape=[token_shape, shape(8, 2, tokens, LANES), shape(8, 2, tokens, LANES)],
+        **params(2 * SHARDS * tokens * D * 3 * D, 4 * SHARDS * 384 * LANES, vmem=48),
+    )(first_near, first_far, first_near, first_far, place_rel, gain_one, bias_one, shift_q, shift_v)
+    attended, _ = attention(queries, by_kind(kv_near), by_kind(kv_far))
+    _, _, _, sent_on = whole_call(
+        ffn_forward,
+        ffn_shapes,
+        (attended, ordered_inputs, place_abs, *vectors_two, later_all),
+        in_hbm=(8,),
+        **ffn_cost,
+    )
     received = lax.ppermute(sent_on, "section", [(0, 1)])
     layer_in = jnp.where(is_first, ordered_inputs, received)
-    out_low, kept = forward_layer(layer_in)
-    normed_one, queries, keys_values, kv_near, kv_far, attended, log_total, hidden, normed_two, pre_act = kept
+
+    own_cotangent = cotangent.reshape(tokens, D)
+    normed_one, queries, keys_values = whole_call(
+        qkv_kernel,
+        [shape(tokens, D), token_shape, shape(2 * tokens, LANES)],
+        (layer_in, first_near, first_far, place_rel, gain_one, bias_one, shift_q, shift_v),
+        first_rows=(1, 2),
+        **qkv_cost,
+    )
+    kv_near, kv_far = [by_kind(b) for b in gather_both(keys_values)]
+    attended, log_total = attention(queries, kv_near, kv_far)
+    hidden, normed_two, pre_act, out_low, *first_back = whole_call(
+        ffn_both_kernel,
+        ffn_shapes + back_shapes,
+        (attended, layer_in, place_abs, *vectors_two, later_all, own_cotangent),
+        in_hbm=(8,),
+        **ffn_cost,
+    )
 
     lse_own = log_total[:, :, 0]
     part_one = lax.reduce_precision(lse_own, 8, 7)
@@ -550,14 +626,8 @@
     )
     nn_all = lax.all_gather(jnp.concatenate([normed_one, normed_two], 0), "fsdp", axis=0)
 
-    def backward_layer(grad_out):
-        grad_hidden, grad_branch, grad_att, sums_two = whole_call(
-            ffn_back_kernel,
-            [shape(tokens, D, dtype=f32), shape(tokens, D), token_shape, shape(8, D, dtype=f32)],
-            (grad_out, pre_act, hidden, place_abs, gain_two, later_all),
-            in_hbm=(5,),
-            **ffn_cost,
-        )
+    def backward_layer(feed_forward):
+        grad_hidden, grad_branch, grad_att, sums_two = feed_forward
         def row_part():
             return pair_call(
                 row_kernel,
@@ -594,17 +664,25 @@
             qkv_back_kernel,
             [shape(tokens, D), shape(8, D, dtype=f32)],
             (grad_q, grad_k, grad_v, first_near, first_far, place_rel, layer_in, gain_one, grad_hidden),
+            first_rows=(3, 4),
             **qkv_cost,
         )
         norm_grads = jnp.concatenate([sums_one[:2], sums_two[:2]], 0)
         return grad_input, grad_branch, (grad_q, grad_k, grad_v), norm_grads
 
-    own_cotangent = cotangent.reshape(tokens, D)
-    sent_back, _, _, _ = backward_layer(own_cotangent)
+    sent_back, _, _, _ = backward_layer(first_back)
     received_grad = lax.ppermute(sent_back, "section", [(1, 0)])
     grad_out = jnp.where(is_last, own_cotangent, received_grad)
     go_all = lax.all_gather(grad_out, "fsdp", axis=0)
-    grad_input, grad_branch, grad_qkv, norm_grads = backward_layer(grad_out)
+    grad_input, grad_branch, grad_qkv, norm_grads = backward_layer(
+        whole_call(
+            ffn_back_kernel,
+            back_shapes,
+            (grad_out, pre_act, hidden, place_abs, gain_two, later_all),
+            in_hbm=(5,),
+            **ffn_cost,
+        )
+    )
 
     fc_own = lax.dynamic_slice(later_all, (0, (me // 4) * PROWS, (me % 4) * FROWS), (SHARDS, PROWS, FROWS))
     fc_own = fc_own[:, :DROWS].reshape(D, FROWS)
@@ -650,6 +728,7 @@
         return jnp.take(finished, z ^ jnp.arange(4), axis=0)
 
     got_fc = to_owners(grad_fc_w.astype(bf16).reshape(SHARDS, DROWS, FROWS)).reshape(4, 4, height, width)
+    got_fc, grad_columns = lax.optimization_barrier((got_fc, grad_columns))
     own_vectors = jnp.concatenate([grad_fc_b[0], grad_proj_b, jnp.zeros((3 * width - FROWS - DROWS,), f32)])
     proj_part = jnp.pad(grad_proj_w.reshape(4, DROWS, D), ((0, 0), (0, 0), (0, 3 * width - D)))
     own_part = jnp.broadcast_to(own_vectors[None, None], (4, height - DROWS, 3 * width))

time: 682 us -> 650 us (0.953)
  waiting for transfers between devices: 231 us -> 209 us
  Pallas kernels: 219 us -> 230 us
  starting transfers between devices: 95.9 us -> 86.1 us
    ppermute x45 -> x36, waiting for transfers between devices: 165 us -> 135 us  [moved(): return lax.ppermute(value, 'fsdp', xor_pairs(k))]
    pallas_call x8 -> x7, Pallas kernels: 97 us -> 112 us  [the longest x6 79 us: whole_call(): pl.pallas_call(body, grid=(1,) if first_rows else (), in_specs=[hbm if i...]
    ppermute x45 -> x36, starting transfers between devices: 58.4 us -> 43.6 us  [moved(): return lax.ppermute(value, 'fsdp', xor_pairs(k))]
    all_gather x1, waiting for transfers between devices: 4.57 us -> 18.5 us  [shards(): later_all = lax.all_gather(later, 'fsdp', axis=0, tiled=False)]
    all_gather x1, starting transfers between devices: 0.04 us -> 8.79 us  [shards(): lax.all_gather(jnp.concatenate([normed_one, normed_two], 0), 'fsdp', axis=0)]
    unnamed x169 -> x159, local copies, waits for them, and re-layouts: 38.2 us -> 35.8 us
  transfers between devices with their start and end apart: 66 -> 57, of which waited for: 40 -> 36; matrix products, arithmetic and copies ran while one was open for 11% -> 9% of each run, Pallas kernels for 28% -> 31%
where the time goes in v4:
time: 650 us; the launch traced here: 640 us
  Pallas kernels  230 us (35%)
  waiting for transfers between devices  209 us (32%)
  starting transfers between devices  86.1 us (13%)
  local copies, waits for them, and re-layouts  77.9 us (12%)
  other arithmetic  21.7 us (3%)
  between operations  15.6 us (2%)
    ppermute x36, waiting for transfers between devices, moved(): return lax.ppermute(value, 'fsdp', xor_pairs(k))  135 us
    pallas_call x6, Pallas kernels, pair_call(): pl.pallas_call(body, grid=(2, PAIRS), in_specs=in_specs, out_specs=out_sp...  94.1 us
    pallas_call x6, Pallas kernels, whole_call(): pl.pallas_call(body, grid=(1,) if first_rows else (), in_specs=[hbm if i...  79 us
    ppermute x36, starting transfers between devices, moved(): return lax.ppermute(value, 'fsdp', xor_pairs(k))  43.6 us
    unnamed x159, local copies, waits for them, and re-layouts  35.8 us
    pallas_call x1, Pallas kernels, shards(): pl.pallas_call(kv_all_kernel, grid=(8,), in_specs=[x_spec, x_spec, step_f...  32.9 us
    ppermute x12, waiting for transfers between devices, over_replicas(): lax.ppermute(v, 'replica', [(j, j ^ k) for j in range(4)])  25.6 us
    all_gather x1, waiting for transfers between devices, shards(): later_all = lax.all_gather(later, 'fsdp', axis=0, tiled=False)  18.5 us
  transfers between devices with their start and end apart: 57, of which 36 were waited for; matrix products, arithmetic and copies ran while one was open for 9% of the time, Pallas kernels for 31%

profile of v4, /device:TPU:0, one launch (start us, length us, event | category | flops | bytes accessed | tf_op | source)
XLA Modules:
  0.0 640.2 jit_solution(11299711764156017092)
XLA Ops:
  20.0 21.5 %collective-permute-done.1 = bf16[384,1152]{1,0:T(8,128)(2,1)S(1)} collective-permute-done((bf16[384,1152]{1,0:T(8,128)(2,1)S(1)}, bf16[384,1152]{1,0:T(8,128)(2,1)S(1)}, u32[]{:S(2)}, u32[]{:S(2)}) %collective-permute-start.1) | collective-permute-done | bytes 884768 | tf_op jit(solution)/shard_map/ppermute | solution.py:38
  53.9 10.8 %collective-permute-done.3 = bf16[192,1152]{1,0:T(8,128)(2,1)S(1)} collective-permute-done((bf16[192,1152]{1,0:T(8,128)(2,1)S(1)}, bf16[192,1152]{1,0:T(8,128)(2,1)S(1)}, u32[]{:S(2)}, u32[]{:S(2)}) %collective-permute-start.3) | collective-permute-done | bytes 442400 | tf_op jit(solution)/shard_map/ppermute | solution.py:38
  68.7 18.6 %collective-permute-done.2 = bf16[384,1152]{1,0:T(8,128)(2,1)S(1)} collective-permute-done((bf16[384,1152]{1,0:T(8,128)(2,1)S(1)}, bf16[384,1152]{1,0:T(8,128)(2,1)S(1)}, u32[]{:S(2)}, u32[]{:S(2)}) %collective-permute-start.2) | collective-permute-done | bytes 884768 | tf_op jit(solution)/shard_map/ppermute | solution.py:38
  110.4 32.9 %shard_map.263 = (bf16[128,1152]{1,0:T(8,128)(2,1)S(1)}, bf16[8,2,128,1152]{3,2,1,0:T(8,128)(2,1)}, bf16[8,2,128,1152]{3,2,1,0:T(8,128)(2,1)}) custom-call(bf16[8,384,1152]{2,1,0:T(8,128)(2,1)} %bitcast_dynamic-update-slice_fusion.xn_ref.near_ref, bf16[8,384,1152]{2,1,0:T(8,128)(2,1)} %collective-permute-done.8.xf_ref.far_ref, ...), custom_call_target="tpu_custom_call" | custom-call | flops 14545846272 | bytes 28311552 | tf_op jit(solution)/shard_map/pallas_call | solution.py:581
  148.1 14.1 %shard_map.264 = (bf16[128,1152]{1,0:T(8,128)(2,1)S(1)}, f32[2,9,8,128]{3,2,1,0:T(8,128)}) custom-call(bf16[128,1152]{1,0:T(8,128)(2,1)S(1)} %get-tuple-element.62.q_ref, bf16[8,2,2,64,1152]{4,3,2,1,0:T(8,128)(2,1)S(1)} %bitcast.226, bf16[8,2,2,64,1152]{4,3,2,1,0:T(8,128)(2,1)S(1)} %bitcast.228, bf16[8,2,2,64,1152]{4,3,2,1,0:T(8,128)(2,1)S(1)} %bitcast.227, ...), custom_call_target="tpu_custom_call" | custom-call | flops 4831838208 | bytes 9437184 | tf_op jit(solution)/shard_map/pallas_call | solution.py:446
  162.9 18.5 %all-gather.9.cloned.1.call-done = bf16[10752,1088]{1,0:T(8,128)(2,1)} async-done(((bf16[672,1088]{1,0:T(8,128)(2,1)}), bf16[10752,1088]{1,0:T(8,128)(2,1)}) %all-gather.9.cloned.1.call-update) | async-done | bytes 23396368 | tf_op jit(solution)/shard_map/all_gather | solution.py:503
  181.4 12.1 %shard_map.265 = (f32[128,1088]{1,0:T(8,128)}, bf16[128,1088]{1,0:T(8,128)(2,1)}, f32[4,128,1088]{2,1,0:T(8,128)}, bf16[128,1088]{1,0:T(8,128)(2,1)}) custom-call(bf16[128,1152]{1,0:T(8,128)(2,1)} %copy-done.16, bf16[128,1088]{1,0:T(8,128)(2,1)} %bitcast.248, bf16[1088,1280]{1,0:T(8,128)(2,1)} %fusion.1.place_ref, f32[1,1088]{1,0:T(1,128)} %reshape.547.os_ref, ...), custom_call_target="tpu_custom_call" | custom-call | flops 4848615424 | bytes 23396352 | tf_op jit(solution)/shard_map/pallas_call | solution.py:431
  203.8 8.1 %shard_map.266 = (bf16[128,1088]{1,0:T(8,128)(2,1)}, bf16[128,1152]{1,0:T(8,128)(2,1)}, bf16[256,1152]{1,0:T(8,128)(2,1)}) custom-call(bf16[128,1088]{1,0:T(8,128)(2,1)} %broadcast_select_fusion.2.x_ref, bf16[8,384,1152]{2,1,0:T(8,128)(2,1)} %bitcast_dynamic-update-slice_fusion.xn_ref.near_ref, bf16[8,384,1152]{2,1,0:T(8,128)(2,1)} %collective-permute-done.8.xf_ref.far_ref, ...), custom_call_target="tpu_custom_call" | custom-call | flops 3636461568 | bytes 9437184 | tf_op jit(solution)/shard_map/pallas_call | solution.py:431
  216.9 9.9 %collective-permute-done.11 = bf16[256,1152]{1,0:T(8,128)(2,1)S(1)} collective-permute-done((bf16[256,1152]{1,0:T(8,128)(2,1)}, bf16[256,1152]{1,0:T(8,128)(2,1)S(1)}, u32[]{:S(2)}, u32[]{:S(2)}) %collective-permute-start.11) | collective-permute-done | bytes 589856 | tf_op jit(solution)/shard_map/ppermute | solution.py:38
  258.3 13.2 %shard_map.267 = (bf16[128,1152]{1,0:T(8,128)(2,1)S(1)}, f32[2,9,8,128]{3,2,1,0:T(8,128)S(1)}) custom-call(bf16[128,1152]{1,0:T(8,128)(2,1)S(1)} %copy-done.14, bf16[8,2,2,64,1152]{4,3,2,1,0:T(8,128)(2,1)S(1)} %constant_dynamic-update-slice_fusion.6.kn_ref.vn_ref, bf16[8,2,2,64,1152]{4,3,2,1,0:T(8,128)(2,1)S(1)} %bitcast.220, ...), custom_call_target="tpu_custom_call" | custom-call | flops 4831838208 | bytes 9437184 | tf_op jit(solution)/shard_map/pallas_call | solution.py:446
  272.7 8.8 %all-gather.13.cloned.1.call-start = ((), (), s32[]{:S(2)}) async-start(), calls=%async_computation.5 | async-start | bytes 10027008 | tf_op jit(solution)/shard_map/all_gather | solution.py:627
  281.5 21.4 %shard_map.268 = (f32[128,1088]{1,0:T(8,128)}, bf16[128,1088]{1,0:T(8,128)(2,1)}, f32[4,128,1088]{2,1,0:T(8,128)}, bf16[128,1088]{1,0:T(8,128)(2,1)}, f32[128,10...) custom-call(bf16[128,1152]{1,0:T(8,128)(2,1)} %copy-done.9, ...), custom_call_target="tpu_custom_call" | custom-call | flops 4848615424 | bytes 23396352 | tf_op jit(solution)/shard_map/pallas_call | solution.py:431
  315.6 12.5 %shard_map.269.dq_ref = bf16[128,1152]{1,0:T(8,128)(2,1)S(1)} custom-call(bf16[128,1152]{1,0:T(8,128)(2,1)S(1)} %copy-done.14, bf16[128,1152]{1,0:T(8,128)(2,1)S(1)} %copy-done.12, f32[2,9,8,128]{3,2,1,0:T(8,128)S(1)} %get-tuple-element.72.lse_ref, bf16[8,2,2,64,1152]{4,3,2,1,0:T(8,128)(2,1)S(1)} %copy-done.2, bf16[8,2,2,64,1152]{4,3,2,1,0:T(8,128)(2,1)S(1)} %bitcast.222, ...), custom_call_target="tpu_custom_call" | custom-call | flops 7247757312 | bytes 9437184 | tf_op jit(solution)/shard_map/pallas_call | solution.py:446
  333.4 11.6 %collective-permute-done.23 = bf16[64,1152]{1,0:T(8,128)(2,1)S(1)} collective-permute-done((bf16[64,1152]{1,0:T(8,128)(2,1)S(1)}, bf16[64,1152]{1,0:T(8,128)(2,1)S(1)}, u32[]{:S(2)}, u32[]{:S(2)}) %collective-permute-start.23) | collective-permute-done | bytes 147488 | tf_op jit(solution)/shard_map/ppermute | solution.py:38
  358.8 20.7 %shard_map.270 = (bf16[128,1152]{1,0:T(8,128)(2,1)}, bf16[128,1152]{1,0:T(8,128)(2,1)}) custom-call(s32[1]{0:T(128)} %bitcast.45.me_ref, bf16[256,1152]{1,0:T(8,128)(2,1)} %get-tuple-element.68.k_ref.v_ref, bf16[256,1152]{1,0:T(8,128)(2,1)} %get-tuple-element.68.k_ref.v_ref, bf16[16,272,1152]{2,1,0:T(8,128)(2,1)} %bitcast.237, ...), custom_call_target="tpu_custom_call" | custom-call | flops 12079595520 | bytes 9437184 | tf_op jit(solution)/shard_map/pallas_call | solution.py:446
  379.6 9.6 %shard_map.271 = (bf16[128,1088]{1,0:T(8,128)(2,1)}, f32[8,1088]{1,0:T(8,128)}) custom-call(bf16[128,1152]{1,0:T(8,128)(2,1)} %copy-done.15, bf16[128,1152]{1,0:T(8,128)(2,1)} %get-tuple-element.77.dk_ref, bf16[128,1152]{1,0:T(8,128)(2,1)} %get-tuple-element.78.dv_ref, bf16[8,384,1152]{2,1,0:T(8,128)(2,1)} %bitcast_dynamic-update-slice_fusion.xn_ref.near_ref, ...), custom_call_target="tpu_custom_call" | custom-call | flops 3636461568 | bytes 9437184 | tf_op jit(solution)/shard_map/pallas_call | solution.py:431
  390.9 11.7 %collective-permute-done.28 = bf16[128,1088]{1,0:T(8,128)(2,1)S(1)} collective-permute-done((bf16[128,1088]{1,0:T(8,128)(2,1)}, bf16[128,1088]{1,0:T(8,128)(2,1)S(1)}, u32[]{:S(2)}, u32[]{:S(2)}) %collective-permute-start.28) | collective-permute-done | bytes 278560 | tf_op jit(solution)/shard_map/ppermute | solution.py:674
  403.3 18.4 %shard_map.272 = (f32[128,1088]{1,0:T(8,128)}, bf16[128,1088]{1,0:T(8,128)(2,1)}, bf16[128,1152]{1,0:T(8,128)(2,1)}, f32[8,1088]{1,0:T(8,128)}) custom-call(bf16[128,1088]{1,0:T(8,128)(2,1)} %broadcast_select_fusion.1.go_ref, f32[4,128,1088]{2,1,0:T(8,128)} %get-tuple-element.81.pre_ref, f32[128,1088]{1,0:T(8,128)} %get-tuple-element.82.hidden_ref, ...), custom_call_target="tpu_custom_call" | custom-call | flops 4848615424 | bytes 23396352 | tf_op jit(solution)/shard_map/pallas_call | solution.py:431
  430.2 12.5 %shard_map.273.dq_ref = bf16[128,1152]{1,0:T(8,128)(2,1)S(1)} custom-call(bf16[128,1152]{1,0:T(8,128)(2,1)S(1)} %copy-done.14, bf16[128,1152]{1,0:T(8,128)(2,1)S(1)} %copy-done.10, f32[2,9,8,128]{3,2,1,0:T(8,128)S(1)} %get-tuple-element.72.lse_ref, bf16[8,2,2,64,1152]{4,3,2,1,0:T(8,128)(2,1)S(1)} %copy-done.3, bf16[8,2,2,64,1152]{4,3,2,1,0:T(8,128)(2,1)S(1)} %bitcast.224, ...), custom_call_target="tpu_custom_call" | custom-call | flops 7247757312 | bytes 9437184 | tf_op jit(solution)/shard_map/pallas_call | solution.py:446
  474.7 21.1 %shard_map.274 = (bf16[128,1152]{1,0:T(8,128)(2,1)}, bf16[128,1152]{1,0:T(8,128)(2,1)}) custom-call(s32[1]{0:T(128)} %bitcast.45.me_ref, bf16[256,1152]{1,0:T(8,128)(2,1)} %get-tuple-element.68.k_ref.v_ref, bf16[256,1152]{1,0:T(8,128)(2,1)} %get-tuple-element.68.k_ref.v_ref, bf16[16,272,1152]{2,1,0:T(8,128)(2,1)} %bitcast.240, ...), custom_call_target="tpu_custom_call" | custom-call | flops 12079595520 | bytes 9437184 | tf_op jit(solution)/shard_map/pallas_call | solution.py:446
  504.0 14.6 %shard_map.276 = (f32[272,1088]{1,0:T(8,128)}, f32[1088,272]{1,0:T(8,128)}, f32[8,272]{1,0:T(8,128)}, f32[8,1088]{1,0:T(8,128)}) custom-call(bf16[16,256,1088]{2,1,0:T(8,128)(2,1)} %bitcast.244, bf16[16,128,1088]{2,1,0:T(8,128)(2,1)} %bitcast.307, bf16[1088,272]{1,0:T(8,128)(2,1)} %reshape.559.fc_ref, f32[1,272]{1,0:T(1,128)} %get-tuple-element.203.fb_ref, ...), custom_call_target="tpu_custom_call" | custom-call | flops 19394461696 | bytes 13369344 | tf_op jit(solution)/shard_map/pallas_call | solution.py:691
  532.5 9.3 %shard_map.277 = (f32[1088,272]{1,0:T(8,128)}, f32[8,272]{1,0:T(8,128)}) custom-call(s32[1]{0:T(128)} %bitcast.45.me_ref, bf16[16,256,1088]{2,1,0:T(8,128)(2,1)} %bitcast.245, bf16[16,272,1152]{2,1,0:T(8,128)(2,1)} %bitcast.243, bf16[16,128,272]{2,1,0:T(8,128)(2,1)} %copy.87.cols_ref), custom_call_target="tpu_custom_call" | custom-call | flops 4848615424 | bytes 17825792 | tf_op jit(solution)/shard_map/pallas_call | solution.py:704
  551.2 9.5 %shard_map.275 = (bf16[128,1088]{1,0:T(8,128)(2,1)}, f32[8,1088]{1,0:T(8,128)}) custom-call(bf16[128,1152]{1,0:T(8,128)(2,1)} %copy-done.13, bf16[128,1152]{1,0:T(8,128)(2,1)} %get-tuple-element.88.dk_ref, bf16[128,1152]{1,0:T(8,128)(2,1)} %get-tuple-element.89.dv_ref, bf16[8,384,1152]{2,1,0:T(8,128)(2,1)} %bitcast_dynamic-update-slice_fusion.xn_ref.near_ref, ...), custom_call_target="tpu_custom_call" | custom-call | flops 3636461568 | bytes 9437184 | tf_op jit(solution)/shard_map/pallas_call | solution.py:431
  579.1 10.5 %collective-permute-done.43 = bf16[7,72,384]{2,1,0:T(8,128)(2,1)S(1)} collective-permute-done((bf16[7,72,384]{2,1,0:T(8,128)(2,1)S(1)}, bf16[7,72,384]{2,1,0:T(8,128)(2,1)S(1)}, u32[]{:S(2)}, u32[]{:S(2)}) %collective-permute-start.43) | collective-permute-done | bytes 387104 | tf_op jit(solution)/shard_map/ppermute | solution.py:722
  (417 shorter events, 272.9 us)
Async XLA Ops:
  7.2 174.2 %all-gather.9.cloned.1.call-start = ((), (), s32[]{:S(2)}) async-start(), calls=%async_computation.3 | async-start | bytes 26320896 | tf_op jit(solution)/shard_map/all_gather | solution.py:503
  10.2 348.7 %all-gather.11.cloned.1.call-start = ((), (), s32[]{:S(2)}) async-start(), calls=%async_computation.4 | async-start | bytes 10653696 | tf_op jit(solution)/shard_map/all_gather | solution.py:624
  12.1 29.4 %collective-permute-start.1 = (bf16[384,1152]{1,0:T(8,128)(2,1)S(1)}, bf16[384,1152]{1,0:T(8,128)(2,1)S(1)}, u32[]{:S(2)}, u32[]{:S(2)}) collective-permute-start(bf16[384,1152]{1,0:T(8,128)(2,1)S(1)} %pad_dynamic-update-slice_fusion), channel_id=1, source_target_pairs={{0,16},{4,20},{8,24},{12,28},{16,0},{20,4},{24,8},{28,12},{32,48},... | collective-permute-start | bytes 2654216 | tf_op jit(solution)/shard_map/ppermute | solution.py:38
  13.8 32.3 %collective-permute-start.4 = (bf16[384,1152]{1,0:T(8,128)(2,1)S(1)}, bf16[384,1152]{1,0:T(8,128)(2,1)S(1)}, u32[]{:S(2)}, u32[]{:S(2)}) collective-permute-start(bf16[384,1152]{1,0:T(8,128)(2,1)S(1)} %pad_dynamic-update-slice_fusion), channel_id=1, source_target_pairs={{0,48},{4,52},{8,56},{12,60},{16,32},{20,36},{24,40},{28,44},{32,1... | collective-permute-start | bytes 2654216 | tf_op jit(solution)/shard_map/ppermute | solution.py:38
  16.0 35.9 %collective-permute-start = (bf16[384,1152]{1,0:T(8,128)(2,1)S(1)}, bf16[384,1152]{1,0:T(8,128)(2,1)S(1)}, u32[]{:S(2)}, u32[]{:S(2)}) collective-permute-start(bf16[384,1152]{1,0:T(8,128)(2,1)S(1)} %pad_dynamic-update-slice_fusion), channel_id=1, source_target_pairs={{0,8},{4,12},{8,0},{12,4},{16,24},{20,28},{24,16},{28,20},{32,40},... | collective-permute-start | bytes 2654216 | tf_op jit(solution)/shard_map/ppermute | solution.py:38
  41.5 23.2 %collective-permute-start.3 = (bf16[192,1152]{1,0:T(8,128)(2,1)S(1)}, bf16[192,1152]{1,0:T(8,128)(2,1)S(1)}, u32[]{:S(2)}, u32[]{:S(2)}) collective-permute-start(bf16[192,1152]{1,0:T(8,128)(2,1)S(1)} %slice.260), channel_id=1, source_target_pairs={{0,48},{4,52},{8,56},{12,60},{16,32},{20,36},{24,40},{28,44},{32,1... | collective-permute-start | bytes 1327112 | tf_op jit(solution)/shard_map/ppermute | solution.py:38
  46.1 20.3 %collective-permute-start.5 = (bf16[192,1152]{1,0:T(8,128)(2,1)S(1)}, bf16[192,1152]{1,0:T(8,128)(2,1)S(1)}, u32[]{:S(2)}, u32[]{:S(2)}) collective-permute-start(bf16[192,1152]{1,0:T(8,128)(2,1)S(1)} %slice.261), channel_id=1, source_target_pairs={{0,16},{4,20},{8,24},{12,28},{16,0},{20,4},{24,8},{28,12},{32,48},... | collective-permute-start | bytes 1327112 | tf_op jit(solution)/shard_map/ppermute | solution.py:38
  51.9 35.4 %collective-permute-start.2 = (bf16[384,1152]{1,0:T(8,128)(2,1)S(1)}, bf16[384,1152]{1,0:T(8,128)(2,1)S(1)}, u32[]{:S(2)}, u32[]{:S(2)}) collective-permute-start(bf16[384,1152]{1,0:T(8,128)(2,1)S(1)} %collective-permute-done), channel_id=1, source_target_pairs={{0,16},{4,20},{8,24},{12,28},{16,0},{20,4},{24,8},{28,12},{32,48},... | collective-permute-start | bytes 2654216 | tf_op jit(solution)/shard_map/ppermute | solution.py:38
  51.9 39.4 %collective-permute-start.7 = (bf16[384,1152]{1,0:T(8,128)(2,1)S(1)}, bf16[384,1152]{1,0:T(8,128)(2,1)S(1)}, u32[]{:S(2)}, u32[]{:S(2)}) collective-permute-start(bf16[384,1152]{1,0:T(8,128)(2,1)S(1)} %collective-permute-done), channel_id=1, source_target_pairs={{0,48},{4,52},{8,56},{12,60},{16,32},{20,36},{24,40},{28,44},{32,1... | collective-permute-start | bytes 2654216 | tf_op jit(solution)/shard_map/ppermute | solution.py:38
  66.4 22.9 %collective-permute-start.6 = (bf16[384,1152]{1,0:T(8,128)(2,1)S(1)}, bf16[384,1152]{1,0:T(8,128)(2,1)S(1)}, u32[]{:S(2)}, u32[]{:S(2)}) collective-permute-start(bf16[384,1152]{1,0:T(8,128)(2,1)S(1)} %constant_dynamic-update-slice_fusion.1), channel_id=1, source_target_pairs={{0,8},{4,12},{8,0},{12,4},{16,24},{20,28},{24,16},{28,20},{32,40},... | collective-permute-start | bytes 2654216 | tf_op jit(solution)/shard_map/ppermute | solution.py:38
  230.1 20.1 %collective-permute-start.17 = (bf16[256,1152]{1,0:T(8,128)(2,1)S(1)}, bf16[256,1152]{1,0:T(8,128)(2,1)S(1)}, u32[]{:S(2)}, u32[]{:S(2)}) collective-permute-start(bf16[256,1152]{1,0:T(8,128)(2,1)S(1)} %collective-permute-done.10), channel_id=1, source_target_pairs={{0,48},{4,52},{8,56},{12,60},{16,32},{20,36},{24,40},{28,44},{32,1... | collective-permute-start | bytes 1769480 | tf_op jit(solution)/shard_map/ppermute | solution.py:38
  272.7 231.3 %all-gather.13.cloned.1.call-start = ((), (), s32[]{:S(2)}) async-start(), calls=%async_computation.5 | async-start | bytes 10027008 | tf_op jit(solution)/shard_map/all_gather | solution.py:627
  304.9 199.1 %all-gather.15.cloned.1.call-start = ((), (), s32[]{:S(2)}) async-start(), calls=%async_computation.6 | async-start | bytes 5013504 | tf_op jit(solution)/shard_map/all_gather | solution.py:676
  304.9 23.2 %collective-permute-start.19 = (bf16[128,1152]{1,0:T(8,128)(2,1)}, bf16[128,1152]{1,0:T(8,128)(2,1)S(1)}, u32[]{:S(2)}, u32[]{:S(2)}) collective-permute-start(bf16[128,1152]{1,0:T(8,128)(2,1)} %get-tuple-element.71.do_ref), channel_id=1, source_target_pairs={{0,16},{4,20},{8,24},{12,28},{16,0},{20,4},{24,8},{28,12},{32,48},... | collective-permute-start | bytes 884744 | tf_op jit(solution)/shard_map/ppermute | solution.py:38
  305.2 23.0 %collective-permute-start.20 = (bf16[128,1152]{1,0:T(8,128)(2,1)}, bf16[128,1152]{1,0:T(8,128)(2,1)S(1)}, u32[]{:S(2)}, u32[]{:S(2)}) collective-permute-start(bf16[128,1152]{1,0:T(8,128)(2,1)} %get-tuple-element.71.do_ref), channel_id=1, source_target_pairs={{0,48},{4,52},{8,56},{12,60},{16,32},{20,36},{24,40},{28,44},{32,1... | collective-permute-start | bytes 884744 | tf_op jit(solution)/shard_map/ppermute | solution.py:38
  307.3 20.9 %collective-permute-start.21 = (bf16[128,1152]{1,0:T(8,128)(2,1)}, bf16[128,1152]{1,0:T(8,128)(2,1)S(1)}, u32[]{:S(2)}, u32[]{:S(2)}) collective-permute-start(bf16[128,1152]{1,0:T(8,128)(2,1)} %get-tuple-element.71.do_ref), channel_id=1, source_target_pairs={{0,8},{4,12},{8,0},{12,4},{16,24},{20,28},{24,16},{28,20},{32,40},... | collective-permute-start | bytes 884744 | tf_op jit(solution)/shard_map/ppermute | solution.py:38
  329.9 23.7 %collective-permute-start.26 = (bf16[128,1152]{1,0:T(8,128)(2,1)S(1)}, bf16[128,1152]{1,0:T(8,128)(2,1)S(1)}, u32[]{:S(2)}, u32[]{:S(2)}) collective-permute-start(bf16[128,1152]{1,0:T(8,128)(2,1)S(1)} %collective-permute-done.21), channel_id=1, source_target_pairs={{0,48},{4,52},{8,56},{12,60},{16,32},{20,36},{24,40},{28,44},{32,1... | collective-permute-start | bytes 884744 | tf_op jit(solution)/shard_map/ppermute | solution.py:38
  421.7 21.8 %collective-permute-start.29 = (bf16[128,1152]{1,0:T(8,128)(2,1)}, bf16[128,1152]{1,0:T(8,128)(2,1)S(1)}, u32[]{:S(2)}, u32[]{:S(2)}) collective-permute-start(bf16[128,1152]{1,0:T(8,128)(2,1)} %get-tuple-element.83.do_ref), channel_id=1, source_target_pairs={{0,16},{4,20},{8,24},{12,28},{16,0},{20,4},{24,8},{28,12},{32,48},... | collective-permute-start | bytes 884744 | tf_op jit(solution)/shard_map/ppermute | solution.py:38
  422.3 21.2 %collective-permute-start.30 = (bf16[128,1152]{1,0:T(8,128)(2,1)}, bf16[128,1152]{1,0:T(8,128)(2,1)S(1)}, u32[]{:S(2)}, u32[]{:S(2)}) collective-permute-start(bf16[128,1152]{1,0:T(8,128)(2,1)} %get-tuple-element.83.do_ref), channel_id=1, source_target_pairs={{0,48},{4,52},{8,56},{12,60},{16,32},{20,36},{24,40},{28,44},{32,1... | collective-permute-start | bytes 884744 | tf_op jit(solution)/shard_map/ppermute | solution.py:38
  422.3 21.2 %collective-permute-start.31 = (bf16[128,1152]{1,0:T(8,128)(2,1)}, bf16[128,1152]{1,0:T(8,128)(2,1)S(1)}, u32[]{:S(2)}, u32[]{:S(2)}) collective-permute-start(bf16[128,1152]{1,0:T(8,128)(2,1)} %get-tuple-element.83.do_ref), channel_id=1, source_target_pairs={{0,8},{4,12},{8,0},{12,4},{16,24},{20,28},{24,16},{28,20},{32,40},... | collective-permute-start | bytes 884744 | tf_op jit(solution)/shard_map/ppermute | solution.py:38
  445.4 22.5 %collective-permute-start.36 = (bf16[128,1152]{1,0:T(8,128)(2,1)S(1)}, bf16[128,1152]{1,0:T(8,128)(2,1)S(1)}, u32[]{:S(2)}, u32[]{:S(2)}) collective-permute-start(bf16[128,1152]{1,0:T(8,128)(2,1)S(1)} %collective-permute-done.31), channel_id=1, source_target_pairs={{0,48},{4,52},{8,56},{12,60},{16,32},{20,36},{24,40},{28,44},{32,1... | collective-permute-start | bytes 884744 | tf_op jit(solution)/shard_map/ppermute | solution.py:38
  499.7 23.0 %all-to-all-start = ((bf16[16,128,272]{1,2,0:T(8,128)(2,1)}), bf16[16,128,272]{1,2,0:T(8,128)(2,1)S(1)}, u32[]{:S(2)}, u32[]{:S(2)}) async-start(bf16[16,128,272]{1,2,0:T(8,128)(2,1)} %bitcast.84), calls=%async_computation | async-start | bytes 2228224 | tf_op jit(solution)/shard_map/all_to_all | solution.py:702
  569.4 20.2 %collective-permute-start.43 = (bf16[7,72,384]{2,1,0:T(8,128)(2,1)S(1)}, bf16[7,72,384]{2,1,0:T(8,128)(2,1)S(1)}, u32[]{:S(2)}, u32[]{:S(2)}) collective-permute-start(bf16[7,72,384]{2,1,0:T(8,128)(2,1)S(1)} %fusion.12), channel_id=1, source_target_pairs={{0,3},{1,2},{2,1},{3,0},{4,7},{5,6},{6,5},{7,4},{8,11},{9,10},{10,... | collective-permute-start | bytes 1161224 | tf_op jit(solution)/shard_map/ppermute | solution.py:722
  574.6 20.5 %all-to-all-start.2 = ((bf16[16,72,384]{2,1,0:T(8,128)(2,1)}), bf16[16,72,384]{2,1,0:T(8,128)(2,1)}, u32[]{:S(2)}, u32[]{:S(2)}) async-start(bf16[16,72,384]{2,1,0:T(8,128)(2,1)} %fusion.8), calls=%async_computation.2 | async-start | bytes 1769472 | tf_op jit(solution)/shard_map/all_to_all | solution.py:718
  (80 other events, 910.2 us)
Sparse Core Ops, SparseCore 0:
  10.5 170.8 all-gather.8
  272.8 86.0 all-gather.10
  361.3 78.4 all-gather.12
  442.7 57.7 all-gather.14

commit v5 on v4

--- a/solution.py
+++ b/solution.py
@@ -43,10 +43,12 @@
     blocks = {0: x, 4: moved(x, 4), 12: moved(x, 12), 2: moved(x, 2)}
     result = None
     if beside is not None:
-        blocks[4], blocks[12], blocks[2], result = lax.optimization_barrier(
-            (blocks[4], blocks[12], blocks[2], beside())
-        )
-    blocks[8] = jnp.concatenate([moved(blocks[4][:half], 12), moved(blocks[12][half:], 4)], 0)
+        blocks[8] = moved(x, 8)
+        first = (4, 12, 2, 8)
+        *arrived, result = lax.optimization_barrier((*[blocks[k] for k in first], beside()))
+        blocks.update(zip(first, arrived))
+    else:
+        blocks[8] = jnp.concatenate([moved(blocks[4][:half], 12), moved(blocks[12][half:], 4)], 0)
     blocks[6] = moved(blocks[2], 4)
     blocks[14] = moved(blocks[2], 12)
     blocks[10] = moved(blocks[8], 2)
@@ -636,6 +638,7 @@
                 own_spec(span),
                 token_shape,
                 (queries, grad_att, log_total, kv_near, kv_far, kv_near, kv_far, row_bias),
+                vmem=60,
             )
 
         near, grad_q = gather_near(grad_att, row_part)
@@ -700,7 +703,9 @@
     wide = jnp.concatenate([g[:, :D] for g in grad_qkv] + [grad_branch], 1)
     wide = wide.reshape(tokens, SHARDS, FROWS).transpose(1, 0, 2)
     columns = lax.all_to_all(wide, "fsdp", 0, 0)
-    columns, grad_fc_w, grad_proj_w = lax.optimization_barrier((columns, grad_fc_w, grad_proj_w))
+    columns, grad_fc_w, grad_proj_w, norm_grads = lax.optimization_barrier(
+        (columns, grad_fc_w, grad_proj_w, norm_grads)
+    )
     grad_columns, column_sums = pl.pallas_call(
         columns_kernel,
         grid=(8,),
@@ -717,13 +722,16 @@
         pads = ((0, 0), (0, height - columns_of_rows.shape[1]), (0, width - columns_of_rows.shape[2]))
         return lax.all_to_all(jnp.pad(columns_of_rows, pads), "fsdp", 0, 0)
 
-    def over_replicas(quarter):
+    swap = lambda v, k: lax.ppermute(v, "replica", [(j, j ^ k) for j in range(4)])
+
+    def own_quarter(quarter):
         pick = lambda k: lax.dynamic_index_in_dim(quarter, z ^ k, 0, keepdims=False)
-        swap = lambda v, k: lax.ppermute(v, "replica", [(j, j ^ k) for j in range(4)])
         total = pick(0).astype(f32)
         for term in [swap(pick(k), k) for k in (1, 3, 2)]:
             total = total + term.astype(f32)
-        total = total.astype(bf16)
+        return total.astype(bf16)
+
+    def all_quarters(total):
         finished = jnp.stack([total] + [swap(total, k) for k in (1, 2, 3)])
         return jnp.take(finished, z ^ jnp.arange(4), axis=0)
 
@@ -734,7 +742,7 @@
     own_part = jnp.broadcast_to(own_vectors[None, None], (4, height - DROWS, 3 * width))
     proj_part = jnp.concatenate([proj_part, own_part], 1).astype(bf16)
     proj_parts = [proj_part[:, None, :, j * width : (j + 1) * width] for j in range(3)]
-    ffn_total = over_replicas(jnp.concatenate([got_fc] + proj_parts, 1))
+    ffn_quarter = own_quarter(jnp.concatenate([got_fc] + proj_parts, 1))
 
     rows = jnp.concatenate(
         [
@@ -748,8 +756,10 @@
         jnp.pad(column_sums[0].astype(bf16), (0, width - FROWS))[None, None], (SHARDS, 1, width)
     )
     got = to_owners(jnp.concatenate([rows, sums_row], 1))
-    got, ffn_total = lax.optimization_barrier((got, ffn_total))
-    finished = over_replicas(got.reshape(4, 4, height, width)).reshape(SHARDS, height, width).astype(f32)
+    got, ffn_quarter = lax.optimization_barrier((got, ffn_quarter))
+    ffn_total = all_quarters(ffn_quarter)
+    finished = all_quarters(own_quarter(got.reshape(4, 4, height, width)))
+    finished = finished.reshape(SHARDS, height, width).astype(f32)
     proj_total = jnp.concatenate([ffn_total[:, 4], ffn_total[:, 5], ffn_total[:, 6]], 2).astype(f32)
     fc_total = ffn_total[:, :4].reshape(SHARDS, height, width).astype(f32)
 

time: 650 us -> 667 us (1.026)
  waiting for transfers between devices: 209 us -> 225 us
  local copies, waits for them, and re-layouts: 77.9 us -> 64.7 us
  Pallas kernels: 230 us -> 239 us
    ppermute x12, waiting for transfers between devices: 25.6 us -> 38.3 us  [shards(): lax.ppermute(v, 'replica', [(j, j ^ k) for j in range(4)])]
    ppermute x36 -> x34, waiting for transfers between devices: 135 us -> 123 us  [moved(): return lax.ppermute(value, 'fsdp', xor_pairs(k))]
    unnamed x159 -> x153, local copies, waits for them, and re-layouts: 35.8 us -> 24.6 us
    pallas_call x6, Pallas kernels: 94.1 us -> 103 us  [pair_call(): pl.pallas_call(body, grid=(2, PAIRS), in_specs=in_specs, out_specs=out_sp...]
    all_gather x1, waiting for transfers between devices: 0.02 us -> 8.31 us  [shards(): go_all = lax.all_gather(grad_out, 'fsdp', axis=0)]
    all_gather x1, waiting for transfers between devices: 0.12 us -> 7.67 us  [shards(): lax.all_gather(jnp.concatenate([queries, attended, lse_rows, jnp.zeros((1...]
    ppermute x36 -> x34, starting transfers between devices: 43.6 us -> 42.5 us  [moved(): return lax.ppermute(value, 'fsdp', xor_pairs(k))]
  transfers between devices with their start and end apart: 57 -> 55, of which waited for: 36 -> 32; matrix products, arithmetic and copies ran while one was open for 9% -> 9% of each run, Pallas kernels for 31% -> 30%
where the time goes in v5:
time: 667 us; the launch traced here: 657 us
  Pallas kernels  239 us (36%)
  waiting for transfers between devices  225 us (34%)
  starting transfers between devices  88.4 us (13%)
  local copies, waits for them, and re-layouts  64.7 us (10%)
  other arithmetic  23.8 us (4%)
  between operations  15.6 us (2%)
    ppermute x34, waiting for transfers between devices, moved(): return lax.ppermute(value, 'fsdp', xor_pairs(k))  123 us
    pallas_call x6, Pallas kernels, pair_call(): pl.pallas_call(body, grid=(2, PAIRS), in_specs=in_specs, out_specs=out_sp...  103 us
    pallas_call x6, Pallas kernels, whole_call(): pl.pallas_call(body, grid=(1,) if first_rows else (), in_specs=[hbm if i...  79.2 us
    ppermute x34, starting transfers between devices, moved(): return lax.ppermute(value, 'fsdp', xor_pairs(k))  42.5 us
    ppermute x12, waiting for transfers between devices, shards(): lax.ppermute(v, 'replica', [(j, j ^ k) for j in range(4)])  38.3 us
    pallas_call x1, Pallas kernels, shards(): pl.pallas_call(kv_all_kernel, grid=(8,), in_specs=[x_spec, x_spec, step_f...  32.9 us
    unnamed x153, local copies, waits for them, and re-layouts  24.6 us
    all_gather x1, waiting for transfers between devices, shards(): later_all = lax.all_gather(later, 'fsdp', axis=0, tiled=False)  18.5 us
  transfers between devices with their start and end apart: 55, of which 32 were waited for; matrix products, arithmetic and copies ran while one was open for 9% of the time, Pallas kernels for 30%

profile of v5, /device:TPU:0, one launch (start us, length us, event | category | flops | bytes accessed | tf_op | source)
XLA Modules:
  0.0 657.4 jit_solution(8431728361437657018)
XLA Ops:
  20.0 21.6 %collective-permute-done.1 = bf16[384,1152]{1,0:T(8,128)(2,1)S(1)} collective-permute-done((bf16[384,1152]{1,0:T(8,128)(2,1)S(1)}, bf16[384,1152]{1,0:T(8,128)(2,1)S(1)}, u32[]{:S(2)}, u32[]{:S(2)}) %collective-permute-start.1) | collective-permute-done | bytes 884768 | tf_op jit(solution)/shard_map/ppermute | solution.py:38
  54.1 10.7 %collective-permute-done.3 = bf16[192,1152]{1,0:T(8,128)(2,1)S(1)} collective-permute-done((bf16[192,1152]{1,0:T(8,128)(2,1)S(1)}, bf16[192,1152]{1,0:T(8,128)(2,1)S(1)}, u32[]{:S(2)}, u32[]{:S(2)}) %collective-permute-start.3) | collective-permute-done | bytes 442400 | tf_op jit(solution)/shard_map/ppermute | solution.py:38
  69.0 18.5 %collective-permute-done.2 = bf16[384,1152]{1,0:T(8,128)(2,1)S(1)} collective-permute-done((bf16[384,1152]{1,0:T(8,128)(2,1)S(1)}, bf16[384,1152]{1,0:T(8,128)(2,1)S(1)}, u32[]{:S(2)}, u32[]{:S(2)}) %collective-permute-start.2) | collective-permute-done | bytes 884768 | tf_op jit(solution)/shard_map/ppermute | solution.py:38
  110.4 32.9 %shard_map.263 = (bf16[128,1152]{1,0:T(8,128)(2,1)S(1)}, bf16[8,2,128,1152]{3,2,1,0:T(8,128)(2,1)}, bf16[8,2,128,1152]{3,2,1,0:T(8,128)(2,1)}) custom-call(bf16[8,384,1152]{2,1,0:T(8,128)(2,1)} %bitcast_dynamic-update-slice_fusion.xn_ref.near_ref, bf16[8,384,1152]{2,1,0:T(8,128)(2,1)} %collective-permute-done.8.xf_ref.far_ref, ...), custom_call_target="tpu_custom_call" | custom-call | flops 14545846272 | bytes 28311552 | tf_op jit(solution)/shard_map/pallas_call | solution.py:583
  148.1 14.1 %shard_map.264 = (bf16[128,1152]{1,0:T(8,128)(2,1)S(1)}, f32[2,9,8,128]{3,2,1,0:T(8,128)}) custom-call(bf16[128,1152]{1,0:T(8,128)(2,1)S(1)} %get-tuple-element.65.q_ref, bf16[8,2,2,64,1152]{4,3,2,1,0:T(8,128)(2,1)S(1)} %bitcast.230, bf16[8,2,2,64,1152]{4,3,2,1,0:T(8,128)(2,1)S(1)} %bitcast.232, bf16[8,2,2,64,1152]{4,3,2,1,0:T(8,128)(2,1)S(1)} %bitcast.231, ...), custom_call_target="tpu_custom_call" | custom-call | flops 4831838208 | bytes 9437184 | tf_op jit(solution)/shard_map/pallas_call | solution.py:448
  162.9 18.5 %all-gather.9.cloned.1.call-done = bf16[10752,1088]{1,0:T(8,128)(2,1)} async-done(((bf16[672,1088]{1,0:T(8,128)(2,1)}), bf16[10752,1088]{1,0:T(8,128)(2,1)}) %all-gather.9.cloned.1.call-update) | async-done | bytes 23396368 | tf_op jit(solution)/shard_map/all_gather | solution.py:505
  181.5 12.1 %shard_map.265 = (f32[128,1088]{1,0:T(8,128)}, bf16[128,1088]{1,0:T(8,128)(2,1)}, f32[4,128,1088]{2,1,0:T(8,128)}, bf16[128,1088]{1,0:T(8,128)(2,1)}) custom-call(bf16[128,1152]{1,0:T(8,128)(2,1)} %copy-done.8, bf16[128,1088]{1,0:T(8,128)(2,1)} %bitcast.249, bf16[1088,1280]{1,0:T(8,128)(2,1)} %fusion.1.place_ref, f32[1,1088]{1,0:T(1,128)} %reshape.545.os_ref, ...), custom_call_target="tpu_custom_call" | custom-call | flops 4848615424 | bytes 23396352 | tf_op jit(solution)/shard_map/pallas_call | solution.py:433
  216.9 9.9 %collective-permute-done.11 = bf16[256,1152]{1,0:T(8,128)(2,1)S(1)} collective-permute-done((bf16[256,1152]{1,0:T(8,128)(2,1)}, bf16[256,1152]{1,0:T(8,128)(2,1)S(1)}, u32[]{:S(2)}, u32[]{:S(2)}) %collective-permute-start.11) | collective-permute-done | bytes 589856 | tf_op jit(solution)/shard_map/ppermute | solution.py:38
  258.3 13.2 %shard_map.267 = (bf16[128,1152]{1,0:T(8,128)(2,1)S(1)}, f32[2,9,8,128]{3,2,1,0:T(8,128)S(1)}) custom-call(bf16[128,1152]{1,0:T(8,128)(2,1)S(1)} %copy-done.7, bf16[8,2,2,64,1152]{4,3,2,1,0:T(8,128)(2,1)S(1)} %constant_dynamic-update-slice_fusion.6.kn_ref.vn_ref, bf16[8,2,2,64,1152]{4,3,2,1,0:T(8,128)(2,1)S(1)} %bitcast.224, ...), custom_call_target="tpu_custom_call" | custom-call | flops 4831838208 | bytes 9437184 | tf_op jit(solution)/shard_map/pallas_call | solution.py:448
  281.6 21.3 %shard_map.268 = (f32[128,1088]{1,0:T(8,128)}, bf16[128,1088]{1,0:T(8,128)(2,1)}, f32[4,128,1088]{2,1,0:T(8,128)}, bf16[128,1088]{1,0:T(8,128)(2,1)}, f32[128,10...) custom-call(bf16[128,1152]{1,0:T(8,128)(2,1)} %copy-done.6, ...), custom_call_target="tpu_custom_call" | custom-call | flops 4848615424 | bytes 23396352 | tf_op jit(solution)/shard_map/pallas_call | solution.py:433
  311.4 17.0 %shard_map.269.dq_ref = bf16[128,1152]{1,0:T(8,128)(2,1)} custom-call(bf16[128,1152]{1,0:T(8,128)(2,1)} %get-tuple-element.70.q_ref, bf16[128,1152]{1,0:T(8,128)(2,1)} %get-tuple-element.74.do_ref, f32[2,9,8,128]{3,2,1,0:T(8,128)} %copy-done.13, bf16[8,2,2,64,1152]{4,3,2,1,0:T(8,128)(2,1)} %copy-done.1, bf16[8,2,2,64,1152]{4,3,2,1,0:T(8,128)(2,1)} %bitcast.226, ...), custom_call_target="tpu_custom_call" | custom-call | flops 7247757312 | bytes 9437184 | tf_op jit(solution)/shard_map/pallas_call | solution.py:448
  339.9 9.9 %collective-permute-done.24 = bf16[128,1152]{1,0:T(8,128)(2,1)S(1)} collective-permute-done((bf16[128,1152]{1,0:T(8,128)(2,1)S(1)}, bf16[128,1152]{1,0:T(8,128)(2,1)S(1)}, u32[]{:S(2)}, u32[]{:S(2)}) %collective-permute-start.24) | collective-permute-done | bytes 294944 | tf_op jit(solution)/shard_map/ppermute | solution.py:38
  362.4 20.7 %shard_map.270 = (bf16[128,1152]{1,0:T(8,128)(2,1)}, bf16[128,1152]{1,0:T(8,128)(2,1)}) custom-call(s32[1]{0:T(128)} %bitcast.45.me_ref, bf16[256,1152]{1,0:T(8,128)(2,1)} %get-tuple-element.71.k_ref.v_ref, bf16[256,1152]{1,0:T(8,128)(2,1)} %get-tuple-element.71.k_ref.v_ref, bf16[16,272,1152]{2,1,0:T(8,128)(2,1)} %bitcast.238, ...), custom_call_target="tpu_custom_call" | custom-call | flops 12079595520 | bytes 9437184 | tf_op jit(solution)/shard_map/pallas_call | solution.py:448
  383.1 9.6 %shard_map.271 = (bf16[128,1088]{1,0:T(8,128)(2,1)}, f32[8,1088]{1,0:T(8,128)}) custom-call(bf16[128,1152]{1,0:T(8,128)(2,1)} %shard_map.269.dq_ref, bf16[128,1152]{1,0:T(8,128)(2,1)} %get-tuple-element.81.dk_ref, bf16[128,1152]{1,0:T(8,128)(2,1)} %get-tuple-element.82.dv_ref, bf16[8,384,1152]{2,1,0:T(8,128)(2,1)} %bitcast_dynamic-update-slice_fusion.xn_ref.near_ref, ...), custom_call_target="tpu_custom_call" | custom-call | flops 3636461568 | bytes 9437184 | tf_op jit(solution)/shard_map/pallas_call | solution.py:433
  394.3 11.1 %collective-permute-done.27 = bf16[128,1088]{1,0:T(8,128)(2,1)S(1)} collective-permute-done((bf16[128,1088]{1,0:T(8,128)(2,1)}, bf16[128,1088]{1,0:T(8,128)(2,1)S(1)}, u32[]{:S(2)}, u32[]{:S(2)}) %collective-permute-start.27) | collective-permute-done | bytes 278560 | tf_op jit(solution)/shard_map/ppermute | solution.py:677
  406.2 18.4 %shard_map.272 = (f32[128,1088]{1,0:T(8,128)}, bf16[128,1088]{1,0:T(8,128)(2,1)}, bf16[128,1152]{1,0:T(8,128)(2,1)}, f32[8,1088]{1,0:T(8,128)}) custom-call(bf16[128,1088]{1,0:T(8,128)(2,1)} %broadcast_select_fusion.1.go_ref, f32[4,128,1088]{2,1,0:T(8,128)} %get-tuple-element.85.pre_ref, f32[128,1088]{1,0:T(8,128)} %get-tuple-element.86.hidden_ref, ...), custom_call_target="tpu_custom_call" | custom-call | flops 4848615424 | bytes 23396352 | tf_op jit(solution)/shard_map/pallas_call | solution.py:433
  430.6 17.3 %shard_map.273.dq_ref = bf16[128,1152]{1,0:T(8,128)(2,1)} custom-call(bf16[128,1152]{1,0:T(8,128)(2,1)} %get-tuple-element.70.q_ref, bf16[128,1152]{1,0:T(8,128)(2,1)} %get-tuple-element.87.do_ref, f32[2,9,8,128]{3,2,1,0:T(8,128)} %copy-done.13, bf16[8,2,2,64,1152]{4,3,2,1,0:T(8,128)(2,1)} %copy-done.1, bf16[8,2,2,64,1152]{4,3,2,1,0:T(8,128)(2,1)} %bitcast.228, ...), custom_call_target="tpu_custom_call" | custom-call | flops 7247757312 | bytes 9437184 | tf_op jit(solution)/shard_map/pallas_call | solution.py:448
  466.4 20.9 %shard_map.274 = (bf16[128,1152]{1,0:T(8,128)(2,1)}, bf16[128,1152]{1,0:T(8,128)(2,1)}) custom-call(s32[1]{0:T(128)} %bitcast.45.me_ref, bf16[256,1152]{1,0:T(8,128)(2,1)} %get-tuple-element.71.k_ref.v_ref, bf16[256,1152]{1,0:T(8,128)(2,1)} %get-tuple-element.71.k_ref.v_ref, bf16[16,272,1152]{2,1,0:T(8,128)(2,1)} %bitcast.241, ...), custom_call_target="tpu_custom_call" | custom-call | flops 12079595520 | bytes 9437184 | tf_op jit(solution)/shard_map/pallas_call | solution.py:448
  496.9 9.6 %shard_map.275 = (bf16[128,1088]{1,0:T(8,128)(2,1)}, f32[8,1088]{1,0:T(8,128)}) custom-call(bf16[128,1152]{1,0:T(8,128)(2,1)} %shard_map.273.dq_ref, bf16[128,1152]{1,0:T(8,128)(2,1)} %get-tuple-element.93.dk_ref, bf16[128,1152]{1,0:T(8,128)(2,1)} %get-tuple-element.94.dv_ref, bf16[8,384,1152]{2,1,0:T(8,128)(2,1)} %bitcast_dynamic-update-slice_fusion.xn_ref.near_ref, ...), custom_call_target="tpu_custom_call" | custom-call | flops 3636461568 | bytes 9437184 | tf_op jit(solution)/shard_map/pallas_call | solution.py:433
  515.6 14.6 %shard_map.276 = (f32[272,1088]{1,0:T(8,128)}, f32[1088,272]{1,0:T(8,128)}, f32[8,272]{1,0:T(8,128)}, f32[8,1088]{1,0:T(8,128)}) custom-call(bf16[16,256,1088]{2,1,0:T(8,128)(2,1)} %bitcast.245, bf16[16,128,1088]{2,1,0:T(8,128)(2,1)} %bitcast.311, bf16[1088,272]{1,0:T(8,128)(2,1)} %reshape.557.fc_ref, f32[1,272]{1,0:T(1,128)} %get-tuple-element.210.fb_ref, ...), custom_call_target="tpu_custom_call" | custom-call | flops 19394461696 | bytes 13369344 | tf_op jit(solution)/shard_map/pallas_call | solution.py:694
  531.7 9.4 %shard_map.277 = (f32[1088,272]{1,0:T(8,128)}, f32[8,272]{1,0:T(8,128)}) custom-call(s32[1]{0:T(128)} %bitcast.45.me_ref, bf16[16,256,1088]{2,1,0:T(8,128)(2,1)} %bitcast.246, bf16[16,272,1152]{2,1,0:T(8,128)(2,1)} %bitcast.244, bf16[16,128,272]{2,1,0:T(8,128)(2,1)} %copy.84.cols_ref), custom_call_target="tpu_custom_call" | custom-call | flops 4848615424 | bytes 17825792 | tf_op jit(solution)/shard_map/pallas_call | solution.py:709
  553.7 11.0 %all-to-all-done.1 = bf16[16,72,384]{2,1,0:T(8,128)(2,1)S(1)} async-done(((bf16[16,72,384]{2,1,0:T(8,128)(2,1)}), bf16[16,72,384]{2,1,0:T(8,128)(2,1)S(1)}, u32[]{:S(2)}, u32[]{:S(2)}) %all-to-all-start.1) | async-done | bytes 884768 | tf_op jit(solution)/shard_map/all_to_all | solution.py:723
  577.7 9.5 %collective-permute-done.38 = bf16[7,72,384]{2,1,0:T(8,128)(2,1)S(1)} collective-permute-done((bf16[7,72,384]{2,1,0:T(8,128)(2,1)}, bf16[7,72,384]{2,1,0:T(8,128)(2,1)S(1)}, u32[]{:S(2)}, u32[]{:S(2)}) %collective-permute-start.38) | collective-permute-done | bytes 387104 | tf_op jit(solution)/shard_map/ppermute | solution.py:725
  607.8 18.9 %collective-permute-done.40 = bf16[4,72,384]{2,1,0:T(8,128)(2,1)S(1)} collective-permute-done((bf16[4,72,384]{2,1,0:T(8,128)(2,1)S(1)}, bf16[4,72,384]{2,1,0:T(8,128)(2,1)S(1)}, u32[]{:S(2)}, u32[]{:S(2)}) %collective-permute-start.40) | collective-permute-done | bytes 221216 | tf_op jit(solution)/shard_map/ppermute | solution.py:725
  (399 shorter events, 271.0 us)
Async XLA Ops:
  7.2 174.3 %all-gather.9.cloned.1.call-start = ((), (), s32[]{:S(2)}) async-start(), calls=%async_computation.3 | async-start | bytes 26320896 | tf_op jit(solution)/shard_map/all_gather | solution.py:505
  10.2 352.1 %all-gather.11.cloned.1.call-start = ((), (), s32[]{:S(2)}) async-start(), calls=%async_computation.4 | async-start | bytes 10653696 | tf_op jit(solution)/shard_map/all_gather | solution.py:626
  12.1 29.5 %collective-permute-start.1 = (bf16[384,1152]{1,0:T(8,128)(2,1)S(1)}, bf16[384,1152]{1,0:T(8,128)(2,1)S(1)}, u32[]{:S(2)}, u32[]{:S(2)}) collective-permute-start(bf16[384,1152]{1,0:T(8,128)(2,1)S(1)} %pad_dynamic-update-slice_fusion), channel_id=1, source_target_pairs={{0,16},{4,20},{8,24},{12,28},{16,0},{20,4},{24,8},{28,12},{32,48},... | collective-permute-start | bytes 2654216 | tf_op jit(solution)/shard_map/ppermute | solution.py:38
  13.9 32.3 %collective-permute-start.4 = (bf16[384,1152]{1,0:T(8,128)(2,1)S(1)}, bf16[384,1152]{1,0:T(8,128)(2,1)S(1)}, u32[]{:S(2)}, u32[]{:S(2)}) collective-permute-start(bf16[384,1152]{1,0:T(8,128)(2,1)S(1)} %pad_dynamic-update-slice_fusion), channel_id=1, source_target_pairs={{0,48},{4,52},{8,56},{12,60},{16,32},{20,36},{24,40},{28,44},{32,1... | collective-permute-start | bytes 2654216 | tf_op jit(solution)/shard_map/ppermute | solution.py:38
  16.1 36.0 %collective-permute-start = (bf16[384,1152]{1,0:T(8,128)(2,1)S(1)}, bf16[384,1152]{1,0:T(8,128)(2,1)S(1)}, u32[]{:S(2)}, u32[]{:S(2)}) collective-permute-start(bf16[384,1152]{1,0:T(8,128)(2,1)S(1)} %pad_dynamic-update-slice_fusion), channel_id=1, source_target_pairs={{0,8},{4,12},{8,0},{12,4},{16,24},{20,28},{24,16},{28,20},{32,40},... | collective-permute-start | bytes 2654216 | tf_op jit(solution)/shard_map/ppermute | solution.py:38
  41.7 23.1 %collective-permute-start.3 = (bf16[192,1152]{1,0:T(8,128)(2,1)S(1)}, bf16[192,1152]{1,0:T(8,128)(2,1)S(1)}, u32[]{:S(2)}, u32[]{:S(2)}) collective-permute-start(bf16[192,1152]{1,0:T(8,128)(2,1)S(1)} %slice.242), channel_id=1, source_target_pairs={{0,48},{4,52},{8,56},{12,60},{16,32},{20,36},{24,40},{28,44},{32,1... | collective-permute-start | bytes 1327112 | tf_op jit(solution)/shard_map/ppermute | solution.py:38
  52.0 35.4 %collective-permute-start.2 = (bf16[384,1152]{1,0:T(8,128)(2,1)S(1)}, bf16[384,1152]{1,0:T(8,128)(2,1)S(1)}, u32[]{:S(2)}, u32[]{:S(2)}) collective-permute-start(bf16[384,1152]{1,0:T(8,128)(2,1)S(1)} %collective-permute-done), channel_id=1, source_target_pairs={{0,16},{4,20},{8,24},{12,28},{16,0},{20,4},{24,8},{28,12},{32,48},... | collective-permute-start | bytes 2654216 | tf_op jit(solution)/shard_map/ppermute | solution.py:38
  52.1 39.5 %collective-permute-start.7 = (bf16[384,1152]{1,0:T(8,128)(2,1)S(1)}, bf16[384,1152]{1,0:T(8,128)(2,1)S(1)}, u32[]{:S(2)}, u32[]{:S(2)}) collective-permute-start(bf16[384,1152]{1,0:T(8,128)(2,1)S(1)} %collective-permute-done), channel_id=1, source_target_pairs={{0,48},{4,52},{8,56},{12,60},{16,32},{20,36},{24,40},{28,44},{32,1... | collective-permute-start | bytes 2654216 | tf_op jit(solution)/shard_map/ppermute | solution.py:38
  66.5 23.0 %collective-permute-start.6 = (bf16[384,1152]{1,0:T(8,128)(2,1)S(1)}, bf16[384,1152]{1,0:T(8,128)(2,1)S(1)}, u32[]{:S(2)}, u32[]{:S(2)}) collective-permute-start(bf16[384,1152]{1,0:T(8,128)(2,1)S(1)} %constant_dynamic-update-slice_fusion.1), channel_id=1, source_target_pairs={{0,8},{4,12},{8,0},{12,4},{16,24},{20,28},{24,16},{28,20},{32,40},... | collective-permute-start | bytes 2654216 | tf_op jit(solution)/shard_map/ppermute | solution.py:38
  272.8 234.5 %all-gather.13.cloned.1.call-start = ((), (), s32[]{:S(2)}) async-start(), calls=%async_computation.5 | async-start | bytes 10027008 | tf_op jit(solution)/shard_map/all_gather | solution.py:629
  305.0 210.6 %all-gather.15.cloned.1.call-start = ((), (), s32[]{:S(2)}) async-start(), calls=%async_computation.6 | async-start | bytes 5013504 | tf_op jit(solution)/shard_map/all_gather | solution.py:679
  305.1 23.4 %collective-permute-start.19 = (bf16[128,1152]{1,0:T(8,128)(2,1)}, bf16[128,1152]{1,0:T(8,128)(2,1)S(1)}, u32[]{:S(2)}, u32[]{:S(2)}) collective-permute-start(bf16[128,1152]{1,0:T(8,128)(2,1)} %get-tuple-element.74.do_ref), channel_id=1, source_target_pairs={{0,16},{4,20},{8,24},{12,28},{16,0},{20,4},{24,8},{28,12},{32,48},... | collective-permute-start | bytes 884744 | tf_op jit(solution)/shard_map/ppermute | solution.py:38
  305.3 23.2 %collective-permute-start.20 = (bf16[128,1152]{1,0:T(8,128)(2,1)}, bf16[128,1152]{1,0:T(8,128)(2,1)S(1)}, u32[]{:S(2)}, u32[]{:S(2)}) collective-permute-start(bf16[128,1152]{1,0:T(8,128)(2,1)} %get-tuple-element.74.do_ref), channel_id=1, source_target_pairs={{0,48},{4,52},{8,56},{12,60},{16,32},{20,36},{24,40},{28,44},{32,1... | collective-permute-start | bytes 884744 | tf_op jit(solution)/shard_map/ppermute | solution.py:38
  309.6 21.9 %collective-permute-start.22 = (bf16[128,1152]{1,0:T(8,128)(2,1)}, bf16[128,1152]{1,0:T(8,128)(2,1)S(1)}, u32[]{:S(2)}, u32[]{:S(2)}) collective-permute-start(bf16[128,1152]{1,0:T(8,128)(2,1)} %get-tuple-element.74.do_ref), channel_id=1, source_target_pairs={{0,32},{4,36},{8,40},{12,44},{16,48},{20,52},{24,56},{28,60},{32,0... | collective-permute-start | bytes 884744 | tf_op jit(solution)/shard_map/ppermute | solution.py:38
  424.6 24.1 %collective-permute-start.28 = (bf16[128,1152]{1,0:T(8,128)(2,1)}, bf16[128,1152]{1,0:T(8,128)(2,1)S(1)}, u32[]{:S(2)}, u32[]{:S(2)}) collective-permute-start(bf16[128,1152]{1,0:T(8,128)(2,1)} %get-tuple-element.87.do_ref), channel_id=1, source_target_pairs={{0,16},{4,20},{8,24},{12,28},{16,0},{20,4},{24,8},{28,12},{32,48},... | collective-permute-start | bytes 884744 | tf_op jit(solution)/shard_map/ppermute | solution.py:38
  424.7 24.0 %collective-permute-start.29 = (bf16[128,1152]{1,0:T(8,128)(2,1)}, bf16[128,1152]{1,0:T(8,128)(2,1)S(1)}, u32[]{:S(2)}, u32[]{:S(2)}) collective-permute-start(bf16[128,1152]{1,0:T(8,128)(2,1)} %get-tuple-element.87.do_ref), channel_id=1, source_target_pairs={{0,48},{4,52},{8,56},{12,60},{16,32},{20,36},{24,40},{28,44},{32,1... | collective-permute-start | bytes 884744 | tf_op jit(solution)/shard_map/ppermute | solution.py:38
  425.5 23.2 %collective-permute-start.30 = (bf16[128,1152]{1,0:T(8,128)(2,1)}, bf16[128,1152]{1,0:T(8,128)(2,1)S(1)}, u32[]{:S(2)}, u32[]{:S(2)}) collective-permute-start(bf16[128,1152]{1,0:T(8,128)(2,1)} %get-tuple-element.87.do_ref), channel_id=1, source_target_pairs={{0,8},{4,12},{8,0},{12,4},{16,24},{20,28},{24,16},{28,20},{32,40},... | collective-permute-start | bytes 884744 | tf_op jit(solution)/shard_map/ppermute | solution.py:38
  491.2 39.0 %all-to-all-start = ((bf16[16,128,272]{1,2,0:T(8,128)(2,1)}), bf16[16,128,272]{1,2,0:T(8,128)(2,1)S(1)}, u32[]{:S(2)}, u32[]{:S(2)}) async-start(bf16[16,128,272]{1,2,0:T(8,128)(2,1)} %bitcast.84), calls=%async_computation | async-start | bytes 2228224 | tf_op jit(solution)/shard_map/all_to_all | solution.py:705
  542.4 22.3 %all-to-all-start.1 = ((bf16[16,72,384]{2,1,0:T(8,128)(2,1)}), bf16[16,72,384]{2,1,0:T(8,128)(2,1)S(1)}, u32[]{:S(2)}, u32[]{:S(2)}) async-start(bf16[16,72,384]{2,1,0:T(8,128)(2,1)} %pad.74), calls=%async_computation.1 | async-start | bytes 1769472 | tf_op jit(solution)/shard_map/all_to_all | solution.py:723
  567.7 28.6 %all-to-all-start.2 = ((bf16[16,72,384]{2,1,0:T(8,128)(2,1)}), bf16[16,72,384]{2,1,0:T(8,128)(2,1)S(1)}, u32[]{:S(2)}, u32[]{:S(2)}) async-start(bf16[16,72,384]{2,1,0:T(8,128)(2,1)} %fusion.8), calls=%async_computation.2 | async-start | bytes 1769472 | tf_op jit(solution)/shard_map/all_to_all | solution.py:723
  598.4 32.7 %collective-permute-start.47 = (bf16[7,72,384]{2,1,0:T(8,128)(2,1)S(1)}, bf16[7,72,384]{2,1,0:T(8,128)(2,1)S(1)}, u32[]{:S(2)}, u32[]{:S(2)}) collective-permute-start(bf16[7,72,384]{2,1,0:T(8,128)(2,1)S(1)} %fusion.12), channel_id=1, source_target_pairs={{0,3},{1,2},{2,1},{3,0},{4,7},{5,6},{6,5},{7,4},{8,11},{9,10},{10,... | collective-permute-start | bytes 1161224 | tf_op jit(solution)/shard_map/ppermute | solution.py:725
  600.4 31.5 %collective-permute-start.46 = (bf16[7,72,384]{2,1,0:T(8,128)(2,1)S(1)}, bf16[7,72,384]{2,1,0:T(8,128)(2,1)S(1)}, u32[]{:S(2)}, u32[]{:S(2)}) collective-permute-start(bf16[7,72,384]{2,1,0:T(8,128)(2,1)S(1)} %fusion.12), channel_id=1, source_target_pairs={{0,2},{1,3},{2,0},{3,1},{4,6},{5,7},{6,4},{7,5},{8,10},{9,11},{10,... | collective-permute-start | bytes 1161224 | tf_op jit(solution)/shard_map/ppermute | solution.py:725
  601.9 30.0 %collective-permute-start.45 = (bf16[7,72,384]{2,1,0:T(8,128)(2,1)S(1)}, bf16[7,72,384]{2,1,0:T(8,128)(2,1)S(1)}, u32[]{:S(2)}, u32[]{:S(2)}) collective-permute-start(bf16[7,72,384]{2,1,0:T(8,128)(2,1)S(1)} %fusion.12), channel_id=1, source_target_pairs={{0,1},{1,0},{2,3},{3,2},{4,5},{5,4},{6,7},{7,6},{8,9},{9,8},{10,11... | collective-permute-start | bytes 1161224 | tf_op jit(solution)/shard_map/ppermute | solution.py:725
  602.5 24.2 %collective-permute-start.40 = (bf16[4,72,384]{2,1,0:T(8,128)(2,1)S(1)}, bf16[4,72,384]{2,1,0:T(8,128)(2,1)S(1)}, u32[]{:S(2)}, u32[]{:S(2)}) collective-permute-start(bf16[4,72,384]{2,1,0:T(8,128)(2,1)S(1)} %get-tuple-element.186), channel_id=1, source_target_pairs={{0,3},{1,2},{2,1},{3,0},{4,7},{5,6},{6,5},{7,4},{8,11},{9,10},{10,... | collective-permute-start | bytes 663560 | tf_op jit(solution)/shard_map/ppermute | solution.py:725
  (76 other events, 1077.7 us)
Sparse Core Ops, SparseCore 0:
  10.5 170.9 all-gather.8
  272.9 89.4 all-gather.10
  364.8 85.0 all-gather.12
  452.2 63.3 all-gather.14

commit v6 on v4

--- a/solution.py
+++ b/solution.py
@@ -43,10 +43,12 @@
     blocks = {0: x, 4: moved(x, 4), 12: moved(x, 12), 2: moved(x, 2)}
     result = None
     if beside is not None:
-        blocks[4], blocks[12], blocks[2], result = lax.optimization_barrier(
-            (blocks[4], blocks[12], blocks[2], beside())
-        )
-    blocks[8] = jnp.concatenate([moved(blocks[4][:half], 12), moved(blocks[12][half:], 4)], 0)
+        blocks[8] = moved(x, 8)
+        first = (4, 12, 2, 8)
+        *arrived, result = lax.optimization_barrier((*[blocks[k] for k in first], beside()))
+        blocks.update(zip(first, arrived))
+    else:
+        blocks[8] = jnp.concatenate([moved(blocks[4][:half], 12), moved(blocks[12][half:], 4)], 0)
     blocks[6] = moved(blocks[2], 4)
     blocks[14] = moved(blocks[2], 12)
     blocks[10] = moved(blocks[8], 2)
@@ -606,8 +608,10 @@
         first_rows=(1, 2),
         **qkv_cost,
     )
+    q_all = lax.all_gather(queries, "fsdp", axis=0)
     kv_near, kv_far = [by_kind(b) for b in gather_both(keys_values)]
     attended, log_total = attention(queries, kv_near, kv_far)
+    attended, q_all = lax.optimization_barrier((attended, q_all))
     hidden, normed_two, pre_act, out_low, *first_back = whole_call(
         ffn_both_kernel,
         ffn_shapes + back_shapes,
@@ -621,8 +625,8 @@
     part_two = lax.reduce_precision(lse_own - part_one, 8, 7)
     part_three = lse_own - part_one - part_two
     lse_rows = jnp.stack([part_one, part_two, part_three]).astype(bf16).reshape(6, LANES)
-    qa_all = lax.all_gather(
-        jnp.concatenate([queries, attended, lse_rows, jnp.zeros((10, LANES), bf16)], 0), "fsdp", axis=0
+    att_all = lax.all_gather(
+        jnp.concatenate([attended, lse_rows, jnp.zeros((10, LANES), bf16)], 0), "fsdp", axis=0
     )
     nn_all = lax.all_gather(jnp.concatenate([normed_one, normed_two], 0), "fsdp", axis=0)
 
@@ -649,14 +653,14 @@
                 own_half(0),
                 own_half(1),
                 pl.BlockSpec((SHARDS, span, 128), lambda m, h: (0, m, h)),
-                pl.BlockSpec((SHARDS, span, 128), lambda m, h: (0, 2 + m, h)),
-                pl.BlockSpec((SHARDS, 16, 128), lambda m, h: (0, 16, h)),
+                pl.BlockSpec((SHARDS, span, 128), lambda m, h: (0, m, h)),
+                pl.BlockSpec((SHARDS, 16, 128), lambda m, h: (0, 8, h)),
             ]
             + [all_spec(0, span), all_spec(0, span), bias_spec],
             [own_spec(span), own_spec(span)],
             [token_shape, token_shape],
             (
-                me_scalar, keys_values, keys_values, qa_all, qa_all, qa_all, do_near, do_far, column_bias,
+                me_scalar, keys_values, keys_values, q_all, att_all, att_all, do_near, do_far, column_bias,
             ),
             vmem=60,
         )
@@ -704,11 +708,11 @@
     grad_columns, column_sums = pl.pallas_call(
         columns_kernel,
         grid=(8,),
-        in_specs=[pl.BlockSpec(memory_space=pltpu.SMEM), chip(0, D), chip(1, LANES), chip(0, FROWS)],
+        in_specs=[pl.BlockSpec(memory_space=pltpu.SMEM), chip(0, D), chip(0, LANES), chip(0, FROWS)],
         out_specs=[fixed(D, FROWS), fixed(8, FROWS)],
         out_shape=[shape(D, FROWS, dtype=f32), shape(8, FROWS, dtype=f32)],
         **params(4 * 2 * SHARDS * tokens * D * FROWS, 4 * 2 * SHARDS * tokens * D, vmem=60),
-    )(me_scalar, nn_all, qa_all, columns)
+    )(me_scalar, nn_all, att_all, columns)
 
     width, height = 384, 72
     z = lax.axis_index("replica")

time: 650 us -> 656 us (level)
  waiting for transfers between devices: 209 us -> 216 us
    all_gather x1, waiting for transfers between devices: 0.02 us -> 18.6 us  [shards(): go_all = lax.all_gather(grad_out, 'fsdp', axis=0)]
    ppermute x36 -> x34, waiting for transfers between devices: 135 us -> 121 us  [moved(): return lax.ppermute(value, 'fsdp', xor_pairs(k))]
    unnamed x159 -> x167, local copies, waits for them, and re-layouts: 35.8 us -> 36.5 us
    ppermute x36 -> x34, starting transfers between devices: 43.6 us -> 43.1 us  [moved(): return lax.ppermute(value, 'fsdp', xor_pairs(k))]
  transfers between devices with their start and end apart: 57 -> 56, of which waited for: 36 -> 34; matrix products, arithmetic and copies ran while one was open for 9% -> 9% of each run, Pallas kernels for 31% -> 32%
where the time goes in v6:
time: 656 us; the launch traced here: 650 us
  Pallas kernels  230 us (35%)
  waiting for transfers between devices  216 us (33%)
  starting transfers between devices  87.6 us (13%)
  local copies, waits for them, and re-layouts  78.6 us (12%)
  other arithmetic  21.6 us (3%)
  between operations  15.7 us (2%)
    ppermute x34, waiting for transfers between devices, moved(): return lax.ppermute(value, 'fsdp', xor_pairs(k))  121 us
    pallas_call x6, Pallas kernels, pair_call(): pl.pallas_call(body, grid=(2, PAIRS), in_specs=in_specs, out_specs=out_sp...  94 us
    pallas_call x6, Pallas kernels, whole_call(): pl.pallas_call(body, grid=(1,) if first_rows else (), in_specs=[hbm if i...  79.4 us
    ppermute x34, starting transfers between devices, moved(): return lax.ppermute(value, 'fsdp', xor_pairs(k))  43.1 us
    unnamed x167, local copies, waits for them, and re-layouts  36.5 us
    pallas_call x1, Pallas kernels, shards(): pl.pallas_call(kv_all_kernel, grid=(8,), in_specs=[x_spec, x_spec, step_f...  32.9 us
    ppermute x12, waiting for transfers between devices, over_replicas(): lax.ppermute(v, 'replica', [(j, j ^ k) for j in range(4)])  26.3 us
    all_gather x1, waiting for transfers between devices, shards(): go_all = lax.all_gather(grad_out, 'fsdp', axis=0)  18.6 us
  transfers between devices with their start and end apart: 56, of which 34 were waited for; matrix products, arithmetic and copies ran while one was open for 9% of the time, Pallas kernels for 32%

profile of v6, /device:TPU:0, one launch (start us, length us, event | category | flops | bytes accessed | tf_op | source)
XLA Modules:
  0.0 649.7 jit_solution(4228351325304876595)
XLA Ops:
  20.0 21.4 %collective-permute-done.1 = bf16[384,1152]{1,0:T(8,128)(2,1)S(1)} collective-permute-done((bf16[384,1152]{1,0:T(8,128)(2,1)S(1)}, bf16[384,1152]{1,0:T(8,128)(2,1)S(1)}, u32[]{:S(2)}, u32[]{:S(2)}) %collective-permute-start.1) | collective-permute-done | bytes 884768 | tf_op jit(solution)/shard_map/ppermute | solution.py:38
  53.9 10.8 %collective-permute-done.3 = bf16[192,1152]{1,0:T(8,128)(2,1)S(1)} collective-permute-done((bf16[192,1152]{1,0:T(8,128)(2,1)S(1)}, bf16[192,1152]{1,0:T(8,128)(2,1)S(1)}, u32[]{:S(2)}, u32[]{:S(2)}) %collective-permute-start.3) | collective-permute-done | bytes 442400 | tf_op jit(solution)/shard_map/ppermute | solution.py:38
  68.7 18.6 %collective-permute-done.2 = bf16[384,1152]{1,0:T(8,128)(2,1)S(1)} collective-permute-done((bf16[384,1152]{1,0:T(8,128)(2,1)S(1)}, bf16[384,1152]{1,0:T(8,128)(2,1)S(1)}, u32[]{:S(2)}, u32[]{:S(2)}) %collective-permute-start.2) | collective-permute-done | bytes 884768 | tf_op jit(solution)/shard_map/ppermute | solution.py:38
  110.3 32.9 %shard_map.263 = (bf16[128,1152]{1,0:T(8,128)(2,1)S(1)}, bf16[8,2,128,1152]{3,2,1,0:T(8,128)(2,1)}, bf16[8,2,128,1152]{3,2,1,0:T(8,128)(2,1)}) custom-call(bf16[8,384,1152]{2,1,0:T(8,128)(2,1)} %bitcast_dynamic-update-slice_fusion.xn_ref.near_ref, bf16[8,384,1152]{2,1,0:T(8,128)(2,1)} %collective-permute-done.8.xf_ref.far_ref, ...), custom_call_target="tpu_custom_call" | custom-call | flops 14545846272 | bytes 28311552 | tf_op jit(solution)/shard_map/pallas_call | solution.py:583
  148.0 14.1 %shard_map.264 = (bf16[128,1152]{1,0:T(8,128)(2,1)S(1)}, f32[2,9,8,128]{3,2,1,0:T(8,128)}) custom-call(bf16[128,1152]{1,0:T(8,128)(2,1)S(1)} %get-tuple-element.66.q_ref, bf16[8,2,2,64,1152]{4,3,2,1,0:T(8,128)(2,1)S(1)} %bitcast.229, bf16[8,2,2,64,1152]{4,3,2,1,0:T(8,128)(2,1)S(1)} %bitcast.231, bf16[8,2,2,64,1152]{4,3,2,1,0:T(8,128)(2,1)S(1)} %bitcast.230, ...), custom_call_target="tpu_custom_call" | custom-call | flops 4831838208 | bytes 9437184 | tf_op jit(solution)/shard_map/pallas_call | solution.py:448
  162.8 18.6 %all-gather.11.cloned.1.call-done = bf16[10752,1088]{1,0:T(8,128)(2,1)} async-done(((bf16[672,1088]{1,0:T(8,128)(2,1)}), bf16[10752,1088]{1,0:T(8,128)(2,1)}) %all-gather.11.cloned.1.call-update) | async-done | bytes 23396368 | tf_op jit(solution)/shard_map/all_gather | solution.py:505
  181.4 12.1 %shard_map.265 = (f32[128,1088]{1,0:T(8,128)}, bf16[128,1088]{1,0:T(8,128)(2,1)}, f32[4,128,1088]{2,1,0:T(8,128)}, bf16[128,1088]{1,0:T(8,128)(2,1)}) custom-call(bf16[128,1152]{1,0:T(8,128)(2,1)} %copy-done.15, bf16[128,1088]{1,0:T(8,128)(2,1)} %bitcast.242, bf16[1088,1280]{1,0:T(8,128)(2,1)} %fusion.1.place_ref, f32[1,1088]{1,0:T(1,128)} %reshape.547.os_ref, ...), custom_call_target="tpu_custom_call" | custom-call | flops 4848615424 | bytes 23396352 | tf_op jit(solution)/shard_map/pallas_call | solution.py:433
  216.9 9.9 %collective-permute-done.11 = bf16[256,1152]{1,0:T(8,128)(2,1)S(1)} collective-permute-done((bf16[256,1152]{1,0:T(8,128)(2,1)}, bf16[256,1152]{1,0:T(8,128)(2,1)S(1)}, u32[]{:S(2)}, u32[]{:S(2)}) %collective-permute-start.11) | collective-permute-done | bytes 589856 | tf_op jit(solution)/shard_map/ppermute | solution.py:38
  244.8 9.5 %collective-permute-done.12 = bf16[256,1152]{1,0:T(8,128)(2,1)S(1)} collective-permute-done((bf16[256,1152]{1,0:T(8,128)(2,1)}, bf16[256,1152]{1,0:T(8,128)(2,1)S(1)}, u32[]{:S(2)}, u32[]{:S(2)}) %collective-permute-start.12) | collective-permute-done | bytes 589856 | tf_op jit(solution)/shard_map/ppermute | solution.py:38
  266.5 13.2 %shard_map.267 = (bf16[128,1152]{1,0:T(8,128)(2,1)S(1)}, f32[2,9,8,128]{3,2,1,0:T(8,128)S(1)}) custom-call(bf16[128,1152]{1,0:T(8,128)(2,1)S(1)} %copy-done.13, bf16[8,2,2,64,1152]{4,3,2,1,0:T(8,128)(2,1)S(1)} %constant_dynamic-update-slice_fusion.6.kn_ref.vn_ref, bf16[8,2,2,64,1152]{4,3,2,1,0:T(8,128)(2,1)S(1)} %bitcast.223, ...), custom_call_target="tpu_custom_call" | custom-call | flops 4831838208 | bytes 9437184 | tf_op jit(solution)/shard_map/pallas_call | solution.py:448
  280.8 8.8 %all-gather.17.cloned.1.call-start = ((), (), s32[]{:S(2)}) async-start(), calls=%async_computation.6 | async-start | bytes 10027008 | tf_op jit(solution)/shard_map/all_gather | solution.py:631
  289.6 21.4 %shard_map.268 = (f32[128,1088]{1,0:T(8,128)}, bf16[128,1088]{1,0:T(8,128)(2,1)}, f32[4,128,1088]{2,1,0:T(8,128)}, bf16[128,1088]{1,0:T(8,128)(2,1)}, f32[128,10...) custom-call(bf16[128,1152]{1,0:T(8,128)(2,1)} %copy-done.8, ...), custom_call_target="tpu_custom_call" | custom-call | flops 4848615424 | bytes 23396352 | tf_op jit(solution)/shard_map/pallas_call | solution.py:433
  325.0 12.5 %shard_map.269.dq_ref = bf16[128,1152]{1,0:T(8,128)(2,1)S(1)} custom-call(bf16[128,1152]{1,0:T(8,128)(2,1)S(1)} %copy-done.13, bf16[128,1152]{1,0:T(8,128)(2,1)S(1)} %copy-done.11, f32[2,9,8,128]{3,2,1,0:T(8,128)S(1)} %get-tuple-element.77.lse_ref, bf16[8,2,2,64,1152]{4,3,2,1,0:T(8,128)(2,1)S(1)} %copy-done.2, bf16[8,2,2,64,1152]{4,3,2,1,0:T(8,128)(2,1)S(1)} %bitcast.225, ...), custom_call_target="tpu_custom_call" | custom-call | flops 7247757312 | bytes 9437184 | tf_op jit(solution)/shard_map/pallas_call | solution.py:448
  356.0 20.8 %shard_map.270 = (bf16[128,1152]{1,0:T(8,128)(2,1)}, bf16[128,1152]{1,0:T(8,128)(2,1)}) custom-call(s32[1]{0:T(128)} %bitcast.46.me_ref, bf16[256,1152]{1,0:T(8,128)(2,1)} %get-tuple-element.72.k_ref.v_ref, bf16[256,1152]{1,0:T(8,128)(2,1)} %get-tuple-element.72.k_ref.v_ref, bf16[16,128,1152]{2,1,0:T(8,128)(2,1)} %bitcast.307, ...), custom_call_target="tpu_custom_call" | custom-call | flops 12079595520 | bytes 9437184 | tf_op jit(solution)/shard_map/pallas_call | solution.py:448
  376.8 9.6 %shard_map.271 = (bf16[128,1088]{1,0:T(8,128)(2,1)}, f32[8,1088]{1,0:T(8,128)}) custom-call(bf16[128,1152]{1,0:T(8,128)(2,1)} %copy-done.14, bf16[128,1152]{1,0:T(8,128)(2,1)} %get-tuple-element.84.dk_ref, bf16[128,1152]{1,0:T(8,128)(2,1)} %get-tuple-element.85.dv_ref, bf16[8,384,1152]{2,1,0:T(8,128)(2,1)} %bitcast_dynamic-update-slice_fusion.xn_ref.near_ref, ...), custom_call_target="tpu_custom_call" | custom-call | flops 3636461568 | bytes 9437184 | tf_op jit(solution)/shard_map/pallas_call | solution.py:433
  388.1 17.6 %collective-permute-done.27 = bf16[128,1088]{1,0:T(8,128)(2,1)S(1)} collective-permute-done((bf16[128,1088]{1,0:T(8,128)(2,1)}, bf16[128,1088]{1,0:T(8,128)(2,1)S(1)}, u32[]{:S(2)}, u32[]{:S(2)}) %collective-permute-start.27) | collective-permute-done | bytes 278560 | tf_op jit(solution)/shard_map/ppermute | solution.py:678
  406.5 18.8 %shard_map.272 = (f32[128,1088]{1,0:T(8,128)}, bf16[128,1088]{1,0:T(8,128)(2,1)}, bf16[128,1152]{1,0:T(8,128)(2,1)}, f32[8,1088]{1,0:T(8,128)}) custom-call(bf16[128,1088]{1,0:T(8,128)(2,1)} %broadcast_select_fusion.1.go_ref, f32[4,128,1088]{2,1,0:T(8,128)} %get-tuple-element.88.pre_ref, f32[128,1088]{1,0:T(8,128)} %get-tuple-element.89.hidden_ref, ...), custom_call_target="tpu_custom_call" | custom-call | flops 4848615424 | bytes 23396352 | tf_op jit(solution)/shard_map/pallas_call | solution.py:433
  435.3 12.5 %shard_map.273.dq_ref = bf16[128,1152]{1,0:T(8,128)(2,1)S(1)} custom-call(bf16[128,1152]{1,0:T(8,128)(2,1)S(1)} %copy-done.13, bf16[128,1152]{1,0:T(8,128)(2,1)S(1)} %copy-done.9, f32[2,9,8,128]{3,2,1,0:T(8,128)S(1)} %get-tuple-element.77.lse_ref, bf16[8,2,2,64,1152]{4,3,2,1,0:T(8,128)(2,1)S(1)} %bitcast.222, bf16[8,2,2,64,1152]{4,3,2,1,0:T(8,128)(2,1)S(1)} %bitcast.227, ...), custom_call_target="tpu_custom_call" | custom-call | flops 7247757312 | bytes 9437184 | tf_op jit(solution)/shard_map/pallas_call | solution.py:448
  467.4 20.9 %shard_map.274 = (bf16[128,1152]{1,0:T(8,128)(2,1)}, bf16[128,1152]{1,0:T(8,128)(2,1)}) custom-call(s32[1]{0:T(128)} %bitcast.46.me_ref, bf16[256,1152]{1,0:T(8,128)(2,1)} %get-tuple-element.72.k_ref.v_ref, bf16[256,1152]{1,0:T(8,128)(2,1)} %get-tuple-element.72.k_ref.v_ref, bf16[16,128,1152]{2,1,0:T(8,128)(2,1)} %bitcast.308, ...), custom_call_target="tpu_custom_call" | custom-call | flops 12079595520 | bytes 9437184 | tf_op jit(solution)/shard_map/pallas_call | solution.py:448
  496.9 18.6 %all-gather.19.cloned.1.call-done = bf16[2048,1088]{1,0:T(8,128)(2,1)} async-done(((bf16[128,1088]{1,0:T(8,128)(2,1)}), bf16[2048,1088]{1,0:T(8,128)(2,1)}) %all-gather.19.cloned.1.call-update) | async-done | bytes 4456464 | tf_op jit(solution)/shard_map/all_gather | solution.py:680
  515.5 14.5 %shard_map.276 = (f32[272,1088]{1,0:T(8,128)}, f32[1088,272]{1,0:T(8,128)}, f32[8,272]{1,0:T(8,128)}, f32[8,1088]{1,0:T(8,128)}) custom-call(bf16[16,256,1088]{2,1,0:T(8,128)(2,1)} %bitcast.300, bf16[16,128,1088]{2,1,0:T(8,128)(2,1)} %bitcast.309, bf16[1088,272]{1,0:T(8,128)(2,1)} %reshape.559.fc_ref, f32[1,272]{1,0:T(1,128)} %get-tuple-element.211.fb_ref, ...), custom_call_target="tpu_custom_call" | custom-call | flops 19394461696 | bytes 13369344 | tf_op jit(solution)/shard_map/pallas_call | solution.py:695
  542.4 9.3 %shard_map.277 = (f32[1088,272]{1,0:T(8,128)}, f32[8,272]{1,0:T(8,128)}) custom-call(s32[1]{0:T(128)} %bitcast.46.me_ref, bf16[16,256,1088]{2,1,0:T(8,128)(2,1)} %bitcast.301, bf16[16,144,1152]{2,1,0:T(8,128)(2,1)} %bitcast.306, bf16[16,128,272]{2,1,0:T(8,128)(2,1)} %copy.87.cols_ref), custom_call_target="tpu_custom_call" | custom-call | flops 4848615424 | bytes 17825792 | tf_op jit(solution)/shard_map/pallas_call | solution.py:708
  560.4 9.5 %shard_map.275 = (bf16[128,1088]{1,0:T(8,128)(2,1)}, f32[8,1088]{1,0:T(8,128)}) custom-call(bf16[128,1152]{1,0:T(8,128)(2,1)} %copy-done.12, bf16[128,1152]{1,0:T(8,128)(2,1)} %get-tuple-element.96.dk_ref, bf16[128,1152]{1,0:T(8,128)(2,1)} %get-tuple-element.97.dv_ref, bf16[8,384,1152]{2,1,0:T(8,128)(2,1)} %bitcast_dynamic-update-slice_fusion.xn_ref.near_ref, ...), custom_call_target="tpu_custom_call" | custom-call | flops 3636461568 | bytes 9437184 | tf_op jit(solution)/shard_map/pallas_call | solution.py:433
  588.6 10.7 %collective-permute-done.41 = bf16[7,72,384]{2,1,0:T(8,128)(2,1)S(1)} collective-permute-done((bf16[7,72,384]{2,1,0:T(8,128)(2,1)S(1)}, bf16[7,72,384]{2,1,0:T(8,128)(2,1)S(1)}, u32[]{:S(2)}, u32[]{:S(2)}) %collective-permute-start.41) | collective-permute-done | bytes 387104 | tf_op jit(solution)/shard_map/ppermute | solution.py:726
  (419 shorter events, 267.4 us)
Async XLA Ops:
  7.2 174.2 %all-gather.11.cloned.1.call-start = ((), (), s32[]{:S(2)}) async-start(), calls=%async_computation.3 | async-start | bytes 26320896 | tf_op jit(solution)/shard_map/all_gather | solution.py:505
  10.2 269.7 %all-gather.13.cloned.1.call-start = ((), (), s32[]{:S(2)}) async-start(), calls=%async_computation.4 | async-start | bytes 5013504 | tf_op jit(solution)/shard_map/all_gather | solution.py:611
  12.1 29.4 %collective-permute-start.1 = (bf16[384,1152]{1,0:T(8,128)(2,1)S(1)}, bf16[384,1152]{1,0:T(8,128)(2,1)S(1)}, u32[]{:S(2)}, u32[]{:S(2)}) collective-permute-start(bf16[384,1152]{1,0:T(8,128)(2,1)S(1)} %pad_dynamic-update-slice_fusion), channel_id=1, source_target_pairs={{0,16},{4,20},{8,24},{12,28},{16,0},{20,4},{24,8},{28,12},{32,48},... | collective-permute-start | bytes 2654216 | tf_op jit(solution)/shard_map/ppermute | solution.py:38
  13.8 32.3 %collective-permute-start.4 = (bf16[384,1152]{1,0:T(8,128)(2,1)S(1)}, bf16[384,1152]{1,0:T(8,128)(2,1)S(1)}, u32[]{:S(2)}, u32[]{:S(2)}) collective-permute-start(bf16[384,1152]{1,0:T(8,128)(2,1)S(1)} %pad_dynamic-update-slice_fusion), channel_id=1, source_target_pairs={{0,48},{4,52},{8,56},{12,60},{16,32},{20,36},{24,40},{28,44},{32,1... | collective-permute-start | bytes 2654216 | tf_op jit(solution)/shard_map/ppermute | solution.py:38
  16.0 35.9 %collective-permute-start = (bf16[384,1152]{1,0:T(8,128)(2,1)S(1)}, bf16[384,1152]{1,0:T(8,128)(2,1)S(1)}, u32[]{:S(2)}, u32[]{:S(2)}) collective-permute-start(bf16[384,1152]{1,0:T(8,128)(2,1)S(1)} %pad_dynamic-update-slice_fusion), channel_id=1, source_target_pairs={{0,8},{4,12},{8,0},{12,4},{16,24},{20,28},{24,16},{28,20},{32,40},... | collective-permute-start | bytes 2654216 | tf_op jit(solution)/shard_map/ppermute | solution.py:38
  41.5 23.2 %collective-permute-start.3 = (bf16[192,1152]{1,0:T(8,128)(2,1)S(1)}, bf16[192,1152]{1,0:T(8,128)(2,1)S(1)}, u32[]{:S(2)}, u32[]{:S(2)}) collective-permute-start(bf16[192,1152]{1,0:T(8,128)(2,1)S(1)} %slice.244), channel_id=1, source_target_pairs={{0,48},{4,52},{8,56},{12,60},{16,32},{20,36},{24,40},{28,44},{32,1... | collective-permute-start | bytes 1327112 | tf_op jit(solution)/shard_map/ppermute | solution.py:38
  51.9 35.4 %collective-permute-start.2 = (bf16[384,1152]{1,0:T(8,128)(2,1)S(1)}, bf16[384,1152]{1,0:T(8,128)(2,1)S(1)}, u32[]{:S(2)}, u32[]{:S(2)}) collective-permute-start(bf16[384,1152]{1,0:T(8,128)(2,1)S(1)} %collective-permute-done), channel_id=1, source_target_pairs={{0,16},{4,20},{8,24},{12,28},{16,0},{20,4},{24,8},{28,12},{32,48},... | collective-permute-start | bytes 2654216 | tf_op jit(solution)/shard_map/ppermute | solution.py:38
  51.9 39.4 %collective-permute-start.7 = (bf16[384,1152]{1,0:T(8,128)(2,1)S(1)}, bf16[384,1152]{1,0:T(8,128)(2,1)S(1)}, u32[]{:S(2)}, u32[]{:S(2)}) collective-permute-start(bf16[384,1152]{1,0:T(8,128)(2,1)S(1)} %collective-permute-done), channel_id=1, source_target_pairs={{0,48},{4,52},{8,56},{12,60},{16,32},{20,36},{24,40},{28,44},{32,1... | collective-permute-start | bytes 2654216 | tf_op jit(solution)/shard_map/ppermute | solution.py:38
  66.4 22.9 %collective-permute-start.6 = (bf16[384,1152]{1,0:T(8,128)(2,1)S(1)}, bf16[384,1152]{1,0:T(8,128)(2,1)S(1)}, u32[]{:S(2)}, u32[]{:S(2)}) collective-permute-start(bf16[384,1152]{1,0:T(8,128)(2,1)S(1)} %constant_dynamic-update-slice_fusion.1), channel_id=1, source_target_pairs={{0,8},{4,12},{8,0},{12,4},{16,24},{20,28},{24,16},{28,20},{32,40},... | collective-permute-start | bytes 2654216 | tf_op jit(solution)/shard_map/ppermute | solution.py:38
  215.8 140.2 %all-gather.15.cloned.1.call-start = ((), (), s32[]{:S(2)}) async-start(), calls=%async_computation.5 | async-start | bytes 5640192 | tf_op jit(solution)/shard_map/all_gather | solution.py:628
  229.6 24.7 %collective-permute-start.12 = (bf16[256,1152]{1,0:T(8,128)(2,1)}, bf16[256,1152]{1,0:T(8,128)(2,1)S(1)}, u32[]{:S(2)}, u32[]{:S(2)}) collective-permute-start(bf16[256,1152]{1,0:T(8,128)(2,1)} %collective-permute-done.10), channel_id=1, source_target_pairs={{0,16},{4,20},{8,24},{12,28},{16,0},{20,4},{24,8},{28,12},{32,48},... | collective-permute-start | bytes 1769480 | tf_op jit(solution)/shard_map/ppermute | solution.py:38
  230.2 28.1 %collective-permute-start.17 = (bf16[256,1152]{1,0:T(8,128)(2,1)}, bf16[256,1152]{1,0:T(8,128)(2,1)S(1)}, u32[]{:S(2)}, u32[]{:S(2)}) collective-permute-start(bf16[256,1152]{1,0:T(8,128)(2,1)} %collective-permute-done.10), channel_id=1, source_target_pairs={{0,48},{4,52},{8,56},{12,60},{16,32},{20,36},{24,40},{28,44},{32,1... | collective-permute-start | bytes 1769480 | tf_op jit(solution)/shard_map/ppermute | solution.py:38
  280.8 216.1 %all-gather.17.cloned.1.call-start = ((), (), s32[]{:S(2)}) async-start(), calls=%async_computation.6 | async-start | bytes 10027008 | tf_op jit(solution)/shard_map/all_gather | solution.py:631
  313.0 202.5 %all-gather.19.cloned.1.call-start = ((), (), s32[]{:S(2)}) async-start(), calls=%async_computation.7 | async-start | bytes 5013504 | tf_op jit(solution)/shard_map/all_gather | solution.py:680
  313.1 24.5 %collective-permute-start.19 = (bf16[128,1152]{1,0:T(8,128)(2,1)}, bf16[128,1152]{1,0:T(8,128)(2,1)S(1)}, u32[]{:S(2)}, u32[]{:S(2)}) collective-permute-start(bf16[128,1152]{1,0:T(8,128)(2,1)} %get-tuple-element.76.do_ref), channel_id=1, source_target_pairs={{0,16},{4,20},{8,24},{12,28},{16,0},{20,4},{24,8},{28,12},{32,48},... | collective-permute-start | bytes 884744 | tf_op jit(solution)/shard_map/ppermute | solution.py:38
  313.2 24.4 %collective-permute-start.20 = (bf16[128,1152]{1,0:T(8,128)(2,1)}, bf16[128,1152]{1,0:T(8,128)(2,1)S(1)}, u32[]{:S(2)}, u32[]{:S(2)}) collective-permute-start(bf16[128,1152]{1,0:T(8,128)(2,1)} %get-tuple-element.76.do_ref), channel_id=1, source_target_pairs={{0,48},{4,52},{8,56},{12,60},{16,32},{20,36},{24,40},{28,44},{32,1... | collective-permute-start | bytes 884744 | tf_op jit(solution)/shard_map/ppermute | solution.py:38
  313.2 24.4 %collective-permute-start.21 = (bf16[128,1152]{1,0:T(8,128)(2,1)}, bf16[128,1152]{1,0:T(8,128)(2,1)S(1)}, u32[]{:S(2)}, u32[]{:S(2)}) collective-permute-start(bf16[128,1152]{1,0:T(8,128)(2,1)} %get-tuple-element.76.do_ref), channel_id=1, source_target_pairs={{0,8},{4,12},{8,0},{12,4},{16,24},{20,28},{24,16},{28,20},{32,40},... | collective-permute-start | bytes 884744 | tf_op jit(solution)/shard_map/ppermute | solution.py:38
  317.0 20.7 %collective-permute-start.22 = (bf16[128,1152]{1,0:T(8,128)(2,1)}, bf16[128,1152]{1,0:T(8,128)(2,1)S(1)}, u32[]{:S(2)}, u32[]{:S(2)}) collective-permute-start(bf16[128,1152]{1,0:T(8,128)(2,1)} %get-tuple-element.76.do_ref), channel_id=1, source_target_pairs={{0,32},{4,36},{8,40},{12,44},{16,48},{20,52},{24,56},{28,60},{32,0... | collective-permute-start | bytes 884744 | tf_op jit(solution)/shard_map/ppermute | solution.py:38
  425.3 23.3 %collective-permute-start.28 = (bf16[128,1152]{1,0:T(8,128)(2,1)}, bf16[128,1152]{1,0:T(8,128)(2,1)S(1)}, u32[]{:S(2)}, u32[]{:S(2)}) collective-permute-start(bf16[128,1152]{1,0:T(8,128)(2,1)} %get-tuple-element.90.do_ref), channel_id=1, source_target_pairs={{0,16},{4,20},{8,24},{12,28},{16,0},{20,4},{24,8},{28,12},{32,48},... | collective-permute-start | bytes 884744 | tf_op jit(solution)/shard_map/ppermute | solution.py:38
  425.4 23.2 %collective-permute-start.29 = (bf16[128,1152]{1,0:T(8,128)(2,1)}, bf16[128,1152]{1,0:T(8,128)(2,1)S(1)}, u32[]{:S(2)}, u32[]{:S(2)}) collective-permute-start(bf16[128,1152]{1,0:T(8,128)(2,1)} %get-tuple-element.90.do_ref), channel_id=1, source_target_pairs={{0,48},{4,52},{8,56},{12,60},{16,32},{20,36},{24,40},{28,44},{32,1... | collective-permute-start | bytes 884744 | tf_op jit(solution)/shard_map/ppermute | solution.py:38
  426.3 22.3 %collective-permute-start.30 = (bf16[128,1152]{1,0:T(8,128)(2,1)}, bf16[128,1152]{1,0:T(8,128)(2,1)S(1)}, u32[]{:S(2)}, u32[]{:S(2)}) collective-permute-start(bf16[128,1152]{1,0:T(8,128)(2,1)} %get-tuple-element.90.do_ref), channel_id=1, source_target_pairs={{0,8},{4,12},{8,0},{12,4},{16,24},{20,28},{24,16},{28,20},{32,40},... | collective-permute-start | bytes 884744 | tf_op jit(solution)/shard_map/ppermute | solution.py:38
  492.1 37.9 %all-to-all-start = ((bf16[16,128,272]{1,2,0:T(8,128)(2,1)}), bf16[16,128,272]{1,2,0:T(8,128)(2,1)S(1)}, u32[]{:S(2)}, u32[]{:S(2)}) async-start(bf16[16,128,272]{1,2,0:T(8,128)(2,1)} %bitcast.85), calls=%async_computation | async-start | bytes 2228224 | tf_op jit(solution)/shard_map/all_to_all | solution.py:706
  533.0 22.2 %all-to-all-start.1 = ((bf16[16,72,384]{2,1,0:T(8,128)(2,1)}), bf16[16,72,384]{2,1,0:T(8,128)(2,1)S(1)}, u32[]{:S(2)}, u32[]{:S(2)}) async-start(bf16[16,72,384]{2,1,0:T(8,128)(2,1)} %pad.74), calls=%async_computation.1 | async-start | bytes 1769472 | tf_op jit(solution)/shard_map/all_to_all | solution.py:722
  578.6 20.7 %collective-permute-start.41 = (bf16[7,72,384]{2,1,0:T(8,128)(2,1)S(1)}, bf16[7,72,384]{2,1,0:T(8,128)(2,1)S(1)}, u32[]{:S(2)}, u32[]{:S(2)}) collective-permute-start(bf16[7,72,384]{2,1,0:T(8,128)(2,1)S(1)} %fusion.12), channel_id=1, source_target_pairs={{0,3},{1,2},{2,1},{3,0},{4,7},{5,6},{6,5},{7,4},{8,11},{9,10},{10,... | collective-permute-start | bytes 1161224 | tf_op jit(solution)/shard_map/ppermute | solution.py:726
  (84 other events, 991.1 us)
Sparse Core Ops, SparseCore 0:
  10.5 170.8 all-gather.10
  215.9 59.4 all-gather.12
  280.9 70.5 all-gather.14
  353.8 78.6 all-gather.16
  435.4 80.0 all-gather.18
